TPU v7x, 32 devices: a whole 2x2x4 slice. The times are simulated.
32 devices in a mesh: gx: 4 (over z), gy: 8 (over y, x, core).
Axes of the slice: x: 2, y: 2, z: 4, core: 2. Of those that a mesh axis runs over, the one named last changes fastest.
Arguments:
- noise: float32 [4, 512, 512], P('gx', 'gy'), may hold values from -6 to 6
- stencil: float32 [9], replicated, may hold values from 0.04 to 0.2
- mean_counts: float32 [4], replicated, may hold values from 0.5 to 4
- bias_one: float32 [4], replicated, may hold values from 1 to 2
- bias_two: float32 [4], replicated, may hold values from 0.05 to 0.3
- owner: int32 [8, 4, 4, 1], P('gy', 'gx'), may hold values from 0 to 3; in each aligned block of 4 rows (0 to 3, 4 to 7, ..., all dimensions but the last counted through in order) at most 2 rows name the same one
- depth: int32 [4, 8, 8], P('gx', None, 'gy'), may hold values from 0 to 3
- counts: int32 [4, 8, 8, 64, 128], P('gx', None, 'gy'), may hold values from 0 to 6
Outputs:
- gradient: float32 [4, 512, 512], P('gx', 'gy')
- density: float32 [4, 512, 512], P('gx', 'gy')
Inputs may be any that keep to these rules, and one draw needn't show every extreme that they name: Of the tiles of one device (aligned blocks of 4 rows), at most 2 name the same owner, and in every draw some owner is named exactly 2 times by one device.
All inputs are finite; a program needn't handle non-finite values.
Results may differ from a plain program's by a relative error of at most 0.0001.
Values sent between devices are 32-bit elements; how exact they have to be, the bound alone decides.
No kernel may reach another device: no remote copies, remote signals or barrier semaphores. Data moves between devices by JAX's collectives and lax.ppermute only.
A program may use at most 64 MiB of HBM per device.

v0:
```python
import functools
import math

import jax
import jax.numpy as jnp
import ml_dtypes
import numpy as np
from jax import lax
from jax.experimental import pallas as pl
from jax.experimental.pallas import tpu as pltpu
from jax.sharding import PartitionSpec as P

TC = 128
AMPLITUDE = 0.75
PIVOT = 1.0
GROWTH = 7.0 / 8.0
PAD = 16
VMEM = pltpu.VMEM
F32 = jnp.float32
BF16 = jnp.bfloat16


def split_np(table):
    high = table.astype(np.float32).astype(ml_dtypes.bfloat16)
    low = (table - high.astype(np.float64)).astype(np.float32).astype(ml_dtypes.bfloat16)
    return high, low


def make_tables(side, rows):
    half = side // 2
    quarter = side // 4
    freqs = np.concatenate([np.arange(0, half, 2), np.arange(1, half, 2)])
    wave = 2.0 * math.pi / side * freqs

    def basis(cells):
        turn = (freqs[:, None] * cells[None, :]) % side
        angle = 2.0 * math.pi / side * turn
        cos, sin = np.cos(angle), np.sin(angle)
        return np.concatenate([cos[:quarter], sin[:quarter], cos[quarter:], sin[quarter:]])

    def slope(cells):
        turn = (freqs[:, None] * cells[None, :]) % side
        angle = 2.0 * math.pi / side * turn
        cos, sin = -wave[:, None] * np.sin(angle), wave[:, None] * np.cos(angle)
        return np.concatenate([cos[:quarter], sin[:quarter], cos[quarter:], sin[quarter:]])

    plain = basis(np.arange(half))
    even, odd = plain[:half], plain[half:]
    ring = np.concatenate([np.arange(rows + 1), np.zeros(PAD - 2, int), [side - 1]])
    used = np.ones(rows + PAD)
    used[rows + 1 : rows + PAD - 1] = 0.0
    views = np.concatenate([(basis(ring) * used).T, (slope(ring) * used).T])
    wave_sq = wave[:, None] ** 2 + wave[None, :] ** 2
    inverse = np.where(wave_sq > 0, 1.0 / np.where(wave_sq > 0, wave_sq, 1.0), 0.0)
    weight = np.where(freqs == 0, 1.0, 2.0)
    gain = AMPLITUDE * (np.sqrt(wave_sq) / PIVOT) / (1.0 + wave_sq / PIVOT**2)
    gain = gain * weight[:, None] * weight[None, :] / (side * side)
    views_h, views_l = split_np(views)
    up = views.T
    up_h, up_l = split_np(up)
    tables = []
    for table in (even, odd, even.T, odd.T):
        tables.extend(split_np(np.ascontiguousarray(table)))
    fwd = tuple(tables[:4])
    back = tuple(tables[4:])
    waves = np.repeat(wave.reshape(2, quarter).astype(np.float32)[:, None, :], 1, axis=1)
    return dict(
        fwd=fwd,
        back=back,
        views=(views_h, views_l),
        lift=np.concatenate([up_h, up_h, up_l], axis=1),
        gain=gain.astype(np.float32),
        inverse=inverse.astype(np.float32),
        waves=waves,
    )


def mm(a, b):
    return jnp.dot(a, b, preferred_element_type=F32)


def split(a):
    high = a.astype(BF16)
    return high, (a - high.astype(F32)).astype(BF16)


def mm3(a, b):
    return mm(a[0], b[0]) + (mm(a[0], b[1]) + mm(a[1], b[0]))


def turn_rows(a, step):
    return pltpu.roll(a, step % a.shape[0], 0)


def turn_lanes(a, step):
    return pltpu.roll(a, step % a.shape[1], 1)


def slope_lanes(a, waves, orient):
    q = a.shape[1] // 4
    parts = []
    for par in range(2):
        w = waves[par] * orient
        cos, sin = a[:, 2 * par * q : (2 * par + 1) * q], a[:, (2 * par + 1) * q : (2 * par + 2) * q]
        parts.extend([w * sin, -w * cos])
    return jnp.concatenate(parts, axis=1)


def place_of(me, k, n):
    return lax.rem(lax.bitwise_xor(me, k) - me + n, n)


def main_kernel(n, groups, rows, side, tiles, *refs):
    half, q = side // 2, side // 4
    ring = rows + PAD
    refs = list(refs)
    owner, stencil, mean_counts, bias_one, bias_two = refs[:5]
    blocks = refs[5 : 5 + n]
    msgs = refs[5 + n : 5 + n + groups]
    rest = refs[5 + n + groups :]
    eh, el, oh, ol, teh, tel, toh, tol, vh, vl, lift, gain, inverse, waves = rest[:14]
    density_out = rest[14]
    outs = rest[15 : 15 + n]
    fh, fl, yh, yl, zh, zl, cnt, cls, part = rest[15 + n :]
    me = lax.axis_index("gy")
    mine = lax.axis_index("gx")
    fwd = ((eh, el), (oh, ol))
    back = ((teh, tel), (toh, tol))

    for t in range(tiles):
        rank = jnp.int32(0)
        for t2 in range(t):
            rank = rank + (owner[t2] == owner[t]).astype(jnp.int32)
        which = lax.bitwise_xor(owner[t], mine)
        for k in range(groups):

            @pl.when(which == k)
            def _():
                cnt[:, t * TC : (t + 1) * TC] = msgs[k][rank, :rows, :].astype(F32)
                cls[:, t * TC : (t + 1) * TC] = msgs[k][rank, rows : rows + 8, :]

    for k in range(n // 2):
        a, b = blocks[k][...], blocks[k ^ (n // 2)][...]
        place = place_of(me, k, n)
        sign = jnp.where(place < n // 2, 1.0, -1.0).astype(F32)
        off = pl.multiple_of(lax.rem(place, n // 2) * rows, rows)
        for par, v in ((0, a + b), (1, (a - b) * sign)):
            lo, hi = v[:, :half], v[:, half:]
            for ypar, w in ((0, lo + hi), (1, lo - hi)):
                h, l = split(w)
                fh[par, pl.ds(off, rows), ypar * half : (ypar + 1) * half] = h
                fl[par, pl.ds(off, rows), ypar * half : (ypar + 1) * half] = l

    for par in range(2):
        for ypar in range(2):
            cols = slice(ypar * half, (ypar + 1) * half)
            y = mm3((fh[par, :, cols], fl[par, :, cols]), tuple(r[...] for r in back[ypar]))
            yh[par, :, cols], yl[par, :, cols] = split(y)
    for par in range(2):
        for ypar in range(2):
            cols = slice(ypar * half, (ypar + 1) * half)
            x = mm3(tuple(r[...] for r in fwd[par]), (yh[par, :, cols], yl[par, :, cols]))
            g = gain[par * q : (par + 1) * q, ypar * q : (ypar + 1) * q]
            inv = inverse[par * q : (par + 1) * q, ypar * q : (ypar + 1) * q]
            for i in range(2):
                for j in range(2):
                    base = x[i * q : (i + 1) * q, j * q : (j + 1) * q] * g
                    phi = base * inv
                    rs = slice(par * half + i * q, par * half + (i + 1) * q)
                    c0 = ypar * half + j * q
                    zh[rs, c0 : c0 + q], zl[rs, c0 : c0 + q] = split(base)
                    zh[rs, side + c0 : side + c0 + q], zl[rs, side + c0 : side + c0 + q] = split(phi)

    w = mm3((vh[...], vl[...]), (zh[...], zl[...]))
    ky = (waves[0], waves[1])
    base, base_x = w[:ring, :side], w[ring:, :side]
    phi, phi_x = w[:ring, side:], w[ring:, side:]
    stack = jnp.concatenate([base, phi_x, slope_lanes(phi, ky, 1.0), base_x, slope_lanes(base, ky, 1.0)], axis=0)
    sh, sl = split(stack)
    e = mm3((sh[:, :half], sl[:, :half]), (eh[...], el[...]))
    o = mm3((sh[:, half:], sl[:, half:]), (oh[...], ol[...]))
    fields = jnp.concatenate([e + o, e - o], axis=1)
    linear, shift_x, shift_y, slope_x, slope_y = [fields[i * ring : (i + 1) * ring] for i in range(5)]
    density = linear + GROWTH * linear * linear - (shift_x * slope_x + shift_y * slope_y)
    density_out[...] = density[:rows]

    beside = {0: density, 1: turn_lanes(density, -1), -1: turn_lanes(density, 1)}
    smooth = jnp.zeros_like(density)
    for a in (-1, 0, 1):
        band = sum(stencil[(a + 1) * 3 + b + 1] * beside[b] for b in (-1, 0, 1))
        smooth = smooth + (turn_rows(band, -a) if a else band)
    smooth = smooth[:rows]
    classes = cls[...]
    mean_v, one_v, two_v = [jnp.full(classes.shape, ref[0], F32) for ref in (mean_counts, bias_one, bias_two)]
    for d in range(1, mean_counts.shape[0]):
        hit = classes == d
        mean_v = jnp.where(hit, mean_counts[d], mean_v)
        one_v = jnp.where(hit, bias_one[d], one_v)
        two_v = jnp.where(hit, bias_two[d], two_v)
    mean_v, one_v, two_v = mean_v[:1], one_v[:1], two_v[:1]
    rate = mean_v * jnp.exp(one_v * smooth + two_v * smooth * smooth)
    score = (cnt[...] - rate) * (one_v + 2.0 * two_v * smooth)
    score = jnp.concatenate([score, jnp.zeros((PAD, side), F32)], axis=0)
    beside = {0: score, 1: turn_lanes(score, 1), -1: turn_lanes(score, -1)}
    pulled = jnp.zeros_like(score)
    for a in (-1, 0, 1):
        band = sum(stencil[(a + 1) * 3 + b + 1] * beside[b] for b in (-1, 0, 1))
        pulled = pulled + (turn_rows(band, a) if a else band)

    bars = jnp.concatenate(
        [
            pulled * (1.0 + 2.0 * GROWTH * linear),
            -pulled * slope_x,
            -pulled * slope_y,
            -pulled * shift_x,
            -pulled * shift_y,
        ],
        axis=0,
    )
    lo, hi = bars[:, :half], bars[:, half:]
    ye = mm3(split(lo + hi), (teh[...], tel[...]))
    yo = mm3(split(lo - hi), (toh[...], tol[...]))
    modes = jnp.concatenate([ye, yo], axis=1)
    m_lin, m_sx, m_sy, m_gx, m_gy = [modes[i * ring : (i + 1) * ring] for i in range(5)]
    to_base = m_lin + slope_lanes(m_gy, ky, -1.0)
    to_phi = slope_lanes(m_sy, ky, -1.0)
    pile = jnp.concatenate(
        [jnp.concatenate([to_base, to_phi], axis=1), jnp.concatenate([m_gx, m_sx], axis=1)], axis=0
    )
    ph, plow = split(pile)
    zeros = jnp.zeros((lift.shape[1] - 3 * 2 * ring, 2 * side), BF16)
    pile3 = jnp.concatenate([ph, plow, ph] + ([zeros] if zeros.shape[0] else []), axis=0)

    for par in range(2):
        for i in range(2):
            rs = slice(par * half + i * q, par * half + (i + 1) * q)
            x = mm(lift[rs, :], pile3)
            for ypar in range(2):
                g = gain[par * q : (par + 1) * q, ypar * q : (ypar + 1) * q]
                inv = inverse[par * q : (par + 1) * q, ypar * q : (ypar + 1) * q]
                for j in range(2):
                    c0 = ypar * half + j * q
                    d = g * (x[:, c0 : c0 + q] + inv * x[:, side + c0 : side + c0 + q])
                    yh[par, i * q : (i + 1) * q, c0 : c0 + q], yl[par, i * q : (i + 1) * q, c0 : c0 + q] = split(d)
    e = mm3((teh[...], tel[...]), (yh[0], yl[0]))
    o = mm3((toh[...], tol[...]), (yh[1], yl[1]))
    part[0] = e + o
    part[1] = e - o
    for k in range(n):
        place = place_of(me, k, n)
        off = pl.multiple_of(lax.rem(place, n // 2) * rows, rows)
        outs[k][...] = part[place // (n // 2), pl.ds(off, rows), :]


def last_kernel(count, *refs):
    parts = refs[:count]
    noise, eh, el, oh, ol, out = refs[count:]
    total = parts[0][...]
    for p in parts[1:]:
        total = total + p[...]
    half = total.shape[1] // 2
    sh, sl = split(total)
    e = mm3((sh[:, :half], sl[:, :half]), (eh[...], el[...]))
    o = mm3((sh[:, half:], sl[:, half:]), (oh[...], ol[...]))
    out[:, :half] = e + o - noise[:, :half]
    out[:, half:] = e - o - noise[:, half:]


def local(n, groups, noise, stencil, mean_counts, bias_one, bias_two, owner, depth, counts):
    _, rows, side = noise.shape
    own = noise.reshape(rows, side)
    tiles = side // TC
    slots = counts.shape[1]
    capacity = slots // groups
    tables = make_tables(side, rows)

    def swap(value, k, axis="gy", size=n):
        return lax.ppermute(value, axis, [(i, i ^ k) for i in range(size)])

    blocks = {0: own}
    for k in range(n - 2, 0, -2):
        blocks[k] = swap(own, k)
    blocks[1] = swap(own, 1)
    mine = lax.axis_index("gx")
    message = jnp.concatenate(
        [
            counts.reshape(slots, rows, TC),
            jnp.broadcast_to(depth.reshape(slots, 1, 1), (slots, 8, TC)),
        ],
        axis=1,
    )
    msgs = []
    for k in range(groups):
        piece = lax.dynamic_slice_in_dim(message, lax.bitwise_xor(mine, k) * capacity, capacity, 0)
        msgs.append(swap(piece, k, "gx", groups) if k else piece)
    for k in range(2, n, 2):
        blocks[k + 1] = swap(blocks[k], 1)

    ring = rows + PAD
    half = side // 2
    smem = pl.BlockSpec(memory_space=pltpu.SMEM)
    vmem = pl.BlockSpec(memory_space=VMEM)
    consts = [
        jnp.asarray(t)
        for t in (
            *tables["fwd"],
            *tables["back"],
            *tables["views"],
            tables["lift"],
            tables["gain"],
            tables["inverse"],
            tables["waves"],
        )
    ]
    cell = jax.ShapeDtypeStruct((rows, side), F32)
    density, *parts = pl.pallas_call(
        functools.partial(main_kernel, n, groups, rows, side, tiles),
        out_shape=[cell] * (1 + n),
        in_specs=[smem] * 5 + [vmem] * (n + groups + len(consts)),
        out_specs=[vmem] * (1 + n),
        scratch_shapes=[
            VMEM((2, half, side), BF16),
            VMEM((2, half, side), BF16),
            VMEM((2, half, side), BF16),
            VMEM((2, half, side), BF16),
            VMEM((side, 2 * side), BF16),
            VMEM((side, 2 * side), BF16),
            VMEM((rows, side), F32),
            VMEM((8, side), jnp.int32),
            VMEM((2, half, side), F32),
        ],
        compiler_params=pltpu.CompilerParams(vmem_limit_bytes=32 * 1024 * 1024),
        name="fields_and_adjoint",
    )(
        owner.reshape(tiles),
        stencil,
        mean_counts,
        bias_one,
        bias_two,
        *[blocks[k] for k in range(n)],
        *msgs,
        *consts,
    )
    sums = {}
    for k in range(n - 2, -1, -2):
        sums[k] = parts[k] + swap(parts[k + 1], 1)
    pieces = [sums[0]] + [swap(sums[k], k) for k in range(n - 2, 0, -2)]
    gradient = pl.pallas_call(
        functools.partial(last_kernel, len(pieces)),
        out_shape=cell,
        in_specs=[vmem] * (len(pieces) + 5),
        out_specs=vmem,
        compiler_params=pltpu.CompilerParams(vmem_limit_bytes=32 * 1024 * 1024),
        name="sum_and_rows",
    )(*pieces, own, *consts[:4])
    return (gradient.reshape(1, rows, side), density.reshape(1, rows, side))


def solution(mesh):
    return jax.shard_map(
        functools.partial(local, mesh.shape["gy"], mesh.shape["gx"]),
        mesh=mesh,
        in_specs=(
            P("gx", "gy", None),
            P(),
            P(),
            P(),
            P(),
            P("gy", "gx", None, None),
            P("gx", None, "gy"),
            P("gx", None, "gy", None, None),
        ),
        out_specs=(P("gx", "gy", None), P("gx", "gy", None)),
        check_vma=False,
    )
```

profile of v0, /device:TPU:0, one launch (start us, length us, event | category | flops | bytes accessed | tf_op | source)
XLA Modules:
  0.0 47.8 jit_solution(6762644779366967005)
XLA Ops:
  0.6 4.0 %collective-permute-start.5 = (f32[64,512]{1,0:T(8,128)}, f32[64,512]{1,0:T(8,128)S(1)}, u32[]{:S(2)}, u32[]{:S(2)}) collective-permute-start(f32[64,512]{1,0:T(8,128)} %bitcast.6), channel_id=1, source_target_pairs={{0,6},{1,7},{2,4},{3,5},{4,2},{5,3},{6,0},{7,1},{8,14},{9,15},{10,... | collective-permute-start | bytes 393224 | tf_op jit(solution)/shard_map/ppermute | solution.py:278
  4.6 0.5 %collective-permute-start.3 = (f32[64,512]{1,0:T(8,128)}, f32[64,512]{1,0:T(8,128)S(1)}, u32[]{:S(2)}, u32[]{:S(2)}) collective-permute-start(f32[64,512]{1,0:T(8,128)} %bitcast.7), channel_id=1, source_target_pairs={{0,4},{1,5},{2,6},{3,7},{4,0},{5,1},{6,2},{7,3},{8,12},{9,13},{10,... | collective-permute-start | bytes 393224 | tf_op jit(solution)/shard_map/ppermute | solution.py:278
  5.1 0.1 collective-permute-start.1
  5.2 0.7 %copy-done.20 = s32[1,8,1]{1,2,0:T(1,128)S(1)} copy-done((s32[1,8,1]{1,2,0:T(1,128)S(1)}, s32[1,8,1]{1,2,0:T(1,128)}, u32[]{:S(2)}) %copy-start.20) | copy-done | bytes 56
  5.9 0.1 broadcast_in_dim.8
  6.0 0.0 copy-start.3
  6.0 1.0 %fusion = (s32[2,72,128]{2,1,0:T(8,128)S(1)}, s32[2,72,128]{2,1,0:T(8,128)S(1)}, s32[2,72,128]{2,1,0:T(8,128)S(1)}, s32[2,72,128]{2,1,0:T(8,128)S(1)}) fusion(s32[]{:T(128)S(6)} %select_n.15, s32[8,64,128]{2,1,0:T(8,128)} %bitcast.13, s32[8,8,128]{2,1,0:T(8,128)S(1)} %broadcast_in_dim.8, s32[]{:T(128)S(6)} %select_n.12, s32[]{:T(128)S(6)} %select_n.13, ...), kind=kLoop, calls=%fused_computation.8 | loop fusion | flops 73728 | bytes 589840 | tf_op jit(solution)/shard_map/concatenate | solution.py:285
  7.0 0.0 copy-start.16
  7.0 0.0 copy-start.17
  7.1 0.0 copy-start.18
  7.1 4.1 %collective-permute-start.9 = (s32[2,72,128]{2,1,0:T(8,128)S(1)}, s32[2,72,128]{2,1,0:T(8,128)S(1)}, u32[]{:S(2)}, u32[]{:S(2)}) collective-permute-start(s32[2,72,128]{2,1,0:T(8,128)S(1)} %get-tuple-element.20), channel_id=1, source_target_pairs={{0,24},{8,16},{16,8},{24,0},{1,25},{9,17},{17,9},{25,1},{2,26},{10... | collective-permute-start | bytes 221192 | tf_op jit(solution)/shard_map/ppermute | solution.py:278
  11.1 0.0 collective-permute-start.7
  11.1 2.5 %collective-permute-done.9.refs_16_ = s32[2,72,128]{2,1,0:T(8,128)S(1)} collective-permute-done((s32[2,72,128]{2,1,0:T(8,128)S(1)}, s32[2,72,128]{2,1,0:T(8,128)S(1)}, u32[]{:S(2)}, u32[]{:S(2)}) %collective-permute-start.9) | collective-permute-done | bytes 73760 | tf_op jit(solution)/shard_map/ppermute | solution.py:278
  13.6 0.0 copy-done
  13.6 0.0 collective-permute-start
  13.6 0.0 collective-permute-done.5.refs_11_
  13.6 0.5 %collective-permute-start.6 = (f32[64,512]{1,0:T(8,128)S(1)}, f32[64,512]{1,0:T(8,128)S(1)}, u32[]{:S(2)}, u32[]{:S(2)}) collective-permute-start(f32[64,512]{1,0:T(8,128)S(1)} %collective-permute-done.5.refs_11_), channel_id=1, source_target_pairs={{0,1},{1,0},{2,3},{3,2},{4,5},{5,4},{6,7},{7,6},{8,9},{9,8},{10,11... | collective-permute-start | bytes 393224 | tf_op jit(solution)/shard_map/ppermute | solution.py:278
  14.1 0.0 collective-permute-done.3.refs_9_
  14.1 0.1 collective-permute-start.4
  14.2 0.0 collective-permute-done.1.refs_7_
  14.2 0.4 collective-permute-start.2
  14.7 0.8 %collective-permute-done.7.refs_14_ = s32[2,72,128]{2,1,0:T(8,128)S(1)} collective-permute-done((s32[2,72,128]{2,1,0:T(8,128)S(1)}, s32[2,72,128]{2,1,0:T(8,128)S(1)}, u32[]{:S(2)}, u32[]{:S(2)}) %collective-permute-start.7) | collective-permute-done | bytes 73760 | tf_op jit(solution)/shard_map/ppermute | solution.py:278
  15.5 0.8 %collective-permute-start.8 = (s32[2,72,128]{2,1,0:T(8,128)S(1)}, s32[2,72,128]{2,1,0:T(8,128)S(1)}, u32[]{:S(2)}, u32[]{:S(2)}) collective-permute-start(s32[2,72,128]{2,1,0:T(8,128)S(1)} %get-tuple-element.23), channel_id=1, source_target_pairs={{0,16},{8,24},{16,0},{24,8},{1,17},{9,25},{17,1},{25,9},{2,18},{10... | collective-permute-start | bytes 221192 | tf_op jit(solution)/shard_map/ppermute | solution.py:278
  16.2 5.4 %collective-permute-done.8.refs_15_ = s32[2,72,128]{2,1,0:T(8,128)S(1)} collective-permute-done((s32[2,72,128]{2,1,0:T(8,128)S(1)}, s32[2,72,128]{2,1,0:T(8,128)S(1)}, u32[]{:S(2)}, u32[]{:S(2)}) %collective-permute-start.8) | collective-permute-done | bytes 73760 | tf_op jit(solution)/shard_map/ppermute | solution.py:278
  21.6 0.0 collective-permute-done.refs_6_
  21.6 0.0 collective-permute-done.6.refs_12_
  21.6 0.0 collective-permute-done.4.refs_10_
  21.6 0.0 collective-permute-done.2.refs_8_
  21.6 0.0 copy-start.14
  21.7 0.0 copy-start.15
  21.7 0.0 copy-done.19
  21.7 0.0 copy-done.4
  21.7 0.0 copy-done.1
  21.7 0.0 copy-done.2
  21.7 0.0 copy-done.3
  21.7 0.0 copy-done.16
  21.7 0.0 copy-done.17
  21.7 0.0 copy-done.18
  21.7 0.6 %copy-done.14 = f32[2,1,128]{2,1,0:T(1,128)S(1)} copy-done((f32[2,1,128]{2,1,0:T(1,128)S(1)}, f32[2,1,128]{2,1,0:T(1,128)}, u32[]{:S(2)}) %copy-start.14) | copy-done | bytes 1048
  22.3 1.0 %copy-done.5 = bf16[512,480]{1,0:T(8,128)(2,1)S(1)} copy-done((bf16[512,480]{1,0:T(8,128)(2,1)S(1)}, bf16[512,480]{1,0:T(8,128)(2,1)}, u32[]{:S(2)}) %copy-start.5) | copy-done | bytes 491544
  23.4 0.9 %copy-done.6 = f32[256,256]{1,0:T(8,128)S(1)} copy-done((f32[256,256]{1,0:T(8,128)S(1)}, f32[256,256]{1,0:T(8,128)}, u32[]{:S(2)}) %copy-start.6) | copy-done | bytes 262168
  24.3 0.9 %copy-done.7 = f32[256,256]{1,0:T(8,128)S(1)} copy-done((f32[256,256]{1,0:T(8,128)S(1)}, f32[256,256]{1,0:T(8,128)}, u32[]{:S(2)}) %copy-start.7) | copy-done | bytes 262168
  25.3 0.9 %copy-done.8 = bf16[160,512]{1,0:T(8,128)(2,1)S(1)} copy-done((bf16[160,512]{1,0:T(8,128)(2,1)S(1)}, bf16[160,512]{1,0:T(8,128)(2,1)}, u32[]{:S(2)}) %copy-start.8) | copy-done | bytes 163864
  26.2 0.9 %copy-done.9 = bf16[160,512]{1,0:T(8,128)(2,1)S(1)} copy-done((bf16[160,512]{1,0:T(8,128)(2,1)S(1)}, bf16[160,512]{1,0:T(8,128)(2,1)}, u32[]{:S(2)}) %copy-start.9) | copy-done | bytes 163864
  27.1 0.9 %copy-done.10 = bf16[256,256]{1,0:T(8,128)(2,1)S(1)} copy-done((bf16[256,256]{1,0:T(8,128)(2,1)S(1)}, bf16[256,256]{1,0:T(8,128)(2,1)}, u32[]{:S(2)}) %copy-start.10) | copy-done | bytes 131096
  28.0 0.9 %copy-done.11 = bf16[256,256]{1,0:T(8,128)(2,1)S(1)} copy-done((bf16[256,256]{1,0:T(8,128)(2,1)S(1)}, bf16[256,256]{1,0:T(8,128)(2,1)}, u32[]{:S(2)}) %copy-start.11) | copy-done | bytes 131096
  28.9 0.9 %copy-done.12 = bf16[256,256]{1,0:T(8,128)(2,1)S(1)} copy-done((bf16[256,256]{1,0:T(8,128)(2,1)S(1)}, bf16[256,256]{1,0:T(8,128)(2,1)}, u32[]{:S(2)}) %copy-start.12) | copy-done | bytes 131096
  29.8 0.9 %copy-done.13 = bf16[256,256]{1,0:T(8,128)(2,1)S(1)} copy-done((bf16[256,256]{1,0:T(8,128)(2,1)S(1)}, bf16[256,256]{1,0:T(8,128)(2,1)}, u32[]{:S(2)}) %copy-start.13) | copy-done | bytes 131096
  30.7 5.3 %fields_and_adjoint.1 = (f32[64,512]{1,0:T(8,128)}, f32[64,512]{1,0:T(8,128)S(1)}, f32[64,512]{1,0:T(8,128)S(1)}, f32[64,512]{1,0:T(8,128)S(1)}, f32[64,512]{1,0...) custom-call(s32[4]{0:T(128)S(1)} %bitcast.12, ...), custom_call_target="tpu_custom_call" | custom-call | tf_op jit(solution)/shard_map/fields_and_adjoint/pallas_call | solution.py:316
  36.1 0.1 collective-permute-start.11
  36.1 0.5 %collective-permute-start.13 = (f32[64,512]{1,0:T(8,128)S(1)}, f32[64,512]{1,0:T(8,128)S(1)}, u32[]{:S(2)}, u32[]{:S(2)}) collective-permute-start(f32[64,512]{1,0:T(8,128)S(1)} %get-tuple-element.16), channel_id=1, source_target_pairs={{0,1},{1,0},{2,3},{3,2},{4,5},{5,4},{6,7},{7,6},{8,9},{9,8},{10,11... | collective-permute-start | bytes 393224 | tf_op jit(solution)/shard_map/ppermute | solution.py:278
  36.6 0.1 collective-permute-start.15
  36.7 0.4 collective-permute-start.10
  37.1 0.3 collective-permute-done.11
  37.5 2.5 %collective-permute-start.12 = (f32[64,512]{1,0:T(8,128)S(1)}, f32[64,512]{1,0:T(8,128)S(1)}, u32[]{:S(2)}, u32[]{:S(2)}) collective-permute-start(f32[64,512]{1,0:T(8,128)S(1)} %add.29), channel_id=1, source_target_pairs={{0,6},{1,7},{2,4},{3,5},{4,2},{5,3},{6,0},{7,1},{8,14},{9,15},{10,... | collective-permute-start | bytes 393224 | tf_op jit(solution)/shard_map/ppermute | solution.py:278
  40.0 0.0 collective-permute-done.13
  40.0 0.6 %collective-permute-start.14 = (f32[64,512]{1,0:T(8,128)S(1)}, f32[64,512]{1,0:T(8,128)S(1)}, u32[]{:S(2)}, u32[]{:S(2)}) collective-permute-start(f32[64,512]{1,0:T(8,128)S(1)} %add.30), channel_id=1, source_target_pairs={{0,4},{1,5},{2,6},{3,7},{4,0},{5,1},{6,2},{7,3},{8,12},{9,13},{10,... | collective-permute-start | bytes 393224 | tf_op jit(solution)/shard_map/ppermute | solution.py:278
  40.6 0.0 collective-permute-done.15
  40.6 0.6 %collective-permute-start.16 = (f32[64,512]{1,0:T(8,128)S(1)}, f32[64,512]{1,0:T(8,128)S(1)}, u32[]{:S(2)}, u32[]{:S(2)}) collective-permute-start(f32[64,512]{1,0:T(8,128)S(1)} %add.31), channel_id=1, source_target_pairs={{0,2},{1,3},{2,0},{3,1},{4,6},{5,7},{6,4},{7,5},{8,10},{9,11},{10,... | collective-permute-start | bytes 393224 | tf_op jit(solution)/shard_map/ppermute | solution.py:278
  41.2 0.0 collective-permute-done.10
  41.3 2.9 %collective-permute-done.12.refs_1_ = f32[64,512]{1,0:T(8,128)S(1)} collective-permute-done((f32[64,512]{1,0:T(8,128)S(1)}, f32[64,512]{1,0:T(8,128)S(1)}, u32[]{:S(2)}, u32[]{:S(2)}) %collective-permute-start.12) | collective-permute-done | bytes 131104 | tf_op jit(solution)/shard_map/ppermute | solution.py:278
  44.1 2.7 %collective-permute-done.14.refs_2_ = f32[64,512]{1,0:T(8,128)S(1)} collective-permute-done((f32[64,512]{1,0:T(8,128)S(1)}, f32[64,512]{1,0:T(8,128)S(1)}, u32[]{:S(2)}, u32[]{:S(2)}) %collective-permute-start.14) | collective-permute-done | bytes 131104 | tf_op jit(solution)/shard_map/ppermute | solution.py:278
  46.8 0.1 collective-permute-done.16.refs_3_
  46.9 0.9 %sum_and_rows.1 = f32[64,512]{1,0:T(8,128)} custom-call(f32[64,512]{1,0:T(8,128)S(1)} %add.28.refs_0_, f32[64,512]{1,0:T(8,128)S(1)} %collective-permute-done.12.refs_1_, f32[64,512]{1,0:T(8,128)S(1)} %collective-permute-done.14.refs_2_, f32[64,512]{1,0:T(8,128)S(1)} %collective-permute-done.16.refs_3_, f32[64,512]{1,0:T(8,128)S(1)} %bitcast.11, ...), custom_call_target="tpu_custom_call" | custom-call | tf_op jit(solution)/shard_map/sum_and_rows/pallas_call | solution.py:348
  (20 shorter events, 0.1 us)
Async XLA Ops:
  0.6 13.0 %collective-permute-start.5 = (f32[64,512]{1,0:T(8,128)}, f32[64,512]{1,0:T(8,128)S(1)}, u32[]{:S(2)}, u32[]{:S(2)}) collective-permute-start(f32[64,512]{1,0:T(8,128)} %bitcast.6), channel_id=1, source_target_pairs={{0,6},{1,7},{2,4},{3,5},{4,2},{5,3},{6,0},{7,1},{8,14},{9,15},{10,... | collective-permute-start | bytes 393224 | tf_op jit(solution)/shard_map/ppermute | solution.py:278
  4.6 9.6 %collective-permute-start.3 = (f32[64,512]{1,0:T(8,128)}, f32[64,512]{1,0:T(8,128)S(1)}, u32[]{:S(2)}, u32[]{:S(2)}) collective-permute-start(f32[64,512]{1,0:T(8,128)} %bitcast.7), channel_id=1, source_target_pairs={{0,4},{1,5},{2,6},{3,7},{4,0},{5,1},{6,2},{7,3},{8,12},{9,13},{10,... | collective-permute-start | bytes 393224 | tf_op jit(solution)/shard_map/ppermute | solution.py:278
  5.1 9.1 %collective-permute-start.1 = (f32[64,512]{1,0:T(8,128)}, f32[64,512]{1,0:T(8,128)S(1)}, u32[]{:S(2)}, u32[]{:S(2)}) collective-permute-start(f32[64,512]{1,0:T(8,128)} %bitcast.8), channel_id=1, source_target_pairs={{0,2},{1,3},{2,0},{3,1},{4,6},{5,7},{6,4},{7,5},{8,10},{9,11},{10,... | collective-permute-start | bytes 393224 | tf_op jit(solution)/shard_map/ppermute | solution.py:278
  5.2 16.4 %copy-start.19 = (f32[4]{0:T(128)S(1)}, f32[4]{0:T(128)}, u32[]{:S(2)}) copy-start(f32[4]{0:T(128)} %refs_4_.1) | copy-start | bytes 52
  5.2 0.7 %copy-start.20 = (s32[1,8,1]{1,2,0:T(1,128)S(1)}, s32[1,8,1]{1,2,0:T(1,128)}, u32[]{:S(2)}) copy-start(s32[1,8,1]{1,2,0:T(1,128)} %param.28) | copy-start | bytes 100
  5.2 16.4 %copy-start.4 = (bf16[256,256]{1,0:T(8,128)(2,1)S(1)}, bf16[256,256]{1,0:T(8,128)(2,1)}, u32[]{:S(2)}) copy-start(bf16[256,256]{1,0:T(8,128)(2,1)} %constant.43.clone.refs_17_.refs_5_) | copy-start | bytes 393220
  6.0 7.6 %copy-start = (f32[1,64,512]{2,1,0:T(8,128)S(1)}, f32[1,64,512]{2,1,0:T(8,128)}, u32[]{:S(2)}) copy-start(f32[1,64,512]{2,1,0:T(8,128)} %param.22) | copy-start | bytes 393220
  6.0 15.7 %copy-start.1 = (bf16[256,256]{1,0:T(8,128)(2,1)S(1)}, bf16[256,256]{1,0:T(8,128)(2,1)}, u32[]{:S(2)}) copy-start(bf16[256,256]{1,0:T(8,128)(2,1)} %constant.46.clone.refs_20_.refs_8_) | copy-start | bytes 393220
  6.0 15.7 %copy-start.2 = (bf16[256,256]{1,0:T(8,128)(2,1)S(1)}, bf16[256,256]{1,0:T(8,128)(2,1)}, u32[]{:S(2)}) copy-start(bf16[256,256]{1,0:T(8,128)(2,1)} %constant.45.clone.refs_19_.refs_7_) | copy-start | bytes 393220
  6.0 15.7 %copy-start.3 = (bf16[256,256]{1,0:T(8,128)(2,1)S(1)}, bf16[256,256]{1,0:T(8,128)(2,1)}, u32[]{:S(2)}) copy-start(bf16[256,256]{1,0:T(8,128)(2,1)} %constant.44.clone.refs_18_.refs_6_) | copy-start | bytes 393220
  7.0 14.7 %copy-start.16 = (f32[9]{0:T(128)S(1)}, f32[9]{0:T(128)}, u32[]{:S(2)}) copy-start(f32[9]{0:T(128)} %refs_1_.1) | copy-start | bytes 112
  7.0 14.7 %copy-start.17 = (f32[4]{0:T(128)S(1)}, f32[4]{0:T(128)}, u32[]{:S(2)}) copy-start(f32[4]{0:T(128)} %refs_2_.1) | copy-start | bytes 52
  7.1 14.7 %copy-start.18 = (f32[4]{0:T(128)S(1)}, f32[4]{0:T(128)}, u32[]{:S(2)}) copy-start(f32[4]{0:T(128)} %refs_3_.1) | copy-start | bytes 52
  7.1 6.6 %collective-permute-start.9 = (s32[2,72,128]{2,1,0:T(8,128)S(1)}, s32[2,72,128]{2,1,0:T(8,128)S(1)}, u32[]{:S(2)}, u32[]{:S(2)}) collective-permute-start(s32[2,72,128]{2,1,0:T(8,128)S(1)} %get-tuple-element.20), channel_id=1, source_target_pairs={{0,24},{8,16},{16,8},{24,0},{1,25},{9,17},{17,9},{25,1},{2,26},{10... | collective-permute-start | bytes 221192 | tf_op jit(solution)/shard_map/ppermute | solution.py:278
  11.1 4.4 %collective-permute-start.7 = (s32[2,72,128]{2,1,0:T(8,128)S(1)}, s32[2,72,128]{2,1,0:T(8,128)S(1)}, u32[]{:S(2)}, u32[]{:S(2)}) collective-permute-start(s32[2,72,128]{2,1,0:T(8,128)S(1)} %get-tuple-element.22), channel_id=1, source_target_pairs={{0,8},{8,0},{16,24},{24,16},{1,9},{9,1},{17,25},{25,17},{2,10},{10... | collective-permute-start | bytes 221192 | tf_op jit(solution)/shard_map/ppermute | solution.py:278
  13.6 8.0 %collective-permute-start = (f32[64,512]{1,0:T(8,128)S(1)}, f32[64,512]{1,0:T(8,128)S(1)}, u32[]{:S(2)}, u32[]{:S(2)}) collective-permute-start(f32[64,512]{1,0:T(8,128)S(1)} %bitcast.9), channel_id=1, source_target_pairs={{0,1},{1,0},{2,3},{3,2},{4,5},{5,4},{6,7},{7,6},{8,9},{9,8},{10,11... | collective-permute-start | bytes 393224 | tf_op jit(solution)/shard_map/ppermute | solution.py:278
  13.6 8.0 %collective-permute-start.6 = (f32[64,512]{1,0:T(8,128)S(1)}, f32[64,512]{1,0:T(8,128)S(1)}, u32[]{:S(2)}, u32[]{:S(2)}) collective-permute-start(f32[64,512]{1,0:T(8,128)S(1)} %collective-permute-done.5.refs_11_), channel_id=1, source_target_pairs={{0,1},{1,0},{2,3},{3,2},{4,5},{5,4},{6,7},{7,6},{8,9},{9,8},{10,11... | collective-permute-start | bytes 393224 | tf_op jit(solution)/shard_map/ppermute | solution.py:278
  14.1 7.5 %collective-permute-start.4 = (f32[64,512]{1,0:T(8,128)S(1)}, f32[64,512]{1,0:T(8,128)S(1)}, u32[]{:S(2)}, u32[]{:S(2)}) collective-permute-start(f32[64,512]{1,0:T(8,128)S(1)} %collective-permute-done.3.refs_9_), channel_id=1, source_target_pairs={{0,1},{1,0},{2,3},{3,2},{4,5},{5,4},{6,7},{7,6},{8,9},{9,8},{10,11... | collective-permute-start | bytes 393224 | tf_op jit(solution)/shard_map/ppermute | solution.py:278
  14.2 7.4 %collective-permute-start.2 = (f32[64,512]{1,0:T(8,128)S(1)}, f32[64,512]{1,0:T(8,128)S(1)}, u32[]{:S(2)}, u32[]{:S(2)}) collective-permute-start(f32[64,512]{1,0:T(8,128)S(1)} %collective-permute-done.1.refs_7_), channel_id=1, source_target_pairs={{0,1},{1,0},{2,3},{3,2},{4,5},{5,4},{6,7},{7,6},{8,9},{9,8},{10,11... | collective-permute-start | bytes 393224 | tf_op jit(solution)/shard_map/ppermute | solution.py:278
  15.5 6.1 %collective-permute-start.8 = (s32[2,72,128]{2,1,0:T(8,128)S(1)}, s32[2,72,128]{2,1,0:T(8,128)S(1)}, u32[]{:S(2)}, u32[]{:S(2)}) collective-permute-start(s32[2,72,128]{2,1,0:T(8,128)S(1)} %get-tuple-element.23), channel_id=1, source_target_pairs={{0,16},{8,24},{16,0},{24,8},{1,17},{9,25},{17,1},{25,9},{2,18},{10... | collective-permute-start | bytes 221192 | tf_op jit(solution)/shard_map/ppermute | solution.py:278
  21.6 0.7 %copy-start.14 = (f32[2,1,128]{2,1,0:T(1,128)S(1)}, f32[2,1,128]{2,1,0:T(1,128)}, u32[]{:S(2)}) copy-start(f32[2,1,128]{2,1,0:T(1,128)} %constant.56.clone.refs_30_) | copy-start | bytes 3076
  21.7 0.7 %copy-start.15 = (s32[1,1,4,1]{2,3,1,0:T(1,128)S(1)}, s32[1,1,4,1]{2,3,1,0:T(1,128)}, u32[]{:S(2)}) copy-start(s32[1,1,4,1]{2,3,1,0:T(1,128)} %param.27) | copy-start | bytes 52
  22.3 1.0 %copy-start.5 = (bf16[512,480]{1,0:T(8,128)(2,1)S(1)}, bf16[512,480]{1,0:T(8,128)(2,1)}, u32[]{:S(2)}) copy-start(bf16[512,480]{1,0:T(8,128)(2,1)} %constant.53.clone.refs_27_) | copy-start | bytes 1474564
  23.4 0.9 %copy-start.6 = (f32[256,256]{1,0:T(8,128)S(1)}, f32[256,256]{1,0:T(8,128)}, u32[]{:S(2)}) copy-start(f32[256,256]{1,0:T(8,128)} %constant.55.clone.refs_29_) | copy-start | bytes 786436
  24.3 0.9 %copy-start.7 = (f32[256,256]{1,0:T(8,128)S(1)}, f32[256,256]{1,0:T(8,128)}, u32[]{:S(2)}) copy-start(f32[256,256]{1,0:T(8,128)} %constant.54.clone.refs_28_) | copy-start | bytes 786436
  25.3 0.9 %copy-start.8 = (bf16[160,512]{1,0:T(8,128)(2,1)S(1)}, bf16[160,512]{1,0:T(8,128)(2,1)}, u32[]{:S(2)}) copy-start(bf16[160,512]{1,0:T(8,128)(2,1)} %constant.52.clone.refs_26_) | copy-start | bytes 491524
  26.2 0.9 %copy-start.9 = (bf16[160,512]{1,0:T(8,128)(2,1)S(1)}, bf16[160,512]{1,0:T(8,128)(2,1)}, u32[]{:S(2)}) copy-start(bf16[160,512]{1,0:T(8,128)(2,1)} %constant.51.clone.refs_25_) | copy-start | bytes 491524
  27.1 0.9 %copy-start.10 = (bf16[256,256]{1,0:T(8,128)(2,1)S(1)}, bf16[256,256]{1,0:T(8,128)(2,1)}, u32[]{:S(2)}) copy-start(bf16[256,256]{1,0:T(8,128)(2,1)} %constant.50.clone.refs_24_) | copy-start | bytes 393220
  28.0 0.9 %copy-start.11 = (bf16[256,256]{1,0:T(8,128)(2,1)S(1)}, bf16[256,256]{1,0:T(8,128)(2,1)}, u32[]{:S(2)}) copy-start(bf16[256,256]{1,0:T(8,128)(2,1)} %constant.49.clone.refs_23_) | copy-start | bytes 393220
  28.9 0.9 %copy-start.12 = (bf16[256,256]{1,0:T(8,128)(2,1)S(1)}, bf16[256,256]{1,0:T(8,128)(2,1)}, u32[]{:S(2)}) copy-start(bf16[256,256]{1,0:T(8,128)(2,1)} %constant.48.clone.refs_22_) | copy-start | bytes 393220
  29.8 0.9 %copy-start.13 = (bf16[256,256]{1,0:T(8,128)(2,1)S(1)}, bf16[256,256]{1,0:T(8,128)(2,1)}, u32[]{:S(2)}) copy-start(bf16[256,256]{1,0:T(8,128)(2,1)} %constant.47.clone.refs_21_) | copy-start | bytes 393220
  36.1 1.4 %collective-permute-start.11 = (f32[64,512]{1,0:T(8,128)S(1)}, f32[64,512]{1,0:T(8,128)S(1)}, u32[]{:S(2)}, u32[]{:S(2)}) collective-permute-start(f32[64,512]{1,0:T(8,128)S(1)} %get-tuple-element.14), channel_id=1, source_target_pairs={{0,1},{1,0},{2,3},{3,2},{4,5},{5,4},{6,7},{7,6},{8,9},{9,8},{10,11... | collective-permute-start | bytes 393224 | tf_op jit(solution)/shard_map/ppermute | solution.py:278
  36.1 3.9 %collective-permute-start.13 = (f32[64,512]{1,0:T(8,128)S(1)}, f32[64,512]{1,0:T(8,128)S(1)}, u32[]{:S(2)}, u32[]{:S(2)}) collective-permute-start(f32[64,512]{1,0:T(8,128)S(1)} %get-tuple-element.16), channel_id=1, source_target_pairs={{0,1},{1,0},{2,3},{3,2},{4,5},{5,4},{6,7},{7,6},{8,9},{9,8},{10,11... | collective-permute-start | bytes 393224 | tf_op jit(solution)/shard_map/ppermute | solution.py:278
  36.6 4.0 %collective-permute-start.15 = (f32[64,512]{1,0:T(8,128)S(1)}, f32[64,512]{1,0:T(8,128)S(1)}, u32[]{:S(2)}, u32[]{:S(2)}) collective-permute-start(f32[64,512]{1,0:T(8,128)S(1)} %get-tuple-element.18), channel_id=1, source_target_pairs={{0,1},{1,0},{2,3},{3,2},{4,5},{5,4},{6,7},{7,6},{8,9},{9,8},{10,11... | collective-permute-start | bytes 393224 | tf_op jit(solution)/shard_map/ppermute | solution.py:278
  36.7 4.5 %collective-permute-start.10 = (f32[64,512]{1,0:T(8,128)S(1)}, f32[64,512]{1,0:T(8,128)S(1)}, u32[]{:S(2)}, u32[]{:S(2)}) collective-permute-start(f32[64,512]{1,0:T(8,128)S(1)} %get-tuple-element.12), channel_id=1, source_target_pairs={{0,1},{1,0},{2,3},{3,2},{4,5},{5,4},{6,7},{7,6},{8,9},{9,8},{10,11... | collective-permute-start | bytes 393224 | tf_op jit(solution)/shard_map/ppermute | solution.py:278
  37.5 6.6 %collective-permute-start.12 = (f32[64,512]{1,0:T(8,128)S(1)}, f32[64,512]{1,0:T(8,128)S(1)}, u32[]{:S(2)}, u32[]{:S(2)}) collective-permute-start(f32[64,512]{1,0:T(8,128)S(1)} %add.29), channel_id=1, source_target_pairs={{0,6},{1,7},{2,4},{3,5},{4,2},{5,3},{6,0},{7,1},{8,14},{9,15},{10,... | collective-permute-start | bytes 393224 | tf_op jit(solution)/shard_map/ppermute | solution.py:278
  40.0 6.8 %collective-permute-start.14 = (f32[64,512]{1,0:T(8,128)S(1)}, f32[64,512]{1,0:T(8,128)S(1)}, u32[]{:S(2)}, u32[]{:S(2)}) collective-permute-start(f32[64,512]{1,0:T(8,128)S(1)} %add.30), channel_id=1, source_target_pairs={{0,4},{1,5},{2,6},{3,7},{4,0},{5,1},{6,2},{7,3},{8,12},{9,13},{10,... | collective-permute-start | bytes 393224 | tf_op jit(solution)/shard_map/ppermute | solution.py:278
  40.6 6.3 %collective-permute-start.16 = (f32[64,512]{1,0:T(8,128)S(1)}, f32[64,512]{1,0:T(8,128)S(1)}, u32[]{:S(2)}, u32[]{:S(2)}) collective-permute-start(f32[64,512]{1,0:T(8,128)S(1)} %add.31), channel_id=1, source_target_pairs={{0,2},{1,3},{2,0},{3,1},{4,6},{5,7},{6,4},{7,5},{8,10},{9,11},{10,... | collective-permute-start | bytes 393224 | tf_op jit(solution)/shard_map/ppermute | solution.py:278
where the time goes:
time: 48.2 us; the launch traced here: 47.8 us
  starting transfers between devices  15.2 us (32%)
  waiting for transfers between devices  14.7 us (30%)
  local copies, waits for them, and re-layouts  9.76 us (20%)
  Pallas kernels  6.25 us (13%)
  other arithmetic  1.1 us (2%)
  between operations  0.82 us (2%)
    ppermute x17, starting transfers between devices, swap(): return lax.ppermute(value, axis, [(i, i ^ k) for i in range(size)])  15.2 us
    ppermute x17, waiting for transfers between devices, swap(): return lax.ppermute(value, axis, [(i, i ^ k) for i in range(size)])  14.7 us
    unnamed x42, local copies, waits for them, and re-layouts  9.69 us
    pallas_call x1, Pallas kernels, local(): pl.pallas_call(functools.partial(main_kernel, n, groups, rows, side, tile...  5.33 us
    concatenate x1, other arithmetic, local(): jnp.concatenate([counts.reshape(slots, rows, TC), jnp.broadcast_to(depth....  1.03 us
  transfers between devices with their start and end apart: 17, of which 7 were waited for; matrix products, arithmetic and copies ran while one was open for 2% of the time, Pallas kernels for 0%

commit v1 on v0

--- a/solution.py
+++ b/solution.py
@@ -15,6 +15,7 @@
 PIVOT = 1.0
 GROWTH = 7.0 / 8.0
 PAD = 16
+MIB = 1024 * 1024
 VMEM = pltpu.VMEM
 F32 = jnp.float32
 BF16 = jnp.bfloat16
@@ -55,24 +56,56 @@
     weight = np.where(freqs == 0, 1.0, 2.0)
     gain = AMPLITUDE * (np.sqrt(wave_sq) / PIVOT) / (1.0 + wave_sq / PIVOT**2)
     gain = gain * weight[:, None] * weight[None, :] / (side * side)
-    views_h, views_l = split_np(views)
-    up = views.T
-    up_h, up_l = split_np(up)
-    tables = []
+    sections = []
     for table in (even, odd, even.T, odd.T):
-        tables.extend(split_np(np.ascontiguousarray(table)))
-    fwd = tuple(tables[:4])
-    back = tuple(tables[4:])
-    waves = np.repeat(wave.reshape(2, quarter).astype(np.float32)[:, None, :], 1, axis=1)
-    return dict(
-        fwd=fwd,
-        back=back,
-        views=(views_h, views_l),
-        lift=np.concatenate([up_h, up_h, up_l], axis=1),
-        gain=gain.astype(np.float32),
-        inverse=inverse.astype(np.float32),
-        waves=waves,
-    )
+        sections.append(np.concatenate(split_np(np.ascontiguousarray(table)), axis=1))
+    sections.extend(split_np(views))
+    up_h, up_l = split_np(np.ascontiguousarray(views.T))
+    lift = np.concatenate([up_h, up_h, up_l], axis=1)
+    sections.append(np.concatenate([lift, np.zeros((side, side - lift.shape[1]), lift.dtype)], axis=1))
+    waves = np.zeros((8, half))
+    waves[:] = wave[None, :]
+    return np.concatenate(sections), np.concatenate([gain, inverse, waves]).astype(np.float32)
+
+
+class Tables:
+    def __init__(self, packed, reals, side, ring):
+        half = side // 2
+        self.half = half
+        self.ring = ring
+        self.packed = packed
+        self.reals = reals
+        self.lift_at = 4 * half + 4 * ring
+
+    def _pair(self, at):
+        half = self.half
+        return self.packed[at : at + half, :half], self.packed[at : at + half, half:]
+
+    def fwd(self, par):
+        return self._pair(par * self.half)
+
+    def back(self, par):
+        return self._pair((2 + par) * self.half)
+
+    def views(self):
+        at, count = 4 * self.half, 2 * self.ring
+        return self.packed[at : at + count, :], self.packed[at + count : at + 2 * count, :]
+
+    def lift(self, start, count):
+        return self.packed[self.lift_at + start : self.lift_at + start + count, : 6 * self.ring]
+
+    def gain(self, par, ypar):
+        q = self.half // 2
+        return self.reals[par * q : (par + 1) * q, ypar * q : (ypar + 1) * q]
+
+    def inverse(self, par, ypar):
+        q, half = self.half // 2, self.half
+        return self.reals[half + par * q : half + (par + 1) * q, ypar * q : (ypar + 1) * q]
+
+    def waves(self):
+        q, half = self.half // 2, self.half
+        row = self.reals[2 * half : 2 * half + 1, :]
+        return row[:, :q], row[:, q:]
 
 
 def mm(a, b):
@@ -114,30 +147,22 @@
     half, q = side // 2, side // 4
     ring = rows + PAD
     refs = list(refs)
-    owner, stencil, mean_counts, bias_one, bias_two = refs[:5]
+    small = refs[:5]
     blocks = refs[5 : 5 + n]
     msgs = refs[5 + n : 5 + n + groups]
     rest = refs[5 + n + groups :]
-    eh, el, oh, ol, teh, tel, toh, tol, vh, vl, lift, gain, inverse, waves = rest[:14]
-    density_out = rest[14]
-    outs = rest[15 : 15 + n]
-    fh, fl, yh, yl, zh, zl, cnt, cls, part = rest[15 + n :]
+    tabs = Tables(rest[0], rest[1], side, ring)
+    density_out = rest[2]
+    outs = rest[3 : 3 + n]
+    fh, fl, yh, yl, zh, zl, cnt, cls, part = rest[3 + n : 12 + n]
+    held = rest[12 + n : 17 + n]
+    sems = rest[17 + n]
+    owner, stencil, mean_counts, bias_one, bias_two = held
+    copies = [pltpu.make_async_copy(a, b, sems.at[i]) for i, (a, b) in enumerate(zip(small, held))]
+    for copy in copies:
+        copy.start()
     me = lax.axis_index("gy")
     mine = lax.axis_index("gx")
-    fwd = ((eh, el), (oh, ol))
-    back = ((teh, tel), (toh, tol))
-
-    for t in range(tiles):
-        rank = jnp.int32(0)
-        for t2 in range(t):
-            rank = rank + (owner[t2] == owner[t]).astype(jnp.int32)
-        which = lax.bitwise_xor(owner[t], mine)
-        for k in range(groups):
-
-            @pl.when(which == k)
-            def _():
-                cnt[:, t * TC : (t + 1) * TC] = msgs[k][rank, :rows, :].astype(F32)
-                cls[:, t * TC : (t + 1) * TC] = msgs[k][rank, rows : rows + 8, :]
 
     for k in range(n // 2):
         a, b = blocks[k][...], blocks[k ^ (n // 2)][...]
@@ -154,14 +179,14 @@
     for par in range(2):
         for ypar in range(2):
             cols = slice(ypar * half, (ypar + 1) * half)
-            y = mm3((fh[par, :, cols], fl[par, :, cols]), tuple(r[...] for r in back[ypar]))
+            y = mm3((fh[par, :, cols], fl[par, :, cols]), tabs.back(ypar))
             yh[par, :, cols], yl[par, :, cols] = split(y)
     for par in range(2):
         for ypar in range(2):
             cols = slice(ypar * half, (ypar + 1) * half)
-            x = mm3(tuple(r[...] for r in fwd[par]), (yh[par, :, cols], yl[par, :, cols]))
-            g = gain[par * q : (par + 1) * q, ypar * q : (ypar + 1) * q]
-            inv = inverse[par * q : (par + 1) * q, ypar * q : (ypar + 1) * q]
+            x = mm3(tabs.fwd(par), (yh[par, :, cols], yl[par, :, cols]))
+            g = tabs.gain(par, ypar)
+            inv = tabs.inverse(par, ypar)
             for i in range(2):
                 for j in range(2):
                     base = x[i * q : (i + 1) * q, j * q : (j + 1) * q] * g
@@ -171,18 +196,33 @@
                     zh[rs, c0 : c0 + q], zl[rs, c0 : c0 + q] = split(base)
                     zh[rs, side + c0 : side + c0 + q], zl[rs, side + c0 : side + c0 + q] = split(phi)
 
-    w = mm3((vh[...], vl[...]), (zh[...], zl[...]))
-    ky = (waves[0], waves[1])
+    w = mm3(tabs.views(), (zh[...], zl[...]))
+    ky = tabs.waves()
     base, base_x = w[:ring, :side], w[ring:, :side]
     phi, phi_x = w[:ring, side:], w[ring:, side:]
     stack = jnp.concatenate([base, phi_x, slope_lanes(phi, ky, 1.0), base_x, slope_lanes(base, ky, 1.0)], axis=0)
     sh, sl = split(stack)
-    e = mm3((sh[:, :half], sl[:, :half]), (eh[...], el[...]))
-    o = mm3((sh[:, half:], sl[:, half:]), (oh[...], ol[...]))
+    e = mm3((sh[:, :half], sl[:, :half]), tabs.fwd(0))
+    o = mm3((sh[:, half:], sl[:, half:]), tabs.fwd(1))
     fields = jnp.concatenate([e + o, e - o], axis=1)
     linear, shift_x, shift_y, slope_x, slope_y = [fields[i * ring : (i + 1) * ring] for i in range(5)]
     density = linear + GROWTH * linear * linear - (shift_x * slope_x + shift_y * slope_y)
     density_out[...] = density[:rows]
+
+    for copy in copies:
+        copy.wait()
+
+    for t in range(tiles):
+        rank = jnp.int32(0)
+        for t2 in range(t):
+            rank = rank + (owner[t2] == owner[t]).astype(jnp.int32)
+        which = lax.bitwise_xor(owner[t], mine)
+        for k in range(groups):
+
+            @pl.when(which == k)
+            def _():
+                cnt[:, t * TC : (t + 1) * TC] = msgs[k][rank, :rows, :].astype(F32)
+                cls[:, t * TC : (t + 1) * TC] = msgs[k][rank, rows : rows + 8, :]
 
     beside = {0: density, 1: turn_lanes(density, -1), -1: turn_lanes(density, 1)}
     smooth = jnp.zeros_like(density)
@@ -218,8 +258,8 @@
         axis=0,
     )
     lo, hi = bars[:, :half], bars[:, half:]
-    ye = mm3(split(lo + hi), (teh[...], tel[...]))
-    yo = mm3(split(lo - hi), (toh[...], tol[...]))
+    ye = mm3(split(lo + hi), tabs.back(0))
+    yo = mm3(split(lo - hi), tabs.back(1))
     modes = jnp.concatenate([ye, yo], axis=1)
     m_lin, m_sx, m_sy, m_gx, m_gy = [modes[i * ring : (i + 1) * ring] for i in range(5)]
     to_base = m_lin + slope_lanes(m_gy, ky, -1.0)
@@ -228,22 +268,21 @@
         [jnp.concatenate([to_base, to_phi], axis=1), jnp.concatenate([m_gx, m_sx], axis=1)], axis=0
     )
     ph, plow = split(pile)
-    zeros = jnp.zeros((lift.shape[1] - 3 * 2 * ring, 2 * side), BF16)
-    pile3 = jnp.concatenate([ph, plow, ph] + ([zeros] if zeros.shape[0] else []), axis=0)
+    pile3 = jnp.concatenate([ph, plow, ph], axis=0)
 
     for par in range(2):
         for i in range(2):
             rs = slice(par * half + i * q, par * half + (i + 1) * q)
-            x = mm(lift[rs, :], pile3)
+            x = mm(tabs.lift(rs.start, q), pile3)
             for ypar in range(2):
-                g = gain[par * q : (par + 1) * q, ypar * q : (ypar + 1) * q]
-                inv = inverse[par * q : (par + 1) * q, ypar * q : (ypar + 1) * q]
+                g = tabs.gain(par, ypar)
+                inv = tabs.inverse(par, ypar)
                 for j in range(2):
                     c0 = ypar * half + j * q
                     d = g * (x[:, c0 : c0 + q] + inv * x[:, side + c0 : side + c0 + q])
                     yh[par, i * q : (i + 1) * q, c0 : c0 + q], yl[par, i * q : (i + 1) * q, c0 : c0 + q] = split(d)
-    e = mm3((teh[...], tel[...]), (yh[0], yl[0]))
-    o = mm3((toh[...], tol[...]), (yh[1], yl[1]))
+    e = mm3(tabs.back(0), (yh[0], yl[0]))
+    o = mm3(tabs.back(1), (yh[1], yl[1]))
     part[0] = e + o
     part[1] = e - o
     for k in range(n):
@@ -252,16 +291,58 @@
         outs[k][...] = part[place // (n // 2), pl.ds(off, rows), :]
 
 
+def message_kernel(groups, capacity, rows, counts, depth, noise, *refs):
+    msgs = refs[:groups]
+    noise_out, classes, sems = refs[groups:]
+    mine = lax.axis_index("gx")
+    first = pltpu.make_async_copy(depth, classes, sems.at[groups])
+    first.start()
+    copies = []
+    for k in range(groups):
+        start = lax.bitwise_xor(mine, k) * capacity
+        copies.append(
+            pltpu.make_async_copy(
+                counts.at[pl.ds(start, capacity)], msgs[k].at[:, pl.ds(0, rows), :], sems.at[k]
+            )
+        )
+        copies[k].start()
+    copies.append(pltpu.make_async_copy(noise, noise_out, sems.at[groups + 1]))
+    copies[groups].start()
+    first.wait()
+    for k in range(groups):
+        start = lax.bitwise_xor(mine, k) * capacity
+        for r in range(capacity):
+            msgs[k][r, rows : rows + 8, :] = jnp.full((8, TC), classes[start + r], jnp.int32)
+    for copy in copies:
+        copy.wait()
+
+
+def table_kernel(packed, reals, packed_out, reals_out, sems):
+    copies = [
+        pltpu.make_async_copy(packed, packed_out, sems.at[0]),
+        pltpu.make_async_copy(reals, reals_out, sems.at[1]),
+    ]
+    for copy in copies:
+        copy.start()
+    for copy in copies:
+        copy.wait()
+
+
+def in_hbm(value):
+    return pltpu.with_memory_space_constraint(value, pltpu.HBM)
+
+
 def last_kernel(count, *refs):
     parts = refs[:count]
-    noise, eh, el, oh, ol, out = refs[count:]
+    noise, packed, out = refs[count:]
     total = parts[0][...]
     for p in parts[1:]:
         total = total + p[...]
     half = total.shape[1] // 2
+    tabs = Tables(packed, None, 2 * half, 0)
     sh, sl = split(total)
-    e = mm3((sh[:, :half], sl[:, :half]), (eh[...], el[...]))
-    o = mm3((sh[:, half:], sl[:, half:]), (oh[...], ol[...]))
+    e = mm3((sh[:, :half], sl[:, :half]), tabs.fwd(0))
+    o = mm3((sh[:, half:], sl[:, half:]), tabs.fwd(1))
     out[:, :half] = e + o - noise[:, :half]
     out[:, half:] = e - o - noise[:, half:]
 
@@ -272,51 +353,50 @@
     tiles = side // TC
     slots = counts.shape[1]
     capacity = slots // groups
-    tables = make_tables(side, rows)
+    packed, reals = [jnp.asarray(t) for t in make_tables(side, rows)]
+    vmem = pl.BlockSpec(memory_space=VMEM)
+    hbm = pl.BlockSpec(memory_space=pltpu.HBM)
 
     def swap(value, k, axis="gy", size=n):
         return lax.ppermute(value, axis, [(i, i ^ k) for i in range(size)])
 
-    blocks = {0: own}
+    blocks = {}
     for k in range(n - 2, 0, -2):
         blocks[k] = swap(own, k)
-    blocks[1] = swap(own, 1)
-    mine = lax.axis_index("gx")
-    message = jnp.concatenate(
-        [
-            counts.reshape(slots, rows, TC),
-            jnp.broadcast_to(depth.reshape(slots, 1, 1), (slots, 8, TC)),
-        ],
-        axis=1,
-    )
-    msgs = []
-    for k in range(groups):
-        piece = lax.dynamic_slice_in_dim(message, lax.bitwise_xor(mine, k) * capacity, capacity, 0)
-        msgs.append(swap(piece, k, "gx", groups) if k else piece)
-    for k in range(2, n, 2):
+    *msgs, held_own = pl.pallas_call(
+        functools.partial(message_kernel, groups, capacity, rows),
+        out_shape=[VMEM((capacity, rows + 8, TC), jnp.int32)] * groups + [VMEM((rows, side), F32)],
+        in_specs=[hbm] * 3,
+        out_specs=[vmem] * (groups + 1),
+        scratch_shapes=[pltpu.SMEM((slots,), jnp.int32), pltpu.SemaphoreType.DMA((groups + 2,))],
+        compiler_params=pltpu.CompilerParams(vmem_limit_bytes=4 * MIB),
+        name="messages",
+    )(in_hbm(counts.reshape(slots, rows, TC)), in_hbm(depth.reshape(slots)), in_hbm(own))
+    for k in range(groups - 1, 0, -1):
+        if k == 1:
+            msgs[k], _ = lax.optimization_barrier((msgs[k], blocks[n - 2]))
+        msgs[k] = swap(msgs[k], k, "gx", groups)
+    blocks[0], _ = lax.optimization_barrier((held_own, blocks[n - 2]))
+    blocks[1] = swap(blocks[0], 1)
+    for k in range(n - 2, 0, -2):
         blocks[k + 1] = swap(blocks[k], 1)
-
-    ring = rows + PAD
+    packed, reals, _ = lax.optimization_barrier((packed, reals, blocks[n - 2]))
+    packed, reals = pl.pallas_call(
+        table_kernel,
+        out_shape=[VMEM(t.shape, t.dtype) for t in (packed, reals)],
+        in_specs=[hbm] * 2,
+        out_specs=[vmem] * 2,
+        scratch_shapes=[pltpu.SemaphoreType.DMA((2,))],
+        compiler_params=pltpu.CompilerParams(vmem_limit_bytes=4 * MIB),
+        name="tables",
+    )(in_hbm(packed), in_hbm(reals))
     half = side // 2
-    smem = pl.BlockSpec(memory_space=pltpu.SMEM)
-    vmem = pl.BlockSpec(memory_space=VMEM)
-    consts = [
-        jnp.asarray(t)
-        for t in (
-            *tables["fwd"],
-            *tables["back"],
-            *tables["views"],
-            tables["lift"],
-            tables["gain"],
-            tables["inverse"],
-            tables["waves"],
-        )
-    ]
     cell = jax.ShapeDtypeStruct((rows, side), F32)
+    small = (owner.reshape(tiles), stencil, mean_counts, bias_one, bias_two)
     density, *parts = pl.pallas_call(
         functools.partial(main_kernel, n, groups, rows, side, tiles),
         out_shape=[cell] * (1 + n),
-        in_specs=[smem] * 5 + [vmem] * (n + groups + len(consts)),
+        in_specs=[hbm] * 5 + [vmem] * (n + groups + 2),
         out_specs=[vmem] * (1 + n),
         scratch_shapes=[
             VMEM((2, half, side), BF16),
@@ -328,18 +408,17 @@
             VMEM((rows, side), F32),
             VMEM((8, side), jnp.int32),
             VMEM((2, half, side), F32),
+            *[pltpu.SMEM(a.shape, a.dtype) for a in small],
+            pltpu.SemaphoreType.DMA((5,)),
         ],
-        compiler_params=pltpu.CompilerParams(vmem_limit_bytes=32 * 1024 * 1024),
+        compiler_params=pltpu.CompilerParams(vmem_limit_bytes=16 * MIB),
         name="fields_and_adjoint",
     )(
-        owner.reshape(tiles),
-        stencil,
-        mean_counts,
-        bias_one,
-        bias_two,
+        *[in_hbm(a) for a in small],
         *[blocks[k] for k in range(n)],
         *msgs,
-        *consts,
+        packed,
+        reals,
     )
     sums = {}
     for k in range(n - 2, -1, -2):
@@ -348,11 +427,11 @@
     gradient = pl.pallas_call(
         functools.partial(last_kernel, len(pieces)),
         out_shape=cell,
-        in_specs=[vmem] * (len(pieces) + 5),
+        in_specs=[vmem] * (len(pieces) + 2),
         out_specs=vmem,
-        compiler_params=pltpu.CompilerParams(vmem_limit_bytes=32 * 1024 * 1024),
+        compiler_params=pltpu.CompilerParams(vmem_limit_bytes=8 * MIB),
         name="sum_and_rows",
-    )(*pieces, own, *consts[:4])
+    )(*pieces, blocks[0], packed)
     return (gradient.reshape(1, rows, side), density.reshape(1, rows, side))
 
 

time: 48.2 us -> 37.1 us (0.77)
  local copies, waits for them, and re-layouts: 9.76 us -> 0 us
  Pallas kernels: 6.25 us -> 8.82 us
  waiting for transfers between devices: 14.7 us -> 12.4 us
  other arithmetic: 1.1 us -> 0.08 us
    unnamed x42 -> x0, local copies, waits for them, and re-layouts: 9.69 us -> none
    pallas_call x0 -> x2, Pallas kernels: none -> 2.72 us  [the longest x1 1.63 us: local(): pl.pallas_call(table_kernel, out_shape=[VMEM(t.shape, t.dtype) for t in (...]
    ppermute x17, waiting for transfers between devices: 14.7 us -> 12.4 us  [swap(): return lax.ppermute(value, axis, [(i, i ^ k) for i in range(size)])]
    concatenate x1 -> x0, other arithmetic: 1.03 us -> none  [local(): jnp.concatenate([counts.reshape(slots, rows, TC), jnp.broadcast_to(depth....]
  transfers between devices with their start and end apart: 17 -> 17, of which waited for: 7 -> 9; matrix products, arithmetic and copies ran while one was open for 2% -> 0% of each run, Pallas kernels for 0% -> 7%
where the time goes in v1:
time: 37.1 us; the launch traced here: 37 us
  starting transfers between devices  14.9 us (40%)
  waiting for transfers between devices  12.4 us (33%)
  Pallas kernels  8.82 us (24%)
  between operations  0.7 us (2%)
    ppermute x17, starting transfers between devices, swap(): return lax.ppermute(value, axis, [(i, i ^ k) for i in range(size)])  14.9 us
    ppermute x17, waiting for transfers between devices, swap(): return lax.ppermute(value, axis, [(i, i ^ k) for i in range(size)])  12.4 us
    pallas_call x1, Pallas kernels, local(): pl.pallas_call(functools.partial(main_kernel, n, groups, rows, side, tile...  5.19 us
    pallas_call x1, Pallas kernels, local(): pl.pallas_call(table_kernel, out_shape=[VMEM(t.shape, t.dtype) for t in (...  1.63 us
    pallas_call x1, Pallas kernels, local(): pl.pallas_call(functools.partial(message_kernel, groups, capacity, rows),...  1.09 us
    pallas_call x1, Pallas kernels, local(): pl.pallas_call(functools.partial(last_kernel, len(pieces)), out_shape=cel...  0.9 us
  transfers between devices with their start and end apart: 17, of which 9 were waited for; matrix products, arithmetic and copies ran while one was open for 0% of the time, Pallas kernels for 7%

profile of v1, /device:TPU:0, one launch (start us, length us, event | category | flops | bytes accessed | tf_op | source)
XLA Modules:
  0.0 37.0 jit_solution(14662926136466859531)
XLA Ops:
  0.6 4.0 %collective-permute-start = (f32[64,512]{1,0:T(8,128)}, f32[64,512]{1,0:T(8,128)S(1)}, u32[]{:S(2)}, u32[]{:S(2)}) collective-permute-start(f32[64,512]{1,0:T(8,128)} %bitcast.7), channel_id=1, source_target_pairs={{0,6},{1,7},{2,4},{3,5},{4,2},{5,3},{6,0},{7,1},{8,14},{9,15},{10,... | collective-permute-start | bytes 393224 | tf_op jit(solution)/shard_map/ppermute | solution.py:361
  4.6 0.5 %collective-permute-start.4 = (f32[64,512]{1,0:T(8,128)}, f32[64,512]{1,0:T(8,128)S(1)}, u32[]{:S(2)}, u32[]{:S(2)}) collective-permute-start(f32[64,512]{1,0:T(8,128)} %bitcast.8), channel_id=1, source_target_pairs={{0,4},{1,5},{2,6},{3,7},{4,0},{5,1},{6,2},{7,3},{8,12},{9,13},{10,... | collective-permute-start | bytes 393224 | tf_op jit(solution)/shard_map/ppermute | solution.py:361
  5.1 0.1 collective-permute-start.2
  5.2 1.1 %messages.1 = (s32[2,72,128]{2,1,0:T(8,128)S(1)}, s32[2,72,128]{2,1,0:T(8,128)S(1)}, s32[2,72,128]{2,1,0:T(8,128)S(1)}, s32[2,72,128]{2,1,0:T(8,128)S(1)}, f32[64,512]{1,0:T(8,128)S(1)}) custom-call(s32[8,64,128]{2,1,0:T(8,128)} %bitcast.6, s32[8]{0:T(128)} %bitcast.12, f32[64,512]{1,0:T(8,128)} %bitcast.10), custom_call_target="tpu_custom_call" | custom-call | tf_op jit(solution)/shard_map/messages/pallas_call | solution.py:366
  6.3 3.1 %collective-permute-start.8 = (s32[2,72,128]{2,1,0:T(8,128)S(1)}, s32[2,72,128]{2,1,0:T(8,128)S(1)}, u32[]{:S(2)}, u32[]{:S(2)}) collective-permute-start(s32[2,72,128]{2,1,0:T(8,128)S(1)} %get-tuple-element.27), channel_id=1, source_target_pairs={{0,16},{8,24},{16,0},{24,8},{1,17},{9,25},{17,1},{25,9},{2,18},{10... | collective-permute-start | bytes 221192 | tf_op jit(solution)/shard_map/ppermute | solution.py:361
  9.4 1.3 %collective-permute-start.9 = (s32[2,72,128]{2,1,0:T(8,128)S(1)}, s32[2,72,128]{2,1,0:T(8,128)S(1)}, u32[]{:S(2)}, u32[]{:S(2)}) collective-permute-start(s32[2,72,128]{2,1,0:T(8,128)S(1)} %get-tuple-element.28), channel_id=1, source_target_pairs={{0,24},{8,16},{16,8},{24,0},{1,25},{9,17},{17,9},{25,1},{2,26},{10... | collective-permute-start | bytes 221192 | tf_op jit(solution)/shard_map/ppermute | solution.py:361
  10.7 0.0 collective-permute-done.refs_11_
  10.7 0.0 collective-permute-start.6
  10.7 0.4 collective-permute-done.4.refs_9_
  11.1 0.1 collective-permute-start.5
  11.3 0.1 collective-permute-done.2.refs_7_
  11.4 0.3 collective-permute-start.3
  11.6 0.5 %collective-permute-done.8.refs_15_ = s32[2,72,128]{2,1,0:T(8,128)S(1)} collective-permute-done((s32[2,72,128]{2,1,0:T(8,128)S(1)}, s32[2,72,128]{2,1,0:T(8,128)S(1)}, u32[]{:S(2)}, u32[]{:S(2)}) %collective-permute-start.8) | collective-permute-done | bytes 73760 | tf_op jit(solution)/shard_map/ppermute | solution.py:361
  12.1 0.0 collective-permute-start.1
  12.1 3.6 %collective-permute-done.9.refs_16_ = s32[2,72,128]{2,1,0:T(8,128)S(1)} collective-permute-done((s32[2,72,128]{2,1,0:T(8,128)S(1)}, s32[2,72,128]{2,1,0:T(8,128)S(1)}, u32[]{:S(2)}, u32[]{:S(2)}) %collective-permute-start.9) | collective-permute-done | bytes 73760 | tf_op jit(solution)/shard_map/ppermute | solution.py:361
  15.6 0.7 %collective-permute-start.7 = (s32[2,72,128]{2,1,0:T(8,128)S(1)}, s32[2,72,128]{2,1,0:T(8,128)S(1)}, u32[]{:S(2)}, u32[]{:S(2)}) collective-permute-start(s32[2,72,128]{2,1,0:T(8,128)S(1)} %get-tuple-element.26), channel_id=1, source_target_pairs={{0,8},{8,0},{16,24},{24,16},{1,9},{9,1},{17,25},{25,17},{2,10},{10... | collective-permute-start | bytes 221192 | tf_op jit(solution)/shard_map/ppermute | solution.py:361
  16.4 1.6 %tables.1 = (bf16[1856,512]{1,0:T(8,128)(2,1)S(1)}, f32[520,256]{1,0:T(8,128)S(1)}) custom-call(bf16[1856,512]{1,0:T(8,128)(2,1)} %constant.4.clone.packed, f32[520,256]{1,0:T(8,128)} %constant.5.clone.reals), custom_call_target="tpu_custom_call" | custom-call | tf_op jit(solution)/shard_map/tables/pallas_call | solution.py:384
  18.0 2.0 %collective-permute-done.7.refs_14_ = s32[2,72,128]{2,1,0:T(8,128)S(1)} collective-permute-done((s32[2,72,128]{2,1,0:T(8,128)S(1)}, s32[2,72,128]{2,1,0:T(8,128)S(1)}, u32[]{:S(2)}, u32[]{:S(2)}) %collective-permute-start.7) | collective-permute-done | bytes 73760 | tf_op jit(solution)/shard_map/ppermute | solution.py:361
  20.0 0.0 collective-permute-done.5.refs_10_
  20.0 0.0 collective-permute-done.3.refs_8_
  20.0 0.0 collective-permute-done.6.refs_12_
  20.0 0.0 collective-permute-done.1.refs_6_
  20.0 5.2 %fields_and_adjoint.1 = (f32[64,512]{1,0:T(8,128)}, f32[64,512]{1,0:T(8,128)S(1)}, f32[64,512]{1,0:T(8,128)S(1)}, f32[64,512]{1,0:T(8,128)S(1)}, f32[64,512]{1,0...) custom-call(s32[4]{0:T(128)} %bitcast.13, ...), custom_call_target="tpu_custom_call" | custom-call | tf_op jit(solution)/shard_map/fields_and_adjoint/pallas_call | solution.py:396
  25.2 0.1 collective-permute-start.11
  25.3 0.5 %collective-permute-start.13 = (f32[64,512]{1,0:T(8,128)S(1)}, f32[64,512]{1,0:T(8,128)S(1)}, u32[]{:S(2)}, u32[]{:S(2)}) collective-permute-start(f32[64,512]{1,0:T(8,128)S(1)} %get-tuple-element.38), channel_id=1, source_target_pairs={{0,1},{1,0},{2,3},{3,2},{4,5},{5,4},{6,7},{7,6},{8,9},{9,8},{10,11... | collective-permute-start | bytes 393224 | tf_op jit(solution)/shard_map/ppermute | solution.py:361
  25.8 0.1 collective-permute-start.15
  25.9 0.4 %collective-permute-start.10 = (f32[64,512]{1,0:T(8,128)S(1)}, f32[64,512]{1,0:T(8,128)S(1)}, u32[]{:S(2)}, u32[]{:S(2)}) collective-permute-start(f32[64,512]{1,0:T(8,128)S(1)} %get-tuple-element.34), channel_id=1, source_target_pairs={{0,1},{1,0},{2,3},{3,2},{4,5},{5,4},{6,7},{7,6},{8,9},{9,8},{10,11... | collective-permute-start | bytes 393224 | tf_op jit(solution)/shard_map/ppermute | solution.py:361
  26.3 0.3 collective-permute-done.11
  26.7 2.5 %collective-permute-start.12 = (f32[64,512]{1,0:T(8,128)S(1)}, f32[64,512]{1,0:T(8,128)S(1)}, u32[]{:S(2)}, u32[]{:S(2)}) collective-permute-start(f32[64,512]{1,0:T(8,128)S(1)} %add.13), channel_id=1, source_target_pairs={{0,6},{1,7},{2,4},{3,5},{4,2},{5,3},{6,0},{7,1},{8,14},{9,15},{10,... | collective-permute-start | bytes 393224 | tf_op jit(solution)/shard_map/ppermute | solution.py:361
  29.2 0.0 collective-permute-done.13
  29.2 0.6 %collective-permute-start.14 = (f32[64,512]{1,0:T(8,128)S(1)}, f32[64,512]{1,0:T(8,128)S(1)}, u32[]{:S(2)}, u32[]{:S(2)}) collective-permute-start(f32[64,512]{1,0:T(8,128)S(1)} %add.14), channel_id=1, source_target_pairs={{0,4},{1,5},{2,6},{3,7},{4,0},{5,1},{6,2},{7,3},{8,12},{9,13},{10,... | collective-permute-start | bytes 393224 | tf_op jit(solution)/shard_map/ppermute | solution.py:361
  29.8 0.0 collective-permute-done.15
  29.8 0.6 %collective-permute-start.16 = (f32[64,512]{1,0:T(8,128)S(1)}, f32[64,512]{1,0:T(8,128)S(1)}, u32[]{:S(2)}, u32[]{:S(2)}) collective-permute-start(f32[64,512]{1,0:T(8,128)S(1)} %add.15), channel_id=1, source_target_pairs={{0,2},{1,3},{2,0},{3,1},{4,6},{5,7},{6,4},{7,5},{8,10},{9,11},{10,... | collective-permute-start | bytes 393224 | tf_op jit(solution)/shard_map/ppermute | solution.py:361
  30.4 0.0 collective-permute-done.10
  30.4 2.9 %collective-permute-done.12.refs_1_ = f32[64,512]{1,0:T(8,128)S(1)} collective-permute-done((f32[64,512]{1,0:T(8,128)S(1)}, f32[64,512]{1,0:T(8,128)S(1)}, u32[]{:S(2)}, u32[]{:S(2)}) %collective-permute-start.12) | collective-permute-done | bytes 131104 | tf_op jit(solution)/shard_map/ppermute | solution.py:361
  33.3 2.7 %collective-permute-done.14.refs_2_ = f32[64,512]{1,0:T(8,128)S(1)} collective-permute-done((f32[64,512]{1,0:T(8,128)S(1)}, f32[64,512]{1,0:T(8,128)S(1)}, u32[]{:S(2)}, u32[]{:S(2)}) %collective-permute-start.14) | collective-permute-done | bytes 131104 | tf_op jit(solution)/shard_map/ppermute | solution.py:361
  36.0 0.1 collective-permute-done.16.refs_3_
  36.1 0.9 %sum_and_rows.1 = f32[64,512]{1,0:T(8,128)} custom-call(f32[64,512]{1,0:T(8,128)S(1)} %add.12.refs_0_, f32[64,512]{1,0:T(8,128)S(1)} %collective-permute-done.12.refs_1_, f32[64,512]{1,0:T(8,128)S(1)} %collective-permute-done.14.refs_2_, f32[64,512]{1,0:T(8,128)S(1)} %collective-permute-done.16.refs_3_, f32[64,512]{1,0:T(8,128)S(1)} %get-tuple-element.23.refs_5_.refs_4_, ...), custom_call_target="tpu_custom_call" | custom-call | tf_op jit(solution)/shard_map/sum_and_rows/pallas_call | solution.py:427
  (4 shorter events, 0.1 us)
Async XLA Ops:
  0.6 10.1 %collective-permute-start = (f32[64,512]{1,0:T(8,128)}, f32[64,512]{1,0:T(8,128)S(1)}, u32[]{:S(2)}, u32[]{:S(2)}) collective-permute-start(f32[64,512]{1,0:T(8,128)} %bitcast.7), channel_id=1, source_target_pairs={{0,6},{1,7},{2,4},{3,5},{4,2},{5,3},{6,0},{7,1},{8,14},{9,15},{10,... | collective-permute-start | bytes 393224 | tf_op jit(solution)/shard_map/ppermute | solution.py:361
  4.6 6.5 %collective-permute-start.4 = (f32[64,512]{1,0:T(8,128)}, f32[64,512]{1,0:T(8,128)S(1)}, u32[]{:S(2)}, u32[]{:S(2)}) collective-permute-start(f32[64,512]{1,0:T(8,128)} %bitcast.8), channel_id=1, source_target_pairs={{0,4},{1,5},{2,6},{3,7},{4,0},{5,1},{6,2},{7,3},{8,12},{9,13},{10,... | collective-permute-start | bytes 393224 | tf_op jit(solution)/shard_map/ppermute | solution.py:361
  5.1 6.3 %collective-permute-start.2 = (f32[64,512]{1,0:T(8,128)}, f32[64,512]{1,0:T(8,128)S(1)}, u32[]{:S(2)}, u32[]{:S(2)}) collective-permute-start(f32[64,512]{1,0:T(8,128)} %bitcast.9), channel_id=1, source_target_pairs={{0,2},{1,3},{2,0},{3,1},{4,6},{5,7},{6,4},{7,5},{8,10},{9,11},{10,... | collective-permute-start | bytes 393224 | tf_op jit(solution)/shard_map/ppermute | solution.py:361
  6.3 5.7 %collective-permute-start.8 = (s32[2,72,128]{2,1,0:T(8,128)S(1)}, s32[2,72,128]{2,1,0:T(8,128)S(1)}, u32[]{:S(2)}, u32[]{:S(2)}) collective-permute-start(s32[2,72,128]{2,1,0:T(8,128)S(1)} %get-tuple-element.27), channel_id=1, source_target_pairs={{0,16},{8,24},{16,0},{24,8},{1,17},{9,25},{17,1},{25,9},{2,18},{10... | collective-permute-start | bytes 221192 | tf_op jit(solution)/shard_map/ppermute | solution.py:361
  9.4 6.3 %collective-permute-start.9 = (s32[2,72,128]{2,1,0:T(8,128)S(1)}, s32[2,72,128]{2,1,0:T(8,128)S(1)}, u32[]{:S(2)}, u32[]{:S(2)}) collective-permute-start(s32[2,72,128]{2,1,0:T(8,128)S(1)} %get-tuple-element.28), channel_id=1, source_target_pairs={{0,24},{8,16},{16,8},{24,0},{1,25},{9,17},{17,9},{25,1},{2,26},{10... | collective-permute-start | bytes 221192 | tf_op jit(solution)/shard_map/ppermute | solution.py:361
  10.7 9.3 %collective-permute-start.6 = (f32[64,512]{1,0:T(8,128)S(1)}, f32[64,512]{1,0:T(8,128)S(1)}, u32[]{:S(2)}, u32[]{:S(2)}) collective-permute-start(f32[64,512]{1,0:T(8,128)S(1)} %collective-permute-done.refs_11_), channel_id=1, source_target_pairs={{0,1},{1,0},{2,3},{3,2},{4,5},{5,4},{6,7},{7,6},{8,9},{9,8},{10,11... | collective-permute-start | bytes 393224 | tf_op jit(solution)/shard_map/ppermute | solution.py:361
  11.1 8.9 %collective-permute-start.5 = (f32[64,512]{1,0:T(8,128)S(1)}, f32[64,512]{1,0:T(8,128)S(1)}, u32[]{:S(2)}, u32[]{:S(2)}) collective-permute-start(f32[64,512]{1,0:T(8,128)S(1)} %collective-permute-done.4.refs_9_), channel_id=1, source_target_pairs={{0,1},{1,0},{2,3},{3,2},{4,5},{5,4},{6,7},{7,6},{8,9},{9,8},{10,11... | collective-permute-start | bytes 393224 | tf_op jit(solution)/shard_map/ppermute | solution.py:361
  11.4 8.6 %collective-permute-start.3 = (f32[64,512]{1,0:T(8,128)S(1)}, f32[64,512]{1,0:T(8,128)S(1)}, u32[]{:S(2)}, u32[]{:S(2)}) collective-permute-start(f32[64,512]{1,0:T(8,128)S(1)} %collective-permute-done.2.refs_7_), channel_id=1, source_target_pairs={{0,1},{1,0},{2,3},{3,2},{4,5},{5,4},{6,7},{7,6},{8,9},{9,8},{10,11... | collective-permute-start | bytes 393224 | tf_op jit(solution)/shard_map/ppermute | solution.py:361
  12.1 7.9 %collective-permute-start.1 = (f32[64,512]{1,0:T(8,128)S(1)}, f32[64,512]{1,0:T(8,128)S(1)}, u32[]{:S(2)}, u32[]{:S(2)}) collective-permute-start(f32[64,512]{1,0:T(8,128)S(1)} %get-tuple-element.23.refs_5_.refs_4_), channel_id=1, source_target_pairs={{0,1},{1,0},{2,3},{3,2},{4,5},{5,4},{6,7},{7,6},{8,9},{9,8},{10,11... | collective-permute-start | bytes 393224 | tf_op jit(solution)/shard_map/ppermute | solution.py:361
  15.6 4.4 %collective-permute-start.7 = (s32[2,72,128]{2,1,0:T(8,128)S(1)}, s32[2,72,128]{2,1,0:T(8,128)S(1)}, u32[]{:S(2)}, u32[]{:S(2)}) collective-permute-start(s32[2,72,128]{2,1,0:T(8,128)S(1)} %get-tuple-element.26), channel_id=1, source_target_pairs={{0,8},{8,0},{16,24},{24,16},{1,9},{9,1},{17,25},{25,17},{2,10},{10... | collective-permute-start | bytes 221192 | tf_op jit(solution)/shard_map/ppermute | solution.py:361
  25.2 1.4 %collective-permute-start.11 = (f32[64,512]{1,0:T(8,128)S(1)}, f32[64,512]{1,0:T(8,128)S(1)}, u32[]{:S(2)}, u32[]{:S(2)}) collective-permute-start(f32[64,512]{1,0:T(8,128)S(1)} %get-tuple-element.36), channel_id=1, source_target_pairs={{0,1},{1,0},{2,3},{3,2},{4,5},{5,4},{6,7},{7,6},{8,9},{9,8},{10,11... | collective-permute-start | bytes 393224 | tf_op jit(solution)/shard_map/ppermute | solution.py:361
  25.3 3.9 %collective-permute-start.13 = (f32[64,512]{1,0:T(8,128)S(1)}, f32[64,512]{1,0:T(8,128)S(1)}, u32[]{:S(2)}, u32[]{:S(2)}) collective-permute-start(f32[64,512]{1,0:T(8,128)S(1)} %get-tuple-element.38), channel_id=1, source_target_pairs={{0,1},{1,0},{2,3},{3,2},{4,5},{5,4},{6,7},{7,6},{8,9},{9,8},{10,11... | collective-permute-start | bytes 393224 | tf_op jit(solution)/shard_map/ppermute | solution.py:361
  25.8 4.0 %collective-permute-start.15 = (f32[64,512]{1,0:T(8,128)S(1)}, f32[64,512]{1,0:T(8,128)S(1)}, u32[]{:S(2)}, u32[]{:S(2)}) collective-permute-start(f32[64,512]{1,0:T(8,128)S(1)} %get-tuple-element.40), channel_id=1, source_target_pairs={{0,1},{1,0},{2,3},{3,2},{4,5},{5,4},{6,7},{7,6},{8,9},{9,8},{10,11... | collective-permute-start | bytes 393224 | tf_op jit(solution)/shard_map/ppermute | solution.py:361
  25.9 4.5 %collective-permute-start.10 = (f32[64,512]{1,0:T(8,128)S(1)}, f32[64,512]{1,0:T(8,128)S(1)}, u32[]{:S(2)}, u32[]{:S(2)}) collective-permute-start(f32[64,512]{1,0:T(8,128)S(1)} %get-tuple-element.34), channel_id=1, source_target_pairs={{0,1},{1,0},{2,3},{3,2},{4,5},{5,4},{6,7},{7,6},{8,9},{9,8},{10,11... | collective-permute-start | bytes 393224 | tf_op jit(solution)/shard_map/ppermute | solution.py:361
  26.7 6.6 %collective-permute-start.12 = (f32[64,512]{1,0:T(8,128)S(1)}, f32[64,512]{1,0:T(8,128)S(1)}, u32[]{:S(2)}, u32[]{:S(2)}) collective-permute-start(f32[64,512]{1,0:T(8,128)S(1)} %add.13), channel_id=1, source_target_pairs={{0,6},{1,7},{2,4},{3,5},{4,2},{5,3},{6,0},{7,1},{8,14},{9,15},{10,... | collective-permute-start | bytes 393224 | tf_op jit(solution)/shard_map/ppermute | solution.py:361
  29.2 6.8 %collective-permute-start.14 = (f32[64,512]{1,0:T(8,128)S(1)}, f32[64,512]{1,0:T(8,128)S(1)}, u32[]{:S(2)}, u32[]{:S(2)}) collective-permute-start(f32[64,512]{1,0:T(8,128)S(1)} %add.14), channel_id=1, source_target_pairs={{0,4},{1,5},{2,6},{3,7},{4,0},{5,1},{6,2},{7,3},{8,12},{9,13},{10,... | collective-permute-start | bytes 393224 | tf_op jit(solution)/shard_map/ppermute | solution.py:361
  29.8 6.3 %collective-permute-start.16 = (f32[64,512]{1,0:T(8,128)S(1)}, f32[64,512]{1,0:T(8,128)S(1)}, u32[]{:S(2)}, u32[]{:S(2)}) collective-permute-start(f32[64,512]{1,0:T(8,128)S(1)} %add.15), channel_id=1, source_target_pairs={{0,2},{1,3},{2,0},{3,1},{4,6},{5,7},{6,4},{7,5},{8,10},{9,11},{10,... | collective-permute-start | bytes 393224 | tf_op jit(solution)/shard_map/ppermute | solution.py:361

commit v2 on v1

--- a/solution.py
+++ b/solution.py
@@ -65,30 +65,33 @@
     sections.append(np.concatenate([lift, np.zeros((side, side - lift.shape[1]), lift.dtype)], axis=1))
     waves = np.zeros((8, half))
     waves[:] = wave[None, :]
-    return np.concatenate(sections), np.concatenate([gain, inverse, waves]).astype(np.float32)
+    return (
+        np.concatenate(sections[2:4]),
+        np.concatenate(sections[:2] + sections[4:]),
+        np.concatenate([gain, inverse, waves]).astype(np.float32),
+    )
 
 
 class Tables:
-    def __init__(self, packed, reals, side, ring):
+    def __init__(self, backs, packed, reals, side, ring):
         half = side // 2
         self.half = half
         self.ring = ring
+        self.backs = backs
         self.packed = packed
         self.reals = reals
-        self.lift_at = 4 * half + 4 * ring
-
-    def _pair(self, at):
-        half = self.half
+        self.lift_at = 2 * half + 4 * ring
+
+    def fwd(self, par):
+        half, at = self.half, par * self.half
         return self.packed[at : at + half, :half], self.packed[at : at + half, half:]
 
-    def fwd(self, par):
-        return self._pair(par * self.half)
-
     def back(self, par):
-        return self._pair((2 + par) * self.half)
+        half, at = self.half, par * self.half
+        return self.backs[at : at + half, :half], self.backs[at : at + half, half:]
 
     def views(self):
-        at, count = 4 * self.half, 2 * self.ring
+        at, count = 2 * self.half, 2 * self.ring
         return self.packed[at : at + count, :], self.packed[at + count : at + 2 * count, :]
 
     def lift(self, start, count):
@@ -143,44 +146,54 @@
     return lax.rem(lax.bitwise_xor(me, k) - me + n, n)
 
 
-def main_kernel(n, groups, rows, side, tiles, *refs):
-    half, q = side // 2, side // 4
-    ring = rows + PAD
-    refs = list(refs)
-    small = refs[:5]
-    blocks = refs[5 : 5 + n]
-    msgs = refs[5 + n : 5 + n + groups]
-    rest = refs[5 + n + groups :]
-    tabs = Tables(rest[0], rest[1], side, ring)
-    density_out = rest[2]
-    outs = rest[3 : 3 + n]
-    fh, fl, yh, yl, zh, zl, cnt, cls, part = rest[3 + n : 12 + n]
-    held = rest[12 + n : 17 + n]
-    sems = rest[17 + n]
-    owner, stencil, mean_counts, bias_one, bias_two = held
-    copies = [pltpu.make_async_copy(a, b, sems.at[i]) for i, (a, b) in enumerate(zip(small, held))]
-    for copy in copies:
-        copy.start()
+def along_y_kernel(n, rows, side, *refs):
+    half = side // 2
+    blocks = refs[: n // 2]
+    backs, out, fh, fl = refs[n // 2 :]
+    tabs = Tables(backs, None, None, side, 0)
     me = lax.axis_index("gy")
-    mine = lax.axis_index("gx")
-
-    for k in range(n // 2):
-        a, b = blocks[k][...], blocks[k ^ (n // 2)][...]
-        place = place_of(me, k, n)
+    for i in range(n // 4):
+        a, b = blocks[i][...], blocks[i + n // 4][...]
+        place = place_of(me, 2 * i, n)
         sign = jnp.where(place < n // 2, 1.0, -1.0).astype(F32)
-        off = pl.multiple_of(lax.rem(place, n // 2) * rows, rows)
+        off = pl.multiple_of(lax.rem(place, n // 2) // 2 * rows, rows)
         for par, v in ((0, a + b), (1, (a - b) * sign)):
             lo, hi = v[:, :half], v[:, half:]
             for ypar, w in ((0, lo + hi), (1, lo - hi)):
                 h, l = split(w)
                 fh[par, pl.ds(off, rows), ypar * half : (ypar + 1) * half] = h
                 fl[par, pl.ds(off, rows), ypar * half : (ypar + 1) * half] = l
-
     for par in range(2):
         for ypar in range(2):
             cols = slice(ypar * half, (ypar + 1) * half)
-            y = mm3((fh[par, :, cols], fl[par, :, cols]), tabs.back(ypar))
-            yh[par, :, cols], yl[par, :, cols] = split(y)
+            out[par, :, cols] = mm3((fh[par, :, cols], fl[par, :, cols]), tabs.back(ypar))
+
+
+def field_kernel(n, rows, side, *refs):
+    half, q = side // 2, side // 4
+    ring = rows + PAD
+    stencil_in, own, other, packed, reals = refs[:5]
+    density_out, smooth_out, fields_out = refs[5:8]
+    yh, yl, zh, zl, stencil, sem = refs[8:]
+    tabs = Tables(None, packed, reals, side, ring)
+    load = pltpu.make_async_copy(stencil_in, stencil, sem)
+    load.start()
+
+    odd = lax.rem(lax.axis_index("gy"), 2)
+    for i in range(n // 4):
+        place = jnp.where(odd == 1, (2 * i - 1) % (n // 2), 2 * i + 1)
+        off = pl.multiple_of(place * rows, rows)
+        sign = jnp.where(odd == 1, -1.0, 1.0).astype(F32) if i == 0 else 1.0
+        rs = slice(i * rows, (i + 1) * rows)
+        for par in range(2):
+            yh[par, 2 * i * rows : (2 * i + 1) * rows, :], yl[par, 2 * i * rows : (2 * i + 1) * rows, :] = split(
+                own[par, rs, :]
+            )
+            v = other[par, rs, :]
+            h, l = split(v * sign if par else v)
+            yh[par, pl.ds(off, rows), :] = h
+            yl[par, pl.ds(off, rows), :] = l
+
     for par in range(2):
         for ypar in range(2):
             cols = slice(ypar * half, (ypar + 1) * half)
@@ -205,10 +218,36 @@
     e = mm3((sh[:, :half], sl[:, :half]), tabs.fwd(0))
     o = mm3((sh[:, half:], sl[:, half:]), tabs.fwd(1))
     fields = jnp.concatenate([e + o, e - o], axis=1)
+    fields_out[...] = fields
     linear, shift_x, shift_y, slope_x, slope_y = [fields[i * ring : (i + 1) * ring] for i in range(5)]
     density = linear + GROWTH * linear * linear - (shift_x * slope_x + shift_y * slope_y)
     density_out[...] = density[:rows]
 
+    load.wait()
+    beside = {0: density, 1: turn_lanes(density, -1), -1: turn_lanes(density, 1)}
+    smooth = jnp.zeros_like(density)
+    for a in (-1, 0, 1):
+        band = sum(stencil[(a + 1) * 3 + b + 1] * beside[b] for b in (-1, 0, 1))
+        smooth = smooth + (turn_rows(band, -a) if a else band)
+    smooth_out[...] = smooth[:rows]
+
+
+def adjoint_kernel(n, groups, rows, side, tiles, *refs):
+    half, q = side // 2, side // 4
+    ring = rows + PAD
+    small = refs[:5]
+    msgs = refs[5 : 5 + groups]
+    smooth_in, fields, backs, packed, reals = refs[5 + groups : 10 + groups]
+    outs = refs[10 + groups : 10 + groups + n]
+    yh, yl, cnt, cls, part, *held, sems = refs[10 + groups + n :]
+    owner, stencil, mean_counts, bias_one, bias_two = held
+    tabs = Tables(backs, packed, reals, side, ring)
+    ky = tabs.waves()
+    me = lax.axis_index("gy")
+    mine = lax.axis_index("gx")
+    copies = [pltpu.make_async_copy(a, b, sems.at[i]) for i, (a, b) in enumerate(zip(small, held))]
+    for copy in copies:
+        copy.start()
     for copy in copies:
         copy.wait()
 
@@ -224,12 +263,8 @@
                 cnt[:, t * TC : (t + 1) * TC] = msgs[k][rank, :rows, :].astype(F32)
                 cls[:, t * TC : (t + 1) * TC] = msgs[k][rank, rows : rows + 8, :]
 
-    beside = {0: density, 1: turn_lanes(density, -1), -1: turn_lanes(density, 1)}
-    smooth = jnp.zeros_like(density)
-    for a in (-1, 0, 1):
-        band = sum(stencil[(a + 1) * 3 + b + 1] * beside[b] for b in (-1, 0, 1))
-        smooth = smooth + (turn_rows(band, -a) if a else band)
-    smooth = smooth[:rows]
+    smooth = smooth_in[...]
+    linear, shift_x, shift_y, slope_x, slope_y = [fields[i * ring : (i + 1) * ring, :] for i in range(5)]
     classes = cls[...]
     mean_v, one_v, two_v = [jnp.full(classes.shape, ref[0], F32) for ref in (mean_counts, bias_one, bias_two)]
     for d in range(1, mean_counts.shape[0]):
@@ -317,11 +352,10 @@
         copy.wait()
 
 
-def table_kernel(packed, reals, packed_out, reals_out, sems):
-    copies = [
-        pltpu.make_async_copy(packed, packed_out, sems.at[0]),
-        pltpu.make_async_copy(reals, reals_out, sems.at[1]),
-    ]
+def table_kernel(*refs):
+    sems = refs[-1]
+    count = len(refs) // 2
+    copies = [pltpu.make_async_copy(refs[i], refs[count + i], sems.at[i]) for i in range(count)]
     for copy in copies:
         copy.start()
     for copy in copies:
@@ -339,7 +373,7 @@
     for p in parts[1:]:
         total = total + p[...]
     half = total.shape[1] // 2
-    tabs = Tables(packed, None, 2 * half, 0)
+    tabs = Tables(None, packed, None, 2 * half, 0)
     sh, sl = split(total)
     e = mm3((sh[:, :half], sl[:, :half]), tabs.fwd(0))
     o = mm3((sh[:, half:], sl[:, half:]), tabs.fwd(1))
@@ -353,7 +387,7 @@
     tiles = side // TC
     slots = counts.shape[1]
     capacity = slots // groups
-    packed, reals = [jnp.asarray(t) for t in make_tables(side, rows)]
+    backs, packed, reals = [jnp.asarray(t) for t in make_tables(side, rows)]
     vmem = pl.BlockSpec(memory_space=VMEM)
     hbm = pl.BlockSpec(memory_space=pltpu.HBM)
 
@@ -363,9 +397,10 @@
     blocks = {}
     for k in range(n - 2, 0, -2):
         blocks[k] = swap(own, k)
-    *msgs, held_own = pl.pallas_call(
+    *msgs, blocks[0] = pl.pallas_call(
         functools.partial(message_kernel, groups, capacity, rows),
-        out_shape=[VMEM((capacity, rows + 8, TC), jnp.int32)] * groups + [VMEM((rows, side), F32)],
+        out_shape=[VMEM((capacity, rows + 8, TC), jnp.int32)] * groups
+        + [VMEM((rows, side), F32)],
         in_specs=[hbm] * 3,
         out_specs=[vmem] * (groups + 1),
         scratch_shapes=[pltpu.SMEM((slots,), jnp.int32), pltpu.SemaphoreType.DMA((groups + 2,))],
@@ -373,38 +408,57 @@
         name="messages",
     )(in_hbm(counts.reshape(slots, rows, TC)), in_hbm(depth.reshape(slots)), in_hbm(own))
     for k in range(groups - 1, 0, -1):
-        if k == 1:
-            msgs[k], _ = lax.optimization_barrier((msgs[k], blocks[n - 2]))
         msgs[k] = swap(msgs[k], k, "gx", groups)
-    blocks[0], _ = lax.optimization_barrier((held_own, blocks[n - 2]))
-    blocks[1] = swap(blocks[0], 1)
-    for k in range(n - 2, 0, -2):
-        blocks[k + 1] = swap(blocks[k], 1)
-    packed, reals, _ = lax.optimization_barrier((packed, reals, blocks[n - 2]))
-    packed, reals = pl.pallas_call(
+
+    noise_held, backs, packed, reals = lax.optimization_barrier((blocks[0], backs, packed, reals))
+    blocks[0] = noise_held
+    backs, packed, reals = pl.pallas_call(
         table_kernel,
-        out_shape=[VMEM(t.shape, t.dtype) for t in (packed, reals)],
-        in_specs=[hbm] * 2,
-        out_specs=[vmem] * 2,
-        scratch_shapes=[pltpu.SemaphoreType.DMA((2,))],
+        out_shape=[VMEM(t.shape, t.dtype) for t in (backs, packed, reals)],
+        in_specs=[hbm] * 3,
+        out_specs=[vmem] * 3,
+        scratch_shapes=[pltpu.SemaphoreType.DMA((3,))],
         compiler_params=pltpu.CompilerParams(vmem_limit_bytes=4 * MIB),
         name="tables",
-    )(in_hbm(packed), in_hbm(reals))
+    )(in_hbm(backs), in_hbm(packed), in_hbm(reals))
     half = side // 2
+    ring = rows + PAD
     cell = jax.ShapeDtypeStruct((rows, side), F32)
+    along_y = pl.pallas_call(
+        functools.partial(along_y_kernel, n, rows, side),
+        out_shape=jax.ShapeDtypeStruct((2, half // 2, side), F32),
+        in_specs=[vmem] * (n // 2 + 1),
+        out_specs=vmem,
+        scratch_shapes=[VMEM((2, half // 2, side), BF16)] * 2,
+        compiler_params=pltpu.CompilerParams(vmem_limit_bytes=8 * MIB),
+        cost_estimate=pl.CostEstimate(flops=1, bytes_accessed=1, transcendentals=0),
+        name="along_y",
+    )(*[blocks[k] for k in range(0, n, 2)], backs)
+    held, msgs[2], msgs[1] = lax.optimization_barrier((along_y, msgs[2], msgs[1]))
+    other = swap(held, 1)
+    density, smooth, fields = pl.pallas_call(
+        functools.partial(field_kernel, n, rows, side),
+        out_shape=[cell, VMEM((rows, side), F32), VMEM((5 * ring, side), F32)],
+        in_specs=[hbm] + [vmem] * 4,
+        out_specs=[vmem] * 3,
+        scratch_shapes=[
+            *[VMEM((2, half, side), BF16)] * 2,
+            *[VMEM((side, 2 * side), BF16)] * 2,
+            pltpu.SMEM(stencil.shape, F32),
+            pltpu.SemaphoreType.DMA,
+        ],
+        compiler_params=pltpu.CompilerParams(vmem_limit_bytes=16 * MIB),
+        cost_estimate=pl.CostEstimate(flops=1, bytes_accessed=1, transcendentals=0),
+        name="fields",
+    )(in_hbm(stencil), along_y, other, packed, reals)
     small = (owner.reshape(tiles), stencil, mean_counts, bias_one, bias_two)
-    density, *parts = pl.pallas_call(
-        functools.partial(main_kernel, n, groups, rows, side, tiles),
-        out_shape=[cell] * (1 + n),
-        in_specs=[hbm] * 5 + [vmem] * (n + groups + 2),
-        out_specs=[vmem] * (1 + n),
+    parts = pl.pallas_call(
+        functools.partial(adjoint_kernel, n, groups, rows, side, tiles),
+        out_shape=[cell] * n,
+        in_specs=[hbm] * 5 + [vmem] * (groups + 5),
+        out_specs=[vmem] * n,
         scratch_shapes=[
-            VMEM((2, half, side), BF16),
-            VMEM((2, half, side), BF16),
-            VMEM((2, half, side), BF16),
-            VMEM((2, half, side), BF16),
-            VMEM((side, 2 * side), BF16),
-            VMEM((side, 2 * side), BF16),
+            *[VMEM((2, half, side), BF16)] * 2,
             VMEM((rows, side), F32),
             VMEM((8, side), jnp.int32),
             VMEM((2, half, side), F32),
@@ -412,14 +466,8 @@
             pltpu.SemaphoreType.DMA((5,)),
         ],
         compiler_params=pltpu.CompilerParams(vmem_limit_bytes=16 * MIB),
-        name="fields_and_adjoint",
-    )(
-        *[in_hbm(a) for a in small],
-        *[blocks[k] for k in range(n)],
-        *msgs,
-        packed,
-        reals,
-    )
+        name="adjoint",
+    )(*[in_hbm(a) for a in small], *msgs, smooth, fields, backs, packed, reals)
     sums = {}
     for k in range(n - 2, -1, -2):
         sums[k] = parts[k] + swap(parts[k + 1], 1)

time: 37.1 us -> 35.1 us (0.946)
  waiting for transfers between devices: 12.4 us -> 7.9 us
  starting transfers between devices: 14.9 us -> 16.6 us
  Pallas kernels: 8.82 us -> 9.58 us
    ppermute x17 -> x14, waiting for transfers between devices: 12.4 us -> 7.9 us  [swap(): return lax.ppermute(value, axis, [(i, i ^ k) for i in range(size)])]
    ppermute x17 -> x14, starting transfers between devices: 14.9 us -> 16.6 us  [swap(): return lax.ppermute(value, axis, [(i, i ^ k) for i in range(size)])]
    pallas_call x1 -> x3, Pallas kernels: 5.19 us -> 5.94 us  [the longest x1 2.83 us: local(): pl.pallas_call(functools.partial(adjoint_kernel, n, groups, rows, side, t...]
  transfers between devices with their start and end apart: 17 -> 14, of which waited for: 9 -> 6; matrix products, arithmetic and copies ran while one was open for 0% -> 0% of each run, Pallas kernels for 7% -> 17%
where the time goes in v2:
time: 35.1 us; the launch traced here: 34.9 us
  starting transfers between devices  16.6 us (47%)
  Pallas kernels  9.58 us (27%)
  waiting for transfers between devices  7.9 us (23%)
  between operations  0.73 us (2%)
    ppermute x14, starting transfers between devices, swap(): return lax.ppermute(value, axis, [(i, i ^ k) for i in range(size)])  16.6 us
    ppermute x14, waiting for transfers between devices, swap(): return lax.ppermute(value, axis, [(i, i ^ k) for i in range(size)])  7.9 us
    pallas_call x1, Pallas kernels, local(): pl.pallas_call(functools.partial(adjoint_kernel, n, groups, rows, side, t...  2.83 us
    pallas_call x1, Pallas kernels, local(): pl.pallas_call(functools.partial(field_kernel, n, rows, side), out_shape=...  2.61 us
    pallas_call x1, Pallas kernels, local(): pl.pallas_call(table_kernel, out_shape=[VMEM(t.shape, t.dtype) for t in (...  1.64 us
    pallas_call x1, Pallas kernels, local(): pl.pallas_call(functools.partial(message_kernel, groups, capacity, rows),...  1.09 us
    pallas_call x1, Pallas kernels, local(): pl.pallas_call(functools.partial(last_kernel, len(pieces)), out_shape=cel...  0.91 us
  transfers between devices with their start and end apart: 14, of which 6 were waited for; matrix products, arithmetic and copies ran while one was open for 0% of the time, Pallas kernels for 17%

profile of v2, /device:TPU:0, one launch (start us, length us, event | category | flops | bytes accessed | tf_op | source)
XLA Modules:
  0.0 34.9 jit_solution(17299364975266346915)
XLA Ops:
  0.6 4.0 %collective-permute-start.2 = (f32[64,512]{1,0:T(8,128)}, f32[64,512]{1,0:T(8,128)S(1)}, u32[]{:S(2)}, u32[]{:S(2)}) collective-permute-start(f32[64,512]{1,0:T(8,128)} %bitcast.8), channel_id=1, source_target_pairs={{0,6},{1,7},{2,4},{3,5},{4,2},{5,3},{6,0},{7,1},{8,14},{9,15},{10,... | collective-permute-start | bytes 393224 | tf_op jit(solution)/shard_map/ppermute | solution.py:395
  4.6 0.5 %collective-permute-start.1 = (f32[64,512]{1,0:T(8,128)}, f32[64,512]{1,0:T(8,128)S(1)}, u32[]{:S(2)}, u32[]{:S(2)}) collective-permute-start(f32[64,512]{1,0:T(8,128)} %bitcast.9), channel_id=1, source_target_pairs={{0,4},{1,5},{2,6},{3,7},{4,0},{5,1},{6,2},{7,3},{8,12},{9,13},{10,... | collective-permute-start | bytes 393224 | tf_op jit(solution)/shard_map/ppermute | solution.py:395
  5.1 0.1 collective-permute-start
  5.2 1.1 %messages.1 = (s32[2,72,128]{2,1,0:T(8,128)S(1)}, s32[2,72,128]{2,1,0:T(8,128)S(1)}, s32[2,72,128]{2,1,0:T(8,128)S(1)}, s32[2,72,128]{2,1,0:T(8,128)S(1)}, f32[64,512]{1,0:T(8,128)S(1)}) custom-call(s32[8,64,128]{2,1,0:T(8,128)} %bitcast.6, s32[8]{0:T(128)} %bitcast.12, f32[64,512]{1,0:T(8,128)} %bitcast.11), custom_call_target="tpu_custom_call" | custom-call | tf_op jit(solution)/shard_map/messages/pallas_call | solution.py:400
  6.3 3.1 %collective-permute-start.3 = (s32[2,72,128]{2,1,0:T(8,128)S(1)}, s32[2,72,128]{2,1,0:T(8,128)S(1)}, u32[]{:S(2)}, u32[]{:S(2)}) collective-permute-start(s32[2,72,128]{2,1,0:T(8,128)S(1)} %get-tuple-element.35), channel_id=1, source_target_pairs={{0,16},{8,24},{16,0},{24,8},{1,17},{9,25},{17,1},{25,9},{2,18},{10... | collective-permute-start | bytes 221192 | tf_op jit(solution)/shard_map/ppermute | solution.py:395
  9.4 1.6 %collective-permute-start.4 = (s32[2,72,128]{2,1,0:T(8,128)S(1)}, s32[2,72,128]{2,1,0:T(8,128)S(1)}, u32[]{:S(2)}, u32[]{:S(2)}) collective-permute-start(s32[2,72,128]{2,1,0:T(8,128)S(1)} %get-tuple-element.36), channel_id=1, source_target_pairs={{0,8},{8,0},{16,24},{24,16},{1,9},{9,1},{17,25},{25,17},{2,10},{10... | collective-permute-start | bytes 221192 | tf_op jit(solution)/shard_map/ppermute | solution.py:395
  11.0 1.6 %tables.1 = (bf16[512,512]{1,0:T(8,128)(2,1)S(1)}, bf16[1344,512]{1,0:T(8,128)(2,1)S(1)}, f32[520,256]{1,0:T(8,128)S(1)}) custom-call(bf16[512,512]{1,0:T(8,128)(2,1)} %constant.6.clone.refs_0_, bf16[1344,512]{1,0:T(8,128)(2,1)} %constant.7.clone.refs_1_, f32[520,256]{1,0:T(8,128)} %constant.8.clone.refs_2_), custom_call_target="tpu_custom_call" | custom-call | tf_op jit(solution)/shard_map/tables/pallas_call | solution.py:415
  12.6 0.0 collective-permute-done.2.refs_3_
  12.6 0.0 collective-permute-done.1.refs_2_
  12.6 0.0 collective-permute-done.refs_1_
  12.6 0.5 %along_y.1.refs_1_ = f32[2,128,512]{2,1,0:T(8,128)S(1)} custom-call(f32[64,512]{1,0:T(8,128)S(1)} %get-tuple-element.30.refs_0_.refs_4_, f32[64,512]{1,0:T(8,128)S(1)} %collective-permute-done.refs_1_, f32[64,512]{1,0:T(8,128)S(1)} %collective-permute-done.1.refs_2_, f32[64,512]{1,0:T(8,128)S(1)} %collective-permute-done.2.refs_3_, ...), custom_call_target="tpu_custom_call" | custom-call | flops 1 | bytes 1 | tf_op jit(solution)/shard_map/along_y/pallas_call | solution.py:427
  13.1 0.0 collective-permute-done.3.refs_7_
  13.2 0.6 %collective-permute-done.4.refs_6_ = s32[2,72,128]{2,1,0:T(8,128)S(1)} collective-permute-done((s32[2,72,128]{2,1,0:T(8,128)S(1)}, s32[2,72,128]{2,1,0:T(8,128)S(1)}, u32[]{:S(2)}, u32[]{:S(2)}) %collective-permute-start.4) | collective-permute-done | bytes 73760 | tf_op jit(solution)/shard_map/ppermute | solution.py:395
  13.7 0.0 collective-permute-start.6
  13.7 2.6 %collective-permute-start.5 = (s32[2,72,128]{2,1,0:T(8,128)S(1)}, s32[2,72,128]{2,1,0:T(8,128)S(1)}, u32[]{:S(2)}, u32[]{:S(2)}) collective-permute-start(s32[2,72,128]{2,1,0:T(8,128)S(1)} %get-tuple-element.39), channel_id=1, source_target_pairs={{0,24},{8,16},{16,8},{24,0},{1,25},{9,17},{17,9},{25,1},{2,26},{10... | collective-permute-start | bytes 221192 | tf_op jit(solution)/shard_map/ppermute | solution.py:395
  16.4 0.0 collective-permute-done.6.refs_2_
  16.4 2.6 %fields.1 = (f32[64,512]{1,0:T(8,128)}, f32[64,512]{1,0:T(8,128)S(1)}, f32[400,512]{1,0:T(8,128)S(1)}) custom-call(f32[9]{0:T(128)} %refs_1_.1, f32[2,128,512]{2,1,0:T(8,128)S(1)} %along_y.1.refs_1_, f32[2,128,512]{2,1,0:T(8,128)S(1)} %collective-permute-done.6.refs_2_, bf16[1344,512]{1,0:T(8,128)(2,1)S(1)} %get-tuple-element.41.refs_3_.refs_12_.refs_5_, ...), custom_call_target="tpu_custom_call" | custom-call | flops 1 | bytes 1 | tf_op jit(solution)/shard_map/fields/pallas_call | solution.py:439
  19.0 1.3 %collective-permute-done.5.refs_8_ = s32[2,72,128]{2,1,0:T(8,128)S(1)} collective-permute-done((s32[2,72,128]{2,1,0:T(8,128)S(1)}, s32[2,72,128]{2,1,0:T(8,128)S(1)}, u32[]{:S(2)}, u32[]{:S(2)}) %collective-permute-start.5) | collective-permute-done | bytes 73760 | tf_op jit(solution)/shard_map/ppermute | solution.py:395
  20.3 2.8 %adjoint.1 = (f32[64,512]{1,0:T(8,128)S(1)}, f32[64,512]{1,0:T(8,128)S(1)}, f32[64,512]{1,0:T(8,128)S(1)}, f32[64,512]{1,0:T(8,128)S(1)}, f32[64,512]{1,0:T(8,12...) custom-call(s32[4]{0:T(128)} %bitcast.13, f32[9]{0:T(128)} %refs_1_.1, f32[4]{0:T(128)} %refs_2_.1, ...), custom_call_target="tpu_custom_call" | custom-call | tf_op jit(solution)/shard_map/adjoint/pallas_call | solution.py:455
  23.2 0.1 collective-permute-start.8
  23.2 0.5 %collective-permute-start.10 = (f32[64,512]{1,0:T(8,128)S(1)}, f32[64,512]{1,0:T(8,128)S(1)}, u32[]{:S(2)}, u32[]{:S(2)}) collective-permute-start(f32[64,512]{1,0:T(8,128)S(1)} %get-tuple-element.50), channel_id=1, source_target_pairs={{0,1},{1,0},{2,3},{3,2},{4,5},{5,4},{6,7},{7,6},{8,9},{9,8},{10,11... | collective-permute-start | bytes 393224 | tf_op jit(solution)/shard_map/ppermute | solution.py:395
  23.7 0.1 collective-permute-start.12
  23.8 0.4 %collective-permute-start.7 = (f32[64,512]{1,0:T(8,128)S(1)}, f32[64,512]{1,0:T(8,128)S(1)}, u32[]{:S(2)}, u32[]{:S(2)}) collective-permute-start(f32[64,512]{1,0:T(8,128)S(1)} %get-tuple-element.46), channel_id=1, source_target_pairs={{0,1},{1,0},{2,3},{3,2},{4,5},{5,4},{6,7},{7,6},{8,9},{9,8},{10,11... | collective-permute-start | bytes 393224 | tf_op jit(solution)/shard_map/ppermute | solution.py:395
  24.3 0.3 collective-permute-done.8
  24.6 2.5 %collective-permute-start.9 = (f32[64,512]{1,0:T(8,128)S(1)}, f32[64,512]{1,0:T(8,128)S(1)}, u32[]{:S(2)}, u32[]{:S(2)}) collective-permute-start(f32[64,512]{1,0:T(8,128)S(1)} %add.13), channel_id=1, source_target_pairs={{0,6},{1,7},{2,4},{3,5},{4,2},{5,3},{6,0},{7,1},{8,14},{9,15},{10,... | collective-permute-start | bytes 393224 | tf_op jit(solution)/shard_map/ppermute | solution.py:395
  27.1 0.0 collective-permute-done.10
  27.1 0.6 %collective-permute-start.11 = (f32[64,512]{1,0:T(8,128)S(1)}, f32[64,512]{1,0:T(8,128)S(1)}, u32[]{:S(2)}, u32[]{:S(2)}) collective-permute-start(f32[64,512]{1,0:T(8,128)S(1)} %add.14), channel_id=1, source_target_pairs={{0,4},{1,5},{2,6},{3,7},{4,0},{5,1},{6,2},{7,3},{8,12},{9,13},{10,... | collective-permute-start | bytes 393224 | tf_op jit(solution)/shard_map/ppermute | solution.py:395
  27.7 0.0 collective-permute-done.12
  27.7 0.6 %collective-permute-start.13 = (f32[64,512]{1,0:T(8,128)S(1)}, f32[64,512]{1,0:T(8,128)S(1)}, u32[]{:S(2)}, u32[]{:S(2)}) collective-permute-start(f32[64,512]{1,0:T(8,128)S(1)} %add.15), channel_id=1, source_target_pairs={{0,2},{1,3},{2,0},{3,1},{4,6},{5,7},{6,4},{7,5},{8,10},{9,11},{10,... | collective-permute-start | bytes 393224 | tf_op jit(solution)/shard_map/ppermute | solution.py:395
  28.3 0.0 collective-permute-done.7
  28.4 2.9 %collective-permute-done.9.refs_1_ = f32[64,512]{1,0:T(8,128)S(1)} collective-permute-done((f32[64,512]{1,0:T(8,128)S(1)}, f32[64,512]{1,0:T(8,128)S(1)}, u32[]{:S(2)}, u32[]{:S(2)}) %collective-permute-start.9) | collective-permute-done | bytes 131104 | tf_op jit(solution)/shard_map/ppermute | solution.py:395
  31.2 2.7 %collective-permute-done.11.refs_2_ = f32[64,512]{1,0:T(8,128)S(1)} collective-permute-done((f32[64,512]{1,0:T(8,128)S(1)}, f32[64,512]{1,0:T(8,128)S(1)}, u32[]{:S(2)}, u32[]{:S(2)}) %collective-permute-start.11) | collective-permute-done | bytes 131104 | tf_op jit(solution)/shard_map/ppermute | solution.py:395
  33.9 0.1 collective-permute-done.13.refs_3_
  34.0 0.9 %sum_and_rows.1 = f32[64,512]{1,0:T(8,128)} custom-call(f32[64,512]{1,0:T(8,128)S(1)} %add.12.refs_0_, f32[64,512]{1,0:T(8,128)S(1)} %collective-permute-done.9.refs_1_, f32[64,512]{1,0:T(8,128)S(1)} %collective-permute-done.11.refs_2_, f32[64,512]{1,0:T(8,128)S(1)} %collective-permute-done.13.refs_3_, f32[64,512]{1,0:T(8,128)S(1)} %get-tuple-element.30.refs_0_.refs_4_, ...), custom_call_target="tpu_custom_call" | custom-call | tf_op jit(solution)/shard_map/sum_and_rows/pallas_call | solution.py:475
  (4 shorter events, 0.1 us)
Async XLA Ops:
  0.6 12.0 %collective-permute-start.2 = (f32[64,512]{1,0:T(8,128)}, f32[64,512]{1,0:T(8,128)S(1)}, u32[]{:S(2)}, u32[]{:S(2)}) collective-permute-start(f32[64,512]{1,0:T(8,128)} %bitcast.8), channel_id=1, source_target_pairs={{0,6},{1,7},{2,4},{3,5},{4,2},{5,3},{6,0},{7,1},{8,14},{9,15},{10,... | collective-permute-start | bytes 393224 | tf_op jit(solution)/shard_map/ppermute | solution.py:395
  4.6 8.0 %collective-permute-start.1 = (f32[64,512]{1,0:T(8,128)}, f32[64,512]{1,0:T(8,128)S(1)}, u32[]{:S(2)}, u32[]{:S(2)}) collective-permute-start(f32[64,512]{1,0:T(8,128)} %bitcast.9), channel_id=1, source_target_pairs={{0,4},{1,5},{2,6},{3,7},{4,0},{5,1},{6,2},{7,3},{8,12},{9,13},{10,... | collective-permute-start | bytes 393224 | tf_op jit(solution)/shard_map/ppermute | solution.py:395
  5.1 7.5 %collective-permute-start = (f32[64,512]{1,0:T(8,128)}, f32[64,512]{1,0:T(8,128)S(1)}, u32[]{:S(2)}, u32[]{:S(2)}) collective-permute-start(f32[64,512]{1,0:T(8,128)} %bitcast.10), channel_id=1, source_target_pairs={{0,2},{1,3},{2,0},{3,1},{4,6},{5,7},{6,4},{7,5},{8,10},{9,11},{10,... | collective-permute-start | bytes 393224 | tf_op jit(solution)/shard_map/ppermute | solution.py:395
  6.3 6.8 %collective-permute-start.3 = (s32[2,72,128]{2,1,0:T(8,128)S(1)}, s32[2,72,128]{2,1,0:T(8,128)S(1)}, u32[]{:S(2)}, u32[]{:S(2)}) collective-permute-start(s32[2,72,128]{2,1,0:T(8,128)S(1)} %get-tuple-element.35), channel_id=1, source_target_pairs={{0,16},{8,24},{16,0},{24,8},{1,17},{9,25},{17,1},{25,9},{2,18},{10... | collective-permute-start | bytes 221192 | tf_op jit(solution)/shard_map/ppermute | solution.py:395
  9.4 4.4 %collective-permute-start.4 = (s32[2,72,128]{2,1,0:T(8,128)S(1)}, s32[2,72,128]{2,1,0:T(8,128)S(1)}, u32[]{:S(2)}, u32[]{:S(2)}) collective-permute-start(s32[2,72,128]{2,1,0:T(8,128)S(1)} %get-tuple-element.36), channel_id=1, source_target_pairs={{0,8},{8,0},{16,24},{24,16},{1,9},{9,1},{17,25},{25,17},{2,10},{10... | collective-permute-start | bytes 221192 | tf_op jit(solution)/shard_map/ppermute | solution.py:395
  13.7 2.6 %collective-permute-start.6 = (f32[2,128,512]{2,1,0:T(8,128)S(1)}, f32[2,128,512]{2,1,0:T(8,128)S(1)}, u32[]{:S(2)}, u32[]{:S(2)}) collective-permute-start(f32[2,128,512]{2,1,0:T(8,128)S(1)} %along_y.1.refs_1_), channel_id=1, source_target_pairs={{0,1},{1,0},{2,3},{3,2},{4,5},{5,4},{6,7},{7,6},{8,9},{9,8},{10,11... | collective-permute-start | bytes 1572872 | tf_op jit(solution)/shard_map/ppermute | solution.py:395
  13.7 6.6 %collective-permute-start.5 = (s32[2,72,128]{2,1,0:T(8,128)S(1)}, s32[2,72,128]{2,1,0:T(8,128)S(1)}, u32[]{:S(2)}, u32[]{:S(2)}) collective-permute-start(s32[2,72,128]{2,1,0:T(8,128)S(1)} %get-tuple-element.39), channel_id=1, source_target_pairs={{0,24},{8,16},{16,8},{24,0},{1,25},{9,17},{17,9},{25,1},{2,26},{10... | collective-permute-start | bytes 221192 | tf_op jit(solution)/shard_map/ppermute | solution.py:395
  23.2 1.4 %collective-permute-start.8 = (f32[64,512]{1,0:T(8,128)S(1)}, f32[64,512]{1,0:T(8,128)S(1)}, u32[]{:S(2)}, u32[]{:S(2)}) collective-permute-start(f32[64,512]{1,0:T(8,128)S(1)} %get-tuple-element.48), channel_id=1, source_target_pairs={{0,1},{1,0},{2,3},{3,2},{4,5},{5,4},{6,7},{7,6},{8,9},{9,8},{10,11... | collective-permute-start | bytes 393224 | tf_op jit(solution)/shard_map/ppermute | solution.py:395
  23.2 3.9 %collective-permute-start.10 = (f32[64,512]{1,0:T(8,128)S(1)}, f32[64,512]{1,0:T(8,128)S(1)}, u32[]{:S(2)}, u32[]{:S(2)}) collective-permute-start(f32[64,512]{1,0:T(8,128)S(1)} %get-tuple-element.50), channel_id=1, source_target_pairs={{0,1},{1,0},{2,3},{3,2},{4,5},{5,4},{6,7},{7,6},{8,9},{9,8},{10,11... | collective-permute-start | bytes 393224 | tf_op jit(solution)/shard_map/ppermute | solution.py:395
  23.7 4.0 %collective-permute-start.12 = (f32[64,512]{1,0:T(8,128)S(1)}, f32[64,512]{1,0:T(8,128)S(1)}, u32[]{:S(2)}, u32[]{:S(2)}) collective-permute-start(f32[64,512]{1,0:T(8,128)S(1)} %get-tuple-element.52), channel_id=1, source_target_pairs={{0,1},{1,0},{2,3},{3,2},{4,5},{5,4},{6,7},{7,6},{8,9},{9,8},{10,11... | collective-permute-start | bytes 393224 | tf_op jit(solution)/shard_map/ppermute | solution.py:395
  23.8 4.5 %collective-permute-start.7 = (f32[64,512]{1,0:T(8,128)S(1)}, f32[64,512]{1,0:T(8,128)S(1)}, u32[]{:S(2)}, u32[]{:S(2)}) collective-permute-start(f32[64,512]{1,0:T(8,128)S(1)} %get-tuple-element.46), channel_id=1, source_target_pairs={{0,1},{1,0},{2,3},{3,2},{4,5},{5,4},{6,7},{7,6},{8,9},{9,8},{10,11... | collective-permute-start | bytes 393224 | tf_op jit(solution)/shard_map/ppermute | solution.py:395
  24.6 6.6 %collective-permute-start.9 = (f32[64,512]{1,0:T(8,128)S(1)}, f32[64,512]{1,0:T(8,128)S(1)}, u32[]{:S(2)}, u32[]{:S(2)}) collective-permute-start(f32[64,512]{1,0:T(8,128)S(1)} %add.13), channel_id=1, source_target_pairs={{0,6},{1,7},{2,4},{3,5},{4,2},{5,3},{6,0},{7,1},{8,14},{9,15},{10,... | collective-permute-start | bytes 393224 | tf_op jit(solution)/shard_map/ppermute | solution.py:395
  27.1 6.8 %collective-permute-start.11 = (f32[64,512]{1,0:T(8,128)S(1)}, f32[64,512]{1,0:T(8,128)S(1)}, u32[]{:S(2)}, u32[]{:S(2)}) collective-permute-start(f32[64,512]{1,0:T(8,128)S(1)} %add.14), channel_id=1, source_target_pairs={{0,4},{1,5},{2,6},{3,7},{4,0},{5,1},{6,2},{7,3},{8,12},{9,13},{10,... | collective-permute-start | bytes 393224 | tf_op jit(solution)/shard_map/ppermute | solution.py:395
  27.7 6.3 %collective-permute-start.13 = (f32[64,512]{1,0:T(8,128)S(1)}, f32[64,512]{1,0:T(8,128)S(1)}, u32[]{:S(2)}, u32[]{:S(2)}) collective-permute-start(f32[64,512]{1,0:T(8,128)S(1)} %add.15), channel_id=1, source_target_pairs={{0,2},{1,3},{2,0},{3,1},{4,6},{5,7},{6,4},{7,5},{8,10},{9,11},{10,... | collective-permute-start | bytes 393224 | tf_op jit(solution)/shard_map/ppermute | solution.py:395

commit v3 on v2

--- a/solution.py
+++ b/solution.py
@@ -15,6 +15,7 @@
 PIVOT = 1.0
 GROWTH = 7.0 / 8.0
 PAD = 16
+STENCIL_ROWS = 16
 MIB = 1024 * 1024
 VMEM = pltpu.VMEM
 F32 = jnp.float32
@@ -121,7 +122,9 @@
 
 
 def mm3(a, b):
-    return mm(a[0], b[0]) + (mm(a[0], b[1]) + mm(a[1], b[0]))
+    count = a[0].shape[0]
+    both = mm(jnp.concatenate([a[0], a[1]], axis=0), b[0])
+    return both[:count] + (both[count:] + mm(a[0], b[1]))
 
 
 def turn_rows(a, step):
@@ -172,12 +175,10 @@
 def field_kernel(n, rows, side, *refs):
     half, q = side // 2, side // 4
     ring = rows + PAD
-    stencil_in, own, other, packed, reals = refs[:5]
+    values, own, other, packed, reals = refs[:5]
     density_out, smooth_out, fields_out = refs[5:8]
-    yh, yl, zh, zl, stencil, sem = refs[8:]
+    yh, yl, zh, zl = refs[8:]
     tabs = Tables(None, packed, reals, side, ring)
-    load = pltpu.make_async_copy(stencil_in, stencil, sem)
-    load.start()
 
     odd = lax.rem(lax.axis_index("gy"), 2)
     for i in range(n // 4):
@@ -223,63 +224,39 @@
     density = linear + GROWTH * linear * linear - (shift_x * slope_x + shift_y * slope_y)
     density_out[...] = density[:rows]
 
-    load.wait()
+    weights = [values[i : i + 1, :] for i in range(9)]
     beside = {0: density, 1: turn_lanes(density, -1), -1: turn_lanes(density, 1)}
     smooth = jnp.zeros_like(density)
     for a in (-1, 0, 1):
-        band = sum(stencil[(a + 1) * 3 + b + 1] * beside[b] for b in (-1, 0, 1))
+        band = sum(weights[(a + 1) * 3 + b + 1] * beside[b] for b in (-1, 0, 1))
         smooth = smooth + (turn_rows(band, -a) if a else band)
     smooth_out[...] = smooth[:rows]
 
 
-def adjoint_kernel(n, groups, rows, side, tiles, *refs):
+def adjoint_kernel(n, rows, side, *refs):
     half, q = side // 2, side // 4
     ring = rows + PAD
-    small = refs[:5]
-    msgs = refs[5 : 5 + groups]
-    smooth_in, fields, backs, packed, reals = refs[5 + groups : 10 + groups]
-    outs = refs[10 + groups : 10 + groups + n]
-    yh, yl, cnt, cls, part, *held, sems = refs[10 + groups + n :]
-    owner, stencil, mean_counts, bias_one, bias_two = held
+    values, counts, kinds, smooth_in, fields, density, backs, packed, reals = refs[:9]
+    density_out = refs[9]
+    outs = refs[10 : 10 + n]
+    yh, yl, part, sem = refs[10 + n :]
     tabs = Tables(backs, packed, reals, side, ring)
     ky = tabs.waves()
     me = lax.axis_index("gy")
-    mine = lax.axis_index("gx")
-    copies = [pltpu.make_async_copy(a, b, sems.at[i]) for i, (a, b) in enumerate(zip(small, held))]
-    for copy in copies:
-        copy.start()
-    for copy in copies:
-        copy.wait()
-
-    for t in range(tiles):
-        rank = jnp.int32(0)
-        for t2 in range(t):
-            rank = rank + (owner[t2] == owner[t]).astype(jnp.int32)
-        which = lax.bitwise_xor(owner[t], mine)
-        for k in range(groups):
-
-            @pl.when(which == k)
-            def _():
-                cnt[:, t * TC : (t + 1) * TC] = msgs[k][rank, :rows, :].astype(F32)
-                cls[:, t * TC : (t + 1) * TC] = msgs[k][rank, rows : rows + 8, :]
+    leave = pltpu.make_async_copy(density, density_out, sem)
+    leave.start()
 
     smooth = smooth_in[...]
     linear, shift_x, shift_y, slope_x, slope_y = [fields[i * ring : (i + 1) * ring, :] for i in range(5)]
-    classes = cls[...]
-    mean_v, one_v, two_v = [jnp.full(classes.shape, ref[0], F32) for ref in (mean_counts, bias_one, bias_two)]
-    for d in range(1, mean_counts.shape[0]):
-        hit = classes == d
-        mean_v = jnp.where(hit, mean_counts[d], mean_v)
-        one_v = jnp.where(hit, bias_one[d], one_v)
-        two_v = jnp.where(hit, bias_two[d], two_v)
-    mean_v, one_v, two_v = mean_v[:1], one_v[:1], two_v[:1]
+    mean_v, one_v, two_v = [kinds[i * 8 : i * 8 + 1, :] for i in range(3)]
     rate = mean_v * jnp.exp(one_v * smooth + two_v * smooth * smooth)
-    score = (cnt[...] - rate) * (one_v + 2.0 * two_v * smooth)
+    score = (counts[...] - rate) * (one_v + 2.0 * two_v * smooth)
     score = jnp.concatenate([score, jnp.zeros((PAD, side), F32)], axis=0)
+    weights = [values[i : i + 1, :] for i in range(9)]
     beside = {0: score, 1: turn_lanes(score, 1), -1: turn_lanes(score, -1)}
     pulled = jnp.zeros_like(score)
     for a in (-1, 0, 1):
-        band = sum(stencil[(a + 1) * 3 + b + 1] * beside[b] for b in (-1, 0, 1))
+        band = sum(weights[(a + 1) * 3 + b + 1] * beside[b] for b in (-1, 0, 1))
         pulled = pulled + (turn_rows(band, a) if a else band)
 
     bars = jnp.concatenate(
@@ -324,32 +301,82 @@
         place = place_of(me, k, n)
         off = pl.multiple_of(lax.rem(place, n // 2) * rows, rows)
         outs[k][...] = part[place // (n // 2), pl.ds(off, rows), :]
-
-
-def message_kernel(groups, capacity, rows, counts, depth, noise, *refs):
-    msgs = refs[:groups]
-    noise_out, classes, sems = refs[groups:]
+    leave.wait()
+
+
+def message_kernel(groups, capacity, rows, side, *refs):
+    counts, depth, noise, *small = refs[:8]
+    msgs = refs[8 : 8 + groups]
+    noise_out, picks, values = refs[8 + groups : 11 + groups]
+    classes, owner, stencil, *kinds, sems = refs[11 + groups :]
     mine = lax.axis_index("gx")
-    first = pltpu.make_async_copy(depth, classes, sems.at[groups])
-    first.start()
+    heads = [
+        pltpu.make_async_copy(a, b, sems.at[i]) for i, (a, b) in enumerate(zip((depth, *small), (classes, owner, stencil, *kinds)))
+    ]
+    for copy in heads:
+        copy.start()
     copies = []
     for k in range(groups):
         start = lax.bitwise_xor(mine, k) * capacity
         copies.append(
             pltpu.make_async_copy(
-                counts.at[pl.ds(start, capacity)], msgs[k].at[:, pl.ds(0, rows), :], sems.at[k]
+                counts.at[pl.ds(start * rows, capacity * rows)], msgs[k].at[pl.ds(0, capacity * rows), :], sems.at[6 + k]
             )
         )
-        copies[k].start()
-    copies.append(pltpu.make_async_copy(noise, noise_out, sems.at[groups + 1]))
-    copies[groups].start()
-    first.wait()
+    copies.append(pltpu.make_async_copy(noise, noise_out, sems.at[6 + groups]))
+    for copy in copies:
+        copy.start()
+    for copy in heads:
+        copy.wait()
     for k in range(groups):
         start = lax.bitwise_xor(mine, k) * capacity
         for r in range(capacity):
-            msgs[k][r, rows : rows + 8, :] = jnp.full((8, TC), classes[start + r], jnp.int32)
+            at = capacity * rows + r
+            msgs[k][at : at + 1, :] = jnp.full((1, TC), classes[start + r], jnp.int32)
+    for t in range(owner.shape[0]):
+        rank = jnp.int32(0)
+        for t2 in range(t):
+            rank = rank + (owner[t2] == owner[t]).astype(jnp.int32)
+        pick = lax.bitwise_xor(owner[t], mine) * capacity + rank
+        picks[:, t * TC : (t + 1) * TC] = jnp.full((8, TC), pick, jnp.int32)
+    for i in range(stencil.shape[0]):
+        values[i : i + 1, :] = jnp.full((1, side), stencil[i], F32)
+    at = STENCIL_ROWS
+    for kind in kinds:
+        for d in range(kind.shape[0]):
+            values[at : at + 1, :] = jnp.full((1, side), kind[d], F32)
+            at += 1
     for copy in copies:
         copy.wait()
+
+
+def select_kernel(groups, capacity, rows, depths, *refs):
+    msgs = refs[:groups][::-1]
+    picks, values, counts_out, kinds_out = refs[groups:]
+    side = counts_out.shape[1]
+
+    def piece(k, r):
+        at = capacity * rows + r
+        return msgs[k][r * rows : (r + 1) * rows, :], msgs[k][at : at + 1, :]
+
+    for t in range(side // TC):
+        cols = slice(t * TC, (t + 1) * TC)
+        pick = picks[:1, cols]
+        cells, classes = piece(0, 0)
+        for k in range(groups):
+            for r in range(capacity):
+                if k + r:
+                    hit = pick == k * capacity + r
+                    more, kind = piece(k, r)
+                    cells = jnp.where(hit, more, cells)
+                    classes = jnp.where(hit, kind, classes)
+        counts_out[:, cols] = cells.astype(F32)
+        for i in range(3):
+            at = STENCIL_ROWS + i * depths
+            value = values[at : at + 1, cols]
+            for d in range(1, depths):
+                value = jnp.where(classes == d, values[at + d : at + d + 1, cols], value)
+            kinds_out[i * 8 : (i + 1) * 8, cols] = jnp.broadcast_to(value, (8, TC))
 
 
 def table_kernel(*refs):
@@ -397,16 +424,26 @@
     blocks = {}
     for k in range(n - 2, 0, -2):
         blocks[k] = swap(own, k)
-    *msgs, blocks[0] = pl.pallas_call(
-        functools.partial(message_kernel, groups, capacity, rows),
-        out_shape=[VMEM((capacity, rows + 8, TC), jnp.int32)] * groups
-        + [VMEM((rows, side), F32)],
-        in_specs=[hbm] * 3,
-        out_specs=[vmem] * (groups + 1),
-        scratch_shapes=[pltpu.SMEM((slots,), jnp.int32), pltpu.SemaphoreType.DMA((groups + 2,))],
+    small = (owner.reshape(tiles), stencil, mean_counts, bias_one, bias_two)
+    depths = mean_counts.shape[0]
+    *msgs, blocks[0], picks, values = pl.pallas_call(
+        functools.partial(message_kernel, groups, capacity, rows, side),
+        out_shape=[VMEM((capacity * rows + 8, TC), jnp.int32)] * groups
+        + [
+            VMEM((rows, side), F32),
+            VMEM((8, side), jnp.int32),
+            VMEM((STENCIL_ROWS + -(-3 * depths // 8) * 8, side), F32),
+        ],
+        in_specs=[hbm] * 8,
+        out_specs=[vmem] * (groups + 3),
+        scratch_shapes=[
+            pltpu.SMEM((slots,), jnp.int32),
+            *[pltpu.SMEM(a.shape, a.dtype) for a in small],
+            pltpu.SemaphoreType.DMA((groups + 7,)),
+        ],
         compiler_params=pltpu.CompilerParams(vmem_limit_bytes=4 * MIB),
         name="messages",
-    )(in_hbm(counts.reshape(slots, rows, TC)), in_hbm(depth.reshape(slots)), in_hbm(own))
+    )(*[in_hbm(a) for a in (counts.reshape(slots * rows, TC), depth.reshape(slots), own, *small)])
     for k in range(groups - 1, 0, -1):
         msgs[k] = swap(msgs[k], k, "gx", groups)
 
@@ -431,43 +468,44 @@
         out_specs=vmem,
         scratch_shapes=[VMEM((2, half // 2, side), BF16)] * 2,
         compiler_params=pltpu.CompilerParams(vmem_limit_bytes=8 * MIB),
-        cost_estimate=pl.CostEstimate(flops=1, bytes_accessed=1, transcendentals=0),
         name="along_y",
     )(*[blocks[k] for k in range(0, n, 2)], backs)
-    held, msgs[2], msgs[1] = lax.optimization_barrier((along_y, msgs[2], msgs[1]))
-    other = swap(held, 1)
+    other = swap(along_y, 1)
+    picked, kinds = pl.pallas_call(
+        functools.partial(select_kernel, groups, capacity, rows, depths),
+        out_shape=[VMEM((rows, side), F32), VMEM((24, side), F32)],
+        in_specs=[vmem] * (groups + 2),
+        out_specs=[vmem] * 2,
+        compiler_params=pltpu.CompilerParams(vmem_limit_bytes=4 * MIB),
+        cost_estimate=pl.CostEstimate(flops=20_000_000_000, bytes_accessed=1, transcendentals=0),
+        name="select",
+    )(*msgs[::-1], picks, values)
+    other, picked, kinds = lax.optimization_barrier((other, picked, kinds))
     density, smooth, fields = pl.pallas_call(
         functools.partial(field_kernel, n, rows, side),
-        out_shape=[cell, VMEM((rows, side), F32), VMEM((5 * ring, side), F32)],
-        in_specs=[hbm] + [vmem] * 4,
+        out_shape=[VMEM((rows, side), F32), VMEM((rows, side), F32), VMEM((5 * ring, side), F32)],
+        in_specs=[vmem] * 5,
         out_specs=[vmem] * 3,
         scratch_shapes=[
             *[VMEM((2, half, side), BF16)] * 2,
             *[VMEM((side, 2 * side), BF16)] * 2,
-            pltpu.SMEM(stencil.shape, F32),
+        ],
+        compiler_params=pltpu.CompilerParams(vmem_limit_bytes=16 * MIB),
+        name="fields",
+    )(values, along_y, other, packed, reals)
+    density, *parts = pl.pallas_call(
+        functools.partial(adjoint_kernel, n, rows, side),
+        out_shape=[cell] * (1 + n),
+        in_specs=[vmem] * 9,
+        out_specs=[hbm] + [vmem] * n,
+        scratch_shapes=[
+            *[VMEM((2, half, side), BF16)] * 2,
+            VMEM((2, half, side), F32),
             pltpu.SemaphoreType.DMA,
         ],
         compiler_params=pltpu.CompilerParams(vmem_limit_bytes=16 * MIB),
-        cost_estimate=pl.CostEstimate(flops=1, bytes_accessed=1, transcendentals=0),
-        name="fields",
-    )(in_hbm(stencil), along_y, other, packed, reals)
-    small = (owner.reshape(tiles), stencil, mean_counts, bias_one, bias_two)
-    parts = pl.pallas_call(
-        functools.partial(adjoint_kernel, n, groups, rows, side, tiles),
-        out_shape=[cell] * n,
-        in_specs=[hbm] * 5 + [vmem] * (groups + 5),
-        out_specs=[vmem] * n,
-        scratch_shapes=[
-            *[VMEM((2, half, side), BF16)] * 2,
-            VMEM((rows, side), F32),
-            VMEM((8, side), jnp.int32),
-            VMEM((2, half, side), F32),
-            *[pltpu.SMEM(a.shape, a.dtype) for a in small],
-            pltpu.SemaphoreType.DMA((5,)),
-        ],
-        compiler_params=pltpu.CompilerParams(vmem_limit_bytes=16 * MIB),
         name="adjoint",
-    )(*[in_hbm(a) for a in small], *msgs, smooth, fields, backs, packed, reals)
+    )(values, picked, kinds, smooth, fields, density, backs, packed, reals)
     sums = {}
     for k in range(n - 2, -1, -2):
         sums[k] = parts[k] + swap(parts[k + 1], 1)

time: 35.1 us -> 31.9 us (0.909)
  starting transfers between devices: 16.6 us -> 14.1 us
  Pallas kernels: 9.58 us -> 8.18 us
  waiting for transfers between devices: 7.9 us -> 8.56 us
    ppermute x14, starting transfers between devices: 16.6 us -> 14.1 us  [swap(): return lax.ppermute(value, axis, [(i, i ^ k) for i in range(size)])]
    pallas_call x2 -> x3, Pallas kernels: 3.92 us -> 3.17 us  [the longest x1 1.96 us: local(): pl.pallas_call(functools.partial(adjoint_kernel, n, rows, side), out_shap...]
    ppermute x14, waiting for transfers between devices: 7.9 us -> 8.56 us  [swap(): return lax.ppermute(value, axis, [(i, i ^ k) for i in range(size)])]
    pallas_call x1, Pallas kernels: 2.61 us -> 2.01 us  [local(): pl.pallas_call(functools.partial(field_kernel, n, rows, side), out_shape=...]
  transfers between devices with their start and end apart: 14 -> 14, of which waited for: 6 -> 5; matrix products, arithmetic and copies ran while one was open for 0% -> 0% of each run, Pallas kernels for 17% -> 11%
where the time goes in v3:
time: 31.9 us; the launch traced here: 31.7 us
  starting transfers between devices  14.1 us (44%)
  waiting for transfers between devices  8.56 us (27%)
  Pallas kernels  8.18 us (26%)
  between operations  0.74 us (2%)
    ppermute x14, starting transfers between devices, swap(): return lax.ppermute(value, axis, [(i, i ^ k) for i in range(size)])  14.1 us
    ppermute x14, waiting for transfers between devices, swap(): return lax.ppermute(value, axis, [(i, i ^ k) for i in range(size)])  8.56 us
    pallas_call x1, Pallas kernels, local(): pl.pallas_call(functools.partial(field_kernel, n, rows, side), out_shape=...  2.01 us
    pallas_call x1, Pallas kernels, local(): pl.pallas_call(functools.partial(adjoint_kernel, n, rows, side), out_shap...  1.96 us
    pallas_call x1, Pallas kernels, local(): pl.pallas_call(table_kernel, out_shape=[VMEM(t.shape, t.dtype) for t in (...  1.64 us
    pallas_call x1, Pallas kernels, local(): pl.pallas_call(functools.partial(message_kernel, groups, capacity, rows,...  1.14 us
    pallas_call x1, Pallas kernels, local(): pl.pallas_call(functools.partial(last_kernel, len(pieces)), out_shape=cel...  0.88 us
  transfers between devices with their start and end apart: 14, of which 5 were waited for; matrix products, arithmetic and copies ran while one was open for 0% of the time, Pallas kernels for 11%

profile of v3, /device:TPU:0, one launch (start us, length us, event | category | flops | bytes accessed | tf_op | source)
XLA Modules:
  0.0 31.7 jit_solution(9507238695919249548)
XLA Ops:
  0.6 4.0 %collective-permute-start.2 = (f32[64,512]{1,0:T(8,128)}, f32[64,512]{1,0:T(8,128)S(1)}, u32[]{:S(2)}, u32[]{:S(2)}) collective-permute-start(f32[64,512]{1,0:T(8,128)} %bitcast.7), channel_id=1, source_target_pairs={{0,6},{1,7},{2,4},{3,5},{4,2},{5,3},{6,0},{7,1},{8,14},{9,15},{10,... | collective-permute-start | bytes 393224 | tf_op jit(solution)/shard_map/ppermute | solution.py:422
  4.6 0.5 %collective-permute-start.1 = (f32[64,512]{1,0:T(8,128)}, f32[64,512]{1,0:T(8,128)S(1)}, u32[]{:S(2)}, u32[]{:S(2)}) collective-permute-start(f32[64,512]{1,0:T(8,128)} %bitcast.8), channel_id=1, source_target_pairs={{0,4},{1,5},{2,6},{3,7},{4,0},{5,1},{6,2},{7,3},{8,12},{9,13},{10,... | collective-permute-start | bytes 393224 | tf_op jit(solution)/shard_map/ppermute | solution.py:422
  5.1 0.1 collective-permute-start
  5.2 1.1 %messages.1 = (s32[136,128]{1,0:T(8,128)S(1)}, s32[136,128]{1,0:T(8,128)S(1)}, s32[136,128]{1,0:T(8,128)S(1)}, s32[136,128]{1,0:T(8,128)S(1)}, f32[64,512]{1,0:T...) custom-call(s32[512,128]{1,0:T(8,128)} %bitcast.6, s32[8]{0:T(128)} %bitcast.12, f32[64,512]{1,0:T(8,128)} %bitcast.10, ...), custom_call_target="tpu_custom_call" | custom-call | tf_op jit(solution)/shard_map/messages/pallas_call | solution.py:429
  6.4 4.1 %collective-permute-start.4 = (s32[136,128]{1,0:T(8,128)S(1)}, s32[136,128]{1,0:T(8,128)S(1)}, u32[]{:S(2)}, u32[]{:S(2)}) collective-permute-start(s32[136,128]{1,0:T(8,128)S(1)} %get-tuple-element.40), channel_id=1, source_target_pairs={{0,24},{8,16},{16,8},{24,0},{1,25},{9,17},{17,9},{25,1},{2,26},{10... | collective-permute-start | bytes 208904 | tf_op jit(solution)/shard_map/ppermute | solution.py:422
  10.4 0.0 collective-permute-start.5
  10.4 0.0 collective-permute-done.2.refs_3_
  10.5 0.6 %collective-permute-start.6 = (s32[136,128]{1,0:T(8,128)S(1)}, s32[136,128]{1,0:T(8,128)S(1)}, u32[]{:S(2)}, u32[]{:S(2)}) collective-permute-start(s32[136,128]{1,0:T(8,128)S(1)} %get-tuple-element.42), channel_id=1, source_target_pairs={{0,8},{8,0},{16,24},{24,16},{1,9},{9,1},{17,25},{25,17},{2,10},{10... | collective-permute-start | bytes 208904 | tf_op jit(solution)/shard_map/ppermute | solution.py:422
  11.1 1.6 %tables.1 = (bf16[512,512]{1,0:T(8,128)(2,1)S(1)}, bf16[1344,512]{1,0:T(8,128)(2,1)S(1)}, f32[520,256]{1,0:T(8,128)S(1)}) custom-call(bf16[512,512]{1,0:T(8,128)(2,1)} %constant.6.clone.refs_0_, bf16[1344,512]{1,0:T(8,128)(2,1)} %constant.7.clone.refs_1_, f32[520,256]{1,0:T(8,128)} %constant.8.clone.refs_2_), custom_call_target="tpu_custom_call" | custom-call | tf_op jit(solution)/shard_map/tables/pallas_call | solution.py:452
  12.7 0.0 collective-permute-done.1.refs_2_
  12.8 0.0 collective-permute-done.refs_1_
  12.8 0.5 %along_y.1.refs_1_ = f32[2,128,512]{2,1,0:T(8,128)S(1)} custom-call(f32[64,512]{1,0:T(8,128)S(1)} %get-tuple-element.35.refs_0_.refs_4_, f32[64,512]{1,0:T(8,128)S(1)} %collective-permute-done.refs_1_, f32[64,512]{1,0:T(8,128)S(1)} %collective-permute-done.1.refs_2_, f32[64,512]{1,0:T(8,128)S(1)} %collective-permute-done.2.refs_3_, ...), custom_call_target="tpu_custom_call" | custom-call | tf_op jit(solution)/shard_map/along_y/pallas_call | solution.py:464
  13.2 0.1 collective-permute-start.3
  13.3 0.0 collective-permute-done.4.refs_0_
  13.3 2.6 %collective-permute-done.5.refs_1_ = s32[136,128]{1,0:T(8,128)S(1)} collective-permute-done((s32[136,128]{1,0:T(8,128)S(1)}, s32[136,128]{1,0:T(8,128)S(1)}, u32[]{:S(2)}, u32[]{:S(2)}) %collective-permute-start.5) | collective-permute-done | bytes 69664 | tf_op jit(solution)/shard_map/ppermute | solution.py:422
  15.9 0.0 collective-permute-done.6.refs_2_
  15.9 0.1 select.1
  16.0 0.0 collective-permute-done.3.refs_2_
  16.0 2.0 %fields.1 = (f32[64,512]{1,0:T(8,128)S(1)}, f32[64,512]{1,0:T(8,128)S(1)}, f32[400,512]{1,0:T(8,128)S(1)}) custom-call(f32[32,512]{1,0:T(8,128)S(1)} %get-tuple-element.33.refs_5_.refs_0_, f32[2,128,512]{2,1,0:T(8,128)S(1)} %along_y.1.refs_1_, f32[2,128,512]{2,1,0:T(8,128)S(1)} %collective-permute-done.3.refs_2_, ...), custom_call_target="tpu_custom_call" | custom-call | tf_op jit(solution)/shard_map/fields/pallas_call | solution.py:484
  18.0 2.0 %adjoint.1 = (f32[64,512]{1,0:T(8,128)}, f32[64,512]{1,0:T(8,128)S(1)}, f32[64,512]{1,0:T(8,128)S(1)}, f32[64,512]{1,0:T(8,128)S(1)}, f32[64,512]{1,0:T(8,128)S(...) custom-call(f32[32,512]{1,0:T(8,128)S(1)} %get-tuple-element.33.refs_5_.refs_, ...), custom_call_target="tpu_custom_call" | custom-call | tf_op jit(solution)/shard_map/adjoint/pallas_call | solution.py:496
  20.0 0.1 collective-permute-start.8
  20.1 0.5 %collective-permute-start.10 = (f32[64,512]{1,0:T(8,128)S(1)}, f32[64,512]{1,0:T(8,128)S(1)}, u32[]{:S(2)}, u32[]{:S(2)}) collective-permute-start(f32[64,512]{1,0:T(8,128)S(1)} %get-tuple-element.60), channel_id=1, source_target_pairs={{0,1},{1,0},{2,3},{3,2},{4,5},{5,4},{6,7},{7,6},{8,9},{9,8},{10,11... | collective-permute-start | bytes 393224 | tf_op jit(solution)/shard_map/ppermute | solution.py:422
  20.6 0.1 collective-permute-start.12
  20.6 0.4 %collective-permute-start.7 = (f32[64,512]{1,0:T(8,128)S(1)}, f32[64,512]{1,0:T(8,128)S(1)}, u32[]{:S(2)}, u32[]{:S(2)}) collective-permute-start(f32[64,512]{1,0:T(8,128)S(1)} %get-tuple-element.56), channel_id=1, source_target_pairs={{0,1},{1,0},{2,3},{3,2},{4,5},{5,4},{6,7},{7,6},{8,9},{9,8},{10,11... | collective-permute-start | bytes 393224 | tf_op jit(solution)/shard_map/ppermute | solution.py:422
  21.1 0.3 %collective-permute-done.8 = f32[64,512]{1,0:T(8,128)S(1)} collective-permute-done((f32[64,512]{1,0:T(8,128)S(1)}, f32[64,512]{1,0:T(8,128)S(1)}, u32[]{:S(2)}, u32[]{:S(2)}) %collective-permute-start.8) | collective-permute-done | bytes 131104 | tf_op jit(solution)/shard_map/ppermute | solution.py:422
  21.4 2.5 %collective-permute-start.9 = (f32[64,512]{1,0:T(8,128)S(1)}, f32[64,512]{1,0:T(8,128)S(1)}, u32[]{:S(2)}, u32[]{:S(2)}) collective-permute-start(f32[64,512]{1,0:T(8,128)S(1)} %add.13), channel_id=1, source_target_pairs={{0,6},{1,7},{2,4},{3,5},{4,2},{5,3},{6,0},{7,1},{8,14},{9,15},{10,... | collective-permute-start | bytes 393224 | tf_op jit(solution)/shard_map/ppermute | solution.py:422
  23.9 0.0 collective-permute-done.10
  24.0 0.6 %collective-permute-start.11 = (f32[64,512]{1,0:T(8,128)S(1)}, f32[64,512]{1,0:T(8,128)S(1)}, u32[]{:S(2)}, u32[]{:S(2)}) collective-permute-start(f32[64,512]{1,0:T(8,128)S(1)} %add.14), channel_id=1, source_target_pairs={{0,4},{1,5},{2,6},{3,7},{4,0},{5,1},{6,2},{7,3},{8,12},{9,13},{10,... | collective-permute-start | bytes 393224 | tf_op jit(solution)/shard_map/ppermute | solution.py:422
  24.5 0.0 collective-permute-done.12
  24.6 0.6 %collective-permute-start.13 = (f32[64,512]{1,0:T(8,128)S(1)}, f32[64,512]{1,0:T(8,128)S(1)}, u32[]{:S(2)}, u32[]{:S(2)}) collective-permute-start(f32[64,512]{1,0:T(8,128)S(1)} %add.15), channel_id=1, source_target_pairs={{0,2},{1,3},{2,0},{3,1},{4,6},{5,7},{6,4},{7,5},{8,10},{9,11},{10,... | collective-permute-start | bytes 393224 | tf_op jit(solution)/shard_map/ppermute | solution.py:422
  25.2 0.0 collective-permute-done.7
  25.2 2.9 %collective-permute-done.9.refs_1_ = f32[64,512]{1,0:T(8,128)S(1)} collective-permute-done((f32[64,512]{1,0:T(8,128)S(1)}, f32[64,512]{1,0:T(8,128)S(1)}, u32[]{:S(2)}, u32[]{:S(2)}) %collective-permute-start.9) | collective-permute-done | bytes 131104 | tf_op jit(solution)/shard_map/ppermute | solution.py:422
  28.0 2.7 %collective-permute-done.11.refs_2_ = f32[64,512]{1,0:T(8,128)S(1)} collective-permute-done((f32[64,512]{1,0:T(8,128)S(1)}, f32[64,512]{1,0:T(8,128)S(1)}, u32[]{:S(2)}, u32[]{:S(2)}) %collective-permute-start.11) | collective-permute-done | bytes 131104 | tf_op jit(solution)/shard_map/ppermute | solution.py:422
  30.7 0.1 collective-permute-done.13.refs_3_
  30.8 0.9 %sum_and_rows.1 = f32[64,512]{1,0:T(8,128)} custom-call(f32[64,512]{1,0:T(8,128)S(1)} %add.12.refs_0_, f32[64,512]{1,0:T(8,128)S(1)} %collective-permute-done.9.refs_1_, f32[64,512]{1,0:T(8,128)S(1)} %collective-permute-done.11.refs_2_, f32[64,512]{1,0:T(8,128)S(1)} %collective-permute-done.13.refs_3_, f32[64,512]{1,0:T(8,128)S(1)} %get-tuple-element.35.refs_0_.refs_4_, ...), custom_call_target="tpu_custom_call" | custom-call | tf_op jit(solution)/shard_map/sum_and_rows/pallas_call | solution.py:513
  (4 shorter events, 0.1 us)
Async XLA Ops:
  0.6 9.8 %collective-permute-start.2 = (f32[64,512]{1,0:T(8,128)}, f32[64,512]{1,0:T(8,128)S(1)}, u32[]{:S(2)}, u32[]{:S(2)}) collective-permute-start(f32[64,512]{1,0:T(8,128)} %bitcast.7), channel_id=1, source_target_pairs={{0,6},{1,7},{2,4},{3,5},{4,2},{5,3},{6,0},{7,1},{8,14},{9,15},{10,... | collective-permute-start | bytes 393224 | tf_op jit(solution)/shard_map/ppermute | solution.py:422
  4.6 8.2 %collective-permute-start.1 = (f32[64,512]{1,0:T(8,128)}, f32[64,512]{1,0:T(8,128)S(1)}, u32[]{:S(2)}, u32[]{:S(2)}) collective-permute-start(f32[64,512]{1,0:T(8,128)} %bitcast.8), channel_id=1, source_target_pairs={{0,4},{1,5},{2,6},{3,7},{4,0},{5,1},{6,2},{7,3},{8,12},{9,13},{10,... | collective-permute-start | bytes 393224 | tf_op jit(solution)/shard_map/ppermute | solution.py:422
  5.1 7.7 %collective-permute-start = (f32[64,512]{1,0:T(8,128)}, f32[64,512]{1,0:T(8,128)S(1)}, u32[]{:S(2)}, u32[]{:S(2)}) collective-permute-start(f32[64,512]{1,0:T(8,128)} %bitcast.9), channel_id=1, source_target_pairs={{0,2},{1,3},{2,0},{3,1},{4,6},{5,7},{6,4},{7,5},{8,10},{9,11},{10,... | collective-permute-start | bytes 393224 | tf_op jit(solution)/shard_map/ppermute | solution.py:422
  6.4 6.9 %collective-permute-start.4 = (s32[136,128]{1,0:T(8,128)S(1)}, s32[136,128]{1,0:T(8,128)S(1)}, u32[]{:S(2)}, u32[]{:S(2)}) collective-permute-start(s32[136,128]{1,0:T(8,128)S(1)} %get-tuple-element.40), channel_id=1, source_target_pairs={{0,24},{8,16},{16,8},{24,0},{1,25},{9,17},{17,9},{25,1},{2,26},{10... | collective-permute-start | bytes 208904 | tf_op jit(solution)/shard_map/ppermute | solution.py:422
  10.4 5.5 %collective-permute-start.5 = (s32[136,128]{1,0:T(8,128)S(1)}, s32[136,128]{1,0:T(8,128)S(1)}, u32[]{:S(2)}, u32[]{:S(2)}) collective-permute-start(s32[136,128]{1,0:T(8,128)S(1)} %get-tuple-element.41), channel_id=1, source_target_pairs={{0,16},{8,24},{16,0},{24,8},{1,17},{9,25},{17,1},{25,9},{2,18},{10... | collective-permute-start | bytes 208904 | tf_op jit(solution)/shard_map/ppermute | solution.py:422
  10.5 5.4 %collective-permute-start.6 = (s32[136,128]{1,0:T(8,128)S(1)}, s32[136,128]{1,0:T(8,128)S(1)}, u32[]{:S(2)}, u32[]{:S(2)}) collective-permute-start(s32[136,128]{1,0:T(8,128)S(1)} %get-tuple-element.42), channel_id=1, source_target_pairs={{0,8},{8,0},{16,24},{24,16},{1,9},{9,1},{17,25},{25,17},{2,10},{10... | collective-permute-start | bytes 208904 | tf_op jit(solution)/shard_map/ppermute | solution.py:422
  13.2 2.7 %collective-permute-start.3 = (f32[2,128,512]{2,1,0:T(8,128)S(1)}, f32[2,128,512]{2,1,0:T(8,128)S(1)}, u32[]{:S(2)}, u32[]{:S(2)}) collective-permute-start(f32[2,128,512]{2,1,0:T(8,128)S(1)} %along_y.1.refs_1_), channel_id=1, source_target_pairs={{0,1},{1,0},{2,3},{3,2},{4,5},{5,4},{6,7},{7,6},{8,9},{9,8},{10,11... | collective-permute-start | bytes 1572872 | tf_op jit(solution)/shard_map/ppermute | solution.py:422
  20.0 1.4 %collective-permute-start.8 = (f32[64,512]{1,0:T(8,128)S(1)}, f32[64,512]{1,0:T(8,128)S(1)}, u32[]{:S(2)}, u32[]{:S(2)}) collective-permute-start(f32[64,512]{1,0:T(8,128)S(1)} %get-tuple-element.58), channel_id=1, source_target_pairs={{0,1},{1,0},{2,3},{3,2},{4,5},{5,4},{6,7},{7,6},{8,9},{9,8},{10,11... | collective-permute-start | bytes 393224 | tf_op jit(solution)/shard_map/ppermute | solution.py:422
  20.1 3.9 %collective-permute-start.10 = (f32[64,512]{1,0:T(8,128)S(1)}, f32[64,512]{1,0:T(8,128)S(1)}, u32[]{:S(2)}, u32[]{:S(2)}) collective-permute-start(f32[64,512]{1,0:T(8,128)S(1)} %get-tuple-element.60), channel_id=1, source_target_pairs={{0,1},{1,0},{2,3},{3,2},{4,5},{5,4},{6,7},{7,6},{8,9},{9,8},{10,11... | collective-permute-start | bytes 393224 | tf_op jit(solution)/shard_map/ppermute | solution.py:422
  20.6 4.0 %collective-permute-start.12 = (f32[64,512]{1,0:T(8,128)S(1)}, f32[64,512]{1,0:T(8,128)S(1)}, u32[]{:S(2)}, u32[]{:S(2)}) collective-permute-start(f32[64,512]{1,0:T(8,128)S(1)} %get-tuple-element.62), channel_id=1, source_target_pairs={{0,1},{1,0},{2,3},{3,2},{4,5},{5,4},{6,7},{7,6},{8,9},{9,8},{10,11... | collective-permute-start | bytes 393224 | tf_op jit(solution)/shard_map/ppermute | solution.py:422
  20.6 4.5 %collective-permute-start.7 = (f32[64,512]{1,0:T(8,128)S(1)}, f32[64,512]{1,0:T(8,128)S(1)}, u32[]{:S(2)}, u32[]{:S(2)}) collective-permute-start(f32[64,512]{1,0:T(8,128)S(1)} %get-tuple-element.56), channel_id=1, source_target_pairs={{0,1},{1,0},{2,3},{3,2},{4,5},{5,4},{6,7},{7,6},{8,9},{9,8},{10,11... | collective-permute-start | bytes 393224 | tf_op jit(solution)/shard_map/ppermute | solution.py:422
  21.4 6.6 %collective-permute-start.9 = (f32[64,512]{1,0:T(8,128)S(1)}, f32[64,512]{1,0:T(8,128)S(1)}, u32[]{:S(2)}, u32[]{:S(2)}) collective-permute-start(f32[64,512]{1,0:T(8,128)S(1)} %add.13), channel_id=1, source_target_pairs={{0,6},{1,7},{2,4},{3,5},{4,2},{5,3},{6,0},{7,1},{8,14},{9,15},{10,... | collective-permute-start | bytes 393224 | tf_op jit(solution)/shard_map/ppermute | solution.py:422
  24.0 6.8 %collective-permute-start.11 = (f32[64,512]{1,0:T(8,128)S(1)}, f32[64,512]{1,0:T(8,128)S(1)}, u32[]{:S(2)}, u32[]{:S(2)}) collective-permute-start(f32[64,512]{1,0:T(8,128)S(1)} %add.14), channel_id=1, source_target_pairs={{0,4},{1,5},{2,6},{3,7},{4,0},{5,1},{6,2},{7,3},{8,12},{9,13},{10,... | collective-permute-start | bytes 393224 | tf_op jit(solution)/shard_map/ppermute | solution.py:422
  24.6 6.3 %collective-permute-start.13 = (f32[64,512]{1,0:T(8,128)S(1)}, f32[64,512]{1,0:T(8,128)S(1)}, u32[]{:S(2)}, u32[]{:S(2)}) collective-permute-start(f32[64,512]{1,0:T(8,128)S(1)} %add.15), channel_id=1, source_target_pairs={{0,2},{1,3},{2,0},{3,1},{4,6},{5,7},{6,4},{7,5},{8,10},{9,11},{10,... | collective-permute-start | bytes 393224 | tf_op jit(solution)/shard_map/ppermute | solution.py:422

commit v4 on v3

--- a/solution.py
+++ b/solution.py
@@ -305,10 +305,10 @@
 
 
 def message_kernel(groups, capacity, rows, side, *refs):
-    counts, depth, noise, *small = refs[:8]
-    msgs = refs[8 : 8 + groups]
-    noise_out, picks, values = refs[8 + groups : 11 + groups]
-    classes, owner, stencil, *kinds, sems = refs[11 + groups :]
+    counts, noise, backs, depth, *small = refs[:9]
+    msgs = refs[9 : 9 + groups]
+    noise_out, backs_out, picks, values = refs[9 + groups : 13 + groups]
+    classes, owner, stencil, *kinds, sems = refs[13 + groups :]
     mine = lax.axis_index("gx")
     heads = [
         pltpu.make_async_copy(a, b, sems.at[i]) for i, (a, b) in enumerate(zip((depth, *small), (classes, owner, stencil, *kinds)))
@@ -324,6 +324,7 @@
             )
         )
     copies.append(pltpu.make_async_copy(noise, noise_out, sems.at[6 + groups]))
+    copies.append(pltpu.make_async_copy(backs, backs_out, sems.at[7 + groups]))
     for copy in copies:
         copy.start()
     for copy in heads:
@@ -426,38 +427,28 @@
         blocks[k] = swap(own, k)
     small = (owner.reshape(tiles), stencil, mean_counts, bias_one, bias_two)
     depths = mean_counts.shape[0]
-    *msgs, blocks[0], picks, values = pl.pallas_call(
+    *msgs, blocks[0], backs, picks, values = pl.pallas_call(
         functools.partial(message_kernel, groups, capacity, rows, side),
         out_shape=[VMEM((capacity * rows + 8, TC), jnp.int32)] * groups
         + [
             VMEM((rows, side), F32),
+            VMEM(backs.shape, backs.dtype),
             VMEM((8, side), jnp.int32),
             VMEM((STENCIL_ROWS + -(-3 * depths // 8) * 8, side), F32),
         ],
-        in_specs=[hbm] * 8,
-        out_specs=[vmem] * (groups + 3),
+        in_specs=[hbm] * 9,
+        out_specs=[vmem] * (groups + 4),
         scratch_shapes=[
             pltpu.SMEM((slots,), jnp.int32),
             *[pltpu.SMEM(a.shape, a.dtype) for a in small],
-            pltpu.SemaphoreType.DMA((groups + 7,)),
+            pltpu.SemaphoreType.DMA((groups + 8,)),
         ],
         compiler_params=pltpu.CompilerParams(vmem_limit_bytes=4 * MIB),
         name="messages",
-    )(*[in_hbm(a) for a in (counts.reshape(slots * rows, TC), depth.reshape(slots), own, *small)])
+    )(*[in_hbm(a) for a in (counts.reshape(slots * rows, TC), own, backs, depth.reshape(slots), *small)])
     for k in range(groups - 1, 0, -1):
         msgs[k] = swap(msgs[k], k, "gx", groups)
 
-    noise_held, backs, packed, reals = lax.optimization_barrier((blocks[0], backs, packed, reals))
-    blocks[0] = noise_held
-    backs, packed, reals = pl.pallas_call(
-        table_kernel,
-        out_shape=[VMEM(t.shape, t.dtype) for t in (backs, packed, reals)],
-        in_specs=[hbm] * 3,
-        out_specs=[vmem] * 3,
-        scratch_shapes=[pltpu.SemaphoreType.DMA((3,))],
-        compiler_params=pltpu.CompilerParams(vmem_limit_bytes=4 * MIB),
-        name="tables",
-    )(in_hbm(backs), in_hbm(packed), in_hbm(reals))
     half = side // 2
     ring = rows + PAD
     cell = jax.ShapeDtypeStruct((rows, side), F32)
@@ -471,16 +462,17 @@
         name="along_y",
     )(*[blocks[k] for k in range(0, n, 2)], backs)
     other = swap(along_y, 1)
-    picked, kinds = pl.pallas_call(
-        functools.partial(select_kernel, groups, capacity, rows, depths),
-        out_shape=[VMEM((rows, side), F32), VMEM((24, side), F32)],
-        in_specs=[vmem] * (groups + 2),
+    packed, reals, _ = lax.optimization_barrier((packed, reals, along_y))
+    packed, reals = pl.pallas_call(
+        table_kernel,
+        out_shape=[VMEM(t.shape, t.dtype) for t in (packed, reals)],
+        in_specs=[hbm] * 2,
         out_specs=[vmem] * 2,
+        scratch_shapes=[pltpu.SemaphoreType.DMA((2,))],
         compiler_params=pltpu.CompilerParams(vmem_limit_bytes=4 * MIB),
         cost_estimate=pl.CostEstimate(flops=20_000_000_000, bytes_accessed=1, transcendentals=0),
-        name="select",
-    )(*msgs[::-1], picks, values)
-    other, picked, kinds = lax.optimization_barrier((other, picked, kinds))
+        name="tables",
+    )(in_hbm(packed), in_hbm(reals))
     density, smooth, fields = pl.pallas_call(
         functools.partial(field_kernel, n, rows, side),
         out_shape=[VMEM((rows, side), F32), VMEM((rows, side), F32), VMEM((5 * ring, side), F32)],
@@ -493,6 +485,15 @@
         compiler_params=pltpu.CompilerParams(vmem_limit_bytes=16 * MIB),
         name="fields",
     )(values, along_y, other, packed, reals)
+    picks, smooth = lax.optimization_barrier((picks, smooth))
+    picked, kinds = pl.pallas_call(
+        functools.partial(select_kernel, groups, capacity, rows, depths),
+        out_shape=[VMEM((rows, side), F32), VMEM((24, side), F32)],
+        in_specs=[vmem] * (groups + 2),
+        out_specs=[vmem] * 2,
+        compiler_params=pltpu.CompilerParams(vmem_limit_bytes=4 * MIB),
+        name="select",
+    )(*msgs[::-1], picks, values)
     density, *parts = pl.pallas_call(
         functools.partial(adjoint_kernel, n, rows, side),
         out_shape=[cell] * (1 + n),

time: 31.9 us -> 30.1 us (0.944)
  waiting for transfers between devices: 8.56 us -> 6.72 us
    ppermute x14, waiting for transfers between devices: 8.56 us -> 6.72 us  [swap(): return lax.ppermute(value, axis, [(i, i ^ k) for i in range(size)])]
  transfers between devices with their start and end apart: 14 -> 14, of which waited for: 5 -> 6; matrix products, arithmetic and copies ran while one was open for 0% -> 0% of each run, Pallas kernels for 11% -> 18%
where the time goes in v4:
time: 30.1 us; the launch traced here: 29.9 us
  starting transfers between devices  14.1 us (47%)
  Pallas kernels  8.21 us (27%)
  waiting for transfers between devices  6.72 us (22%)
  between operations  0.72 us (2%)
    ppermute x14, starting transfers between devices, swap(): return lax.ppermute(value, axis, [(i, i ^ k) for i in range(size)])  14.1 us
    ppermute x14, waiting for transfers between devices, swap(): return lax.ppermute(value, axis, [(i, i ^ k) for i in range(size)])  6.72 us
    pallas_call x1, Pallas kernels, local(): pl.pallas_call(functools.partial(field_kernel, n, rows, side), out_shape=...  2 us
    pallas_call x1, Pallas kernels, local(): pl.pallas_call(functools.partial(adjoint_kernel, n, rows, side), out_shap...  1.95 us
    pallas_call x1, Pallas kernels, local(): pl.pallas_call(table_kernel, out_shape=[VMEM(t.shape, t.dtype) for t in (...  1.48 us
    pallas_call x1, Pallas kernels, local(): pl.pallas_call(functools.partial(message_kernel, groups, capacity, rows,...  1.36 us
    pallas_call x1, Pallas kernels, local(): pl.pallas_call(functools.partial(last_kernel, len(pieces)), out_shape=cel...  0.88 us
  transfers between devices with their start and end apart: 14, of which 6 were waited for; matrix products, arithmetic and copies ran while one was open for 0% of the time, Pallas kernels for 18%

profile of v4, /device:TPU:0, one launch (start us, length us, event | category | flops | bytes accessed | tf_op | source)
XLA Modules:
  0.0 29.9 jit_solution(17650258649958265748)
XLA Ops:
  0.6 4.0 %collective-permute-start.5 = (f32[64,512]{1,0:T(8,128)}, f32[64,512]{1,0:T(8,128)S(1)}, u32[]{:S(2)}, u32[]{:S(2)}) collective-permute-start(f32[64,512]{1,0:T(8,128)} %bitcast.8), channel_id=1, source_target_pairs={{0,6},{1,7},{2,4},{3,5},{4,2},{5,3},{6,0},{7,1},{8,14},{9,15},{10,... | collective-permute-start | bytes 393224 | tf_op jit(solution)/shard_map/ppermute | solution.py:423
  4.6 0.5 %collective-permute-start.4 = (f32[64,512]{1,0:T(8,128)}, f32[64,512]{1,0:T(8,128)S(1)}, u32[]{:S(2)}, u32[]{:S(2)}) collective-permute-start(f32[64,512]{1,0:T(8,128)} %bitcast.9), channel_id=1, source_target_pairs={{0,4},{1,5},{2,6},{3,7},{4,0},{5,1},{6,2},{7,3},{8,12},{9,13},{10,... | collective-permute-start | bytes 393224 | tf_op jit(solution)/shard_map/ppermute | solution.py:423
  5.1 0.1 collective-permute-start.3
  5.2 1.4 %messages.1 = (s32[136,128]{1,0:T(8,128)S(1)}, s32[136,128]{1,0:T(8,128)S(1)}, s32[136,128]{1,0:T(8,128)S(1)}, s32[136,128]{1,0:T(8,128)S(1)}, f32[64,512]{1,0:T...) custom-call(s32[512,128]{1,0:T(8,128)} %bitcast.6, f32[64,512]{1,0:T(8,128)} %bitcast.11, ...), custom_call_target="tpu_custom_call" | custom-call | tf_op jit(solution)/shard_map/messages/pallas_call | solution.py:430
  6.6 4.1 %collective-permute-start = (s32[136,128]{1,0:T(8,128)S(1)}, s32[136,128]{1,0:T(8,128)S(1)}, u32[]{:S(2)}, u32[]{:S(2)}) collective-permute-start(s32[136,128]{1,0:T(8,128)S(1)} %get-tuple-element.31), channel_id=1, source_target_pairs={{0,24},{8,16},{16,8},{24,0},{1,25},{9,17},{17,9},{25,1},{2,26},{10... | collective-permute-start | bytes 208904 | tf_op jit(solution)/shard_map/ppermute | solution.py:423
  10.7 0.0 collective-permute-start.1
  10.7 0.0 collective-permute-done.5.refs_3_
  10.7 0.6 %collective-permute-start.2 = (s32[136,128]{1,0:T(8,128)S(1)}, s32[136,128]{1,0:T(8,128)S(1)}, u32[]{:S(2)}, u32[]{:S(2)}) collective-permute-start(s32[136,128]{1,0:T(8,128)S(1)} %get-tuple-element.33), channel_id=1, source_target_pairs={{0,8},{8,0},{16,24},{24,16},{1,9},{9,1},{17,25},{25,17},{2,10},{10... | collective-permute-start | bytes 208904 | tf_op jit(solution)/shard_map/ppermute | solution.py:423
  11.3 0.0 collective-permute-done.4.refs_2_
  11.3 0.0 collective-permute-done.3.refs_1_
  11.4 0.5 %along_y.1.refs_1_ = f32[2,128,512]{2,1,0:T(8,128)S(1)} custom-call(f32[64,512]{1,0:T(8,128)S(1)} %get-tuple-element.36.refs_0_.refs_4_, f32[64,512]{1,0:T(8,128)S(1)} %collective-permute-done.3.refs_1_, f32[64,512]{1,0:T(8,128)S(1)} %collective-permute-done.4.refs_2_, f32[64,512]{1,0:T(8,128)S(1)} %collective-permute-done.5.refs_3_, ...), custom_call_target="tpu_custom_call" | custom-call | tf_op jit(solution)/shard_map/along_y/pallas_call | solution.py:455
  11.8 0.1 collective-permute-start.6
  11.9 1.5 %tables.1 = (bf16[1344,512]{1,0:T(8,128)(2,1)S(1)}, f32[520,256]{1,0:T(8,128)S(1)}) custom-call(bf16[1344,512]{1,0:T(8,128)(2,1)} %constant.7.clone.refs_0_, f32[520,256]{1,0:T(8,128)} %constant.8.clone.refs_1_), custom_call_target="tpu_custom_call" | custom-call | flops 20000000000 | bytes 1 | tf_op jit(solution)/shard_map/tables/pallas_call | solution.py:466
  13.4 0.4 %collective-permute-done.6.refs_2_ = f32[2,128,512]{2,1,0:T(8,128)S(1)} collective-permute-done((f32[2,128,512]{2,1,0:T(8,128)S(1)}, f32[2,128,512]{2,1,0:T(8,128)S(1)}, u32[]{:S(2)}, u32[]{:S(2)}) %collective-permute-start.6) | collective-permute-done | bytes 524320 | tf_op jit(solution)/shard_map/ppermute | solution.py:423
  13.8 2.0 %fields.1 = (f32[64,512]{1,0:T(8,128)S(1)}, f32[64,512]{1,0:T(8,128)S(1)}, f32[400,512]{1,0:T(8,128)S(1)}) custom-call(f32[32,512]{1,0:T(8,128)S(1)} %get-tuple-element.30.refs_0_.refs_5_, f32[2,128,512]{2,1,0:T(8,128)S(1)} %along_y.1.refs_1_, f32[2,128,512]{2,1,0:T(8,128)S(1)} %collective-permute-done.6.refs_2_, ...), custom_call_target="tpu_custom_call" | custom-call | tf_op jit(solution)/shard_map/fields/pallas_call | solution.py:476
  15.8 0.0 collective-permute-done.refs_0_
  15.8 0.3 collective-permute-done.1.refs_1_
  16.1 0.0 collective-permute-done.2.refs_2_
  16.1 0.1 select.1
  16.2 2.0 %adjoint.1 = (f32[64,512]{1,0:T(8,128)}, f32[64,512]{1,0:T(8,128)S(1)}, f32[64,512]{1,0:T(8,128)S(1)}, f32[64,512]{1,0:T(8,128)S(1)}, f32[64,512]{1,0:T(8,128)S(...) custom-call(f32[32,512]{1,0:T(8,128)S(1)} %get-tuple-element.30.refs_0_.refs_, ...), custom_call_target="tpu_custom_call" | custom-call | tf_op jit(solution)/shard_map/adjoint/pallas_call | solution.py:497
  18.2 0.1 collective-permute-start.8
  18.2 0.5 %collective-permute-start.10 = (f32[64,512]{1,0:T(8,128)S(1)}, f32[64,512]{1,0:T(8,128)S(1)}, u32[]{:S(2)}, u32[]{:S(2)}) collective-permute-start(f32[64,512]{1,0:T(8,128)S(1)} %get-tuple-element.54), channel_id=1, source_target_pairs={{0,1},{1,0},{2,3},{3,2},{4,5},{5,4},{6,7},{7,6},{8,9},{9,8},{10,11... | collective-permute-start | bytes 393224 | tf_op jit(solution)/shard_map/ppermute | solution.py:423
  18.7 0.1 collective-permute-start.12
  18.8 0.4 %collective-permute-start.7 = (f32[64,512]{1,0:T(8,128)S(1)}, f32[64,512]{1,0:T(8,128)S(1)}, u32[]{:S(2)}, u32[]{:S(2)}) collective-permute-start(f32[64,512]{1,0:T(8,128)S(1)} %get-tuple-element.50), channel_id=1, source_target_pairs={{0,1},{1,0},{2,3},{3,2},{4,5},{5,4},{6,7},{7,6},{8,9},{9,8},{10,11... | collective-permute-start | bytes 393224 | tf_op jit(solution)/shard_map/ppermute | solution.py:423
  19.3 0.3 %collective-permute-done.8 = f32[64,512]{1,0:T(8,128)S(1)} collective-permute-done((f32[64,512]{1,0:T(8,128)S(1)}, f32[64,512]{1,0:T(8,128)S(1)}, u32[]{:S(2)}, u32[]{:S(2)}) %collective-permute-start.8) | collective-permute-done | bytes 131104 | tf_op jit(solution)/shard_map/ppermute | solution.py:423
  19.6 2.5 %collective-permute-start.9 = (f32[64,512]{1,0:T(8,128)S(1)}, f32[64,512]{1,0:T(8,128)S(1)}, u32[]{:S(2)}, u32[]{:S(2)}) collective-permute-start(f32[64,512]{1,0:T(8,128)S(1)} %add.13), channel_id=1, source_target_pairs={{0,6},{1,7},{2,4},{3,5},{4,2},{5,3},{6,0},{7,1},{8,14},{9,15},{10,... | collective-permute-start | bytes 393224 | tf_op jit(solution)/shard_map/ppermute | solution.py:423
  22.1 0.0 collective-permute-done.10
  22.1 0.6 %collective-permute-start.11 = (f32[64,512]{1,0:T(8,128)S(1)}, f32[64,512]{1,0:T(8,128)S(1)}, u32[]{:S(2)}, u32[]{:S(2)}) collective-permute-start(f32[64,512]{1,0:T(8,128)S(1)} %add.14), channel_id=1, source_target_pairs={{0,4},{1,5},{2,6},{3,7},{4,0},{5,1},{6,2},{7,3},{8,12},{9,13},{10,... | collective-permute-start | bytes 393224 | tf_op jit(solution)/shard_map/ppermute | solution.py:423
  22.7 0.0 collective-permute-done.12
  22.7 0.6 %collective-permute-start.13 = (f32[64,512]{1,0:T(8,128)S(1)}, f32[64,512]{1,0:T(8,128)S(1)}, u32[]{:S(2)}, u32[]{:S(2)}) collective-permute-start(f32[64,512]{1,0:T(8,128)S(1)} %add.15), channel_id=1, source_target_pairs={{0,2},{1,3},{2,0},{3,1},{4,6},{5,7},{6,4},{7,5},{8,10},{9,11},{10,... | collective-permute-start | bytes 393224 | tf_op jit(solution)/shard_map/ppermute | solution.py:423
  23.3 0.0 collective-permute-done.7
  23.4 2.9 %collective-permute-done.9.refs_1_ = f32[64,512]{1,0:T(8,128)S(1)} collective-permute-done((f32[64,512]{1,0:T(8,128)S(1)}, f32[64,512]{1,0:T(8,128)S(1)}, u32[]{:S(2)}, u32[]{:S(2)}) %collective-permute-start.9) | collective-permute-done | bytes 131104 | tf_op jit(solution)/shard_map/ppermute | solution.py:423
  26.2 2.7 %collective-permute-done.11.refs_2_ = f32[64,512]{1,0:T(8,128)S(1)} collective-permute-done((f32[64,512]{1,0:T(8,128)S(1)}, f32[64,512]{1,0:T(8,128)S(1)}, u32[]{:S(2)}, u32[]{:S(2)}) %collective-permute-start.11) | collective-permute-done | bytes 131104 | tf_op jit(solution)/shard_map/ppermute | solution.py:423
  28.9 0.1 collective-permute-done.13.refs_3_
  29.0 0.9 %sum_and_rows.1 = f32[64,512]{1,0:T(8,128)} custom-call(f32[64,512]{1,0:T(8,128)S(1)} %add.12.refs_0_, f32[64,512]{1,0:T(8,128)S(1)} %collective-permute-done.9.refs_1_, f32[64,512]{1,0:T(8,128)S(1)} %collective-permute-done.11.refs_2_, f32[64,512]{1,0:T(8,128)S(1)} %collective-permute-done.13.refs_3_, f32[64,512]{1,0:T(8,128)S(1)} %get-tuple-element.36.refs_0_.refs_4_, ...), custom_call_target="tpu_custom_call" | custom-call | tf_op jit(solution)/shard_map/sum_and_rows/pallas_call | solution.py:514
  (4 shorter events, 0.1 us)
Async XLA Ops:
  0.6 10.0 %collective-permute-start.5 = (f32[64,512]{1,0:T(8,128)}, f32[64,512]{1,0:T(8,128)S(1)}, u32[]{:S(2)}, u32[]{:S(2)}) collective-permute-start(f32[64,512]{1,0:T(8,128)} %bitcast.8), channel_id=1, source_target_pairs={{0,6},{1,7},{2,4},{3,5},{4,2},{5,3},{6,0},{7,1},{8,14},{9,15},{10,... | collective-permute-start | bytes 393224 | tf_op jit(solution)/shard_map/ppermute | solution.py:423
  4.6 6.7 %collective-permute-start.4 = (f32[64,512]{1,0:T(8,128)}, f32[64,512]{1,0:T(8,128)S(1)}, u32[]{:S(2)}, u32[]{:S(2)}) collective-permute-start(f32[64,512]{1,0:T(8,128)} %bitcast.9), channel_id=1, source_target_pairs={{0,4},{1,5},{2,6},{3,7},{4,0},{5,1},{6,2},{7,3},{8,12},{9,13},{10,... | collective-permute-start | bytes 393224 | tf_op jit(solution)/shard_map/ppermute | solution.py:423
  5.1 6.3 %collective-permute-start.3 = (f32[64,512]{1,0:T(8,128)}, f32[64,512]{1,0:T(8,128)S(1)}, u32[]{:S(2)}, u32[]{:S(2)}) collective-permute-start(f32[64,512]{1,0:T(8,128)} %bitcast.10), channel_id=1, source_target_pairs={{0,2},{1,3},{2,0},{3,1},{4,6},{5,7},{6,4},{7,5},{8,10},{9,11},{10,... | collective-permute-start | bytes 393224 | tf_op jit(solution)/shard_map/ppermute | solution.py:423
  6.6 9.2 %collective-permute-start = (s32[136,128]{1,0:T(8,128)S(1)}, s32[136,128]{1,0:T(8,128)S(1)}, u32[]{:S(2)}, u32[]{:S(2)}) collective-permute-start(s32[136,128]{1,0:T(8,128)S(1)} %get-tuple-element.31), channel_id=1, source_target_pairs={{0,24},{8,16},{16,8},{24,0},{1,25},{9,17},{17,9},{25,1},{2,26},{10... | collective-permute-start | bytes 208904 | tf_op jit(solution)/shard_map/ppermute | solution.py:423
  10.7 5.5 %collective-permute-start.1 = (s32[136,128]{1,0:T(8,128)S(1)}, s32[136,128]{1,0:T(8,128)S(1)}, u32[]{:S(2)}, u32[]{:S(2)}) collective-permute-start(s32[136,128]{1,0:T(8,128)S(1)} %get-tuple-element.32), channel_id=1, source_target_pairs={{0,16},{8,24},{16,0},{24,8},{1,17},{9,25},{17,1},{25,9},{2,18},{10... | collective-permute-start | bytes 208904 | tf_op jit(solution)/shard_map/ppermute | solution.py:423
  10.7 5.4 %collective-permute-start.2 = (s32[136,128]{1,0:T(8,128)S(1)}, s32[136,128]{1,0:T(8,128)S(1)}, u32[]{:S(2)}, u32[]{:S(2)}) collective-permute-start(s32[136,128]{1,0:T(8,128)S(1)} %get-tuple-element.33), channel_id=1, source_target_pairs={{0,8},{8,0},{16,24},{24,16},{1,9},{9,1},{17,25},{25,17},{2,10},{10... | collective-permute-start | bytes 208904 | tf_op jit(solution)/shard_map/ppermute | solution.py:423
  11.8 2.0 %collective-permute-start.6 = (f32[2,128,512]{2,1,0:T(8,128)S(1)}, f32[2,128,512]{2,1,0:T(8,128)S(1)}, u32[]{:S(2)}, u32[]{:S(2)}) collective-permute-start(f32[2,128,512]{2,1,0:T(8,128)S(1)} %along_y.1.refs_1_), channel_id=1, source_target_pairs={{0,1},{1,0},{2,3},{3,2},{4,5},{5,4},{6,7},{7,6},{8,9},{9,8},{10,11... | collective-permute-start | bytes 1572872 | tf_op jit(solution)/shard_map/ppermute | solution.py:423
  18.2 1.4 %collective-permute-start.8 = (f32[64,512]{1,0:T(8,128)S(1)}, f32[64,512]{1,0:T(8,128)S(1)}, u32[]{:S(2)}, u32[]{:S(2)}) collective-permute-start(f32[64,512]{1,0:T(8,128)S(1)} %get-tuple-element.52), channel_id=1, source_target_pairs={{0,1},{1,0},{2,3},{3,2},{4,5},{5,4},{6,7},{7,6},{8,9},{9,8},{10,11... | collective-permute-start | bytes 393224 | tf_op jit(solution)/shard_map/ppermute | solution.py:423
  18.2 3.9 %collective-permute-start.10 = (f32[64,512]{1,0:T(8,128)S(1)}, f32[64,512]{1,0:T(8,128)S(1)}, u32[]{:S(2)}, u32[]{:S(2)}) collective-permute-start(f32[64,512]{1,0:T(8,128)S(1)} %get-tuple-element.54), channel_id=1, source_target_pairs={{0,1},{1,0},{2,3},{3,2},{4,5},{5,4},{6,7},{7,6},{8,9},{9,8},{10,11... | collective-permute-start | bytes 393224 | tf_op jit(solution)/shard_map/ppermute | solution.py:423
  18.7 4.0 %collective-permute-start.12 = (f32[64,512]{1,0:T(8,128)S(1)}, f32[64,512]{1,0:T(8,128)S(1)}, u32[]{:S(2)}, u32[]{:S(2)}) collective-permute-start(f32[64,512]{1,0:T(8,128)S(1)} %get-tuple-element.56), channel_id=1, source_target_pairs={{0,1},{1,0},{2,3},{3,2},{4,5},{5,4},{6,7},{7,6},{8,9},{9,8},{10,11... | collective-permute-start | bytes 393224 | tf_op jit(solution)/shard_map/ppermute | solution.py:423
  18.8 4.5 %collective-permute-start.7 = (f32[64,512]{1,0:T(8,128)S(1)}, f32[64,512]{1,0:T(8,128)S(1)}, u32[]{:S(2)}, u32[]{:S(2)}) collective-permute-start(f32[64,512]{1,0:T(8,128)S(1)} %get-tuple-element.50), channel_id=1, source_target_pairs={{0,1},{1,0},{2,3},{3,2},{4,5},{5,4},{6,7},{7,6},{8,9},{9,8},{10,11... | collective-permute-start | bytes 393224 | tf_op jit(solution)/shard_map/ppermute | solution.py:423
  19.6 6.6 %collective-permute-start.9 = (f32[64,512]{1,0:T(8,128)S(1)}, f32[64,512]{1,0:T(8,128)S(1)}, u32[]{:S(2)}, u32[]{:S(2)}) collective-permute-start(f32[64,512]{1,0:T(8,128)S(1)} %add.13), channel_id=1, source_target_pairs={{0,6},{1,7},{2,4},{3,5},{4,2},{5,3},{6,0},{7,1},{8,14},{9,15},{10,... | collective-permute-start | bytes 393224 | tf_op jit(solution)/shard_map/ppermute | solution.py:423
  22.1 6.8 %collective-permute-start.11 = (f32[64,512]{1,0:T(8,128)S(1)}, f32[64,512]{1,0:T(8,128)S(1)}, u32[]{:S(2)}, u32[]{:S(2)}) collective-permute-start(f32[64,512]{1,0:T(8,128)S(1)} %add.14), channel_id=1, source_target_pairs={{0,4},{1,5},{2,6},{3,7},{4,0},{5,1},{6,2},{7,3},{8,12},{9,13},{10,... | collective-permute-start | bytes 393224 | tf_op jit(solution)/shard_map/ppermute | solution.py:423
  22.7 6.3 %collective-permute-start.13 = (f32[64,512]{1,0:T(8,128)S(1)}, f32[64,512]{1,0:T(8,128)S(1)}, u32[]{:S(2)}, u32[]{:S(2)}) collective-permute-start(f32[64,512]{1,0:T(8,128)S(1)} %add.15), channel_id=1, source_target_pairs={{0,2},{1,3},{2,0},{3,1},{4,6},{5,7},{6,4},{7,5},{8,10},{9,11},{10,... | collective-permute-start | bytes 393224 | tf_op jit(solution)/shard_map/ppermute | solution.py:423

commit v5 on v4

--- a/solution.py
+++ b/solution.py
@@ -51,7 +51,10 @@
     ring = np.concatenate([np.arange(rows + 1), np.zeros(PAD - 2, int), [side - 1]])
     used = np.ones(rows + PAD)
     used[rows + 1 : rows + PAD - 1] = 0.0
-    views = np.concatenate([(basis(ring) * used).T, (slope(ring) * used).T])
+    plain_rows, slope_rows = (basis(ring) * used).T, (slope(ring) * used).T
+    twice = np.repeat(wave.reshape(2, 1, quarter), 2, axis=1).reshape(-1) ** 2
+    views = np.concatenate([plain_rows, slope_rows, plain_rows * twice, slope_rows * twice])
+    up = np.concatenate([plain_rows, slope_rows]).T
     wave_sq = wave[:, None] ** 2 + wave[None, :] ** 2
     inverse = np.where(wave_sq > 0, 1.0 / np.where(wave_sq > 0, wave_sq, 1.0), 0.0)
     weight = np.where(freqs == 0, 1.0, 2.0)
@@ -61,7 +64,7 @@
     for table in (even, odd, even.T, odd.T):
         sections.append(np.concatenate(split_np(np.ascontiguousarray(table)), axis=1))
     sections.extend(split_np(views))
-    up_h, up_l = split_np(np.ascontiguousarray(views.T))
+    up_h, up_l = split_np(np.ascontiguousarray(up))
     lift = np.concatenate([up_h, up_h, up_l], axis=1)
     sections.append(np.concatenate([lift, np.zeros((side, side - lift.shape[1]), lift.dtype)], axis=1))
     waves = np.zeros((8, half))
@@ -69,7 +72,7 @@
     return (
         np.concatenate(sections[2:4]),
         np.concatenate(sections[:2] + sections[4:]),
-        np.concatenate([gain, inverse, waves]).astype(np.float32),
+        np.concatenate([gain, gain * inverse, waves]).astype(np.float32),
     )
 
 
@@ -81,7 +84,7 @@
         self.backs = backs
         self.packed = packed
         self.reals = reals
-        self.lift_at = 2 * half + 4 * ring
+        self.lift_at = 2 * half + 8 * ring
 
     def fwd(self, par):
         half, at = self.half, par * self.half
@@ -92,7 +95,7 @@
         return self.backs[at : at + half, :half], self.backs[at : at + half, half:]
 
     def views(self):
-        at, count = 2 * self.half, 2 * self.ring
+        at, count = 2 * self.half, 4 * self.ring
         return self.packed[at : at + count, :], self.packed[at + count : at + 2 * count, :]
 
     def lift(self, start, count):
@@ -102,7 +105,7 @@
         q = self.half // 2
         return self.reals[par * q : (par + 1) * q, ypar * q : (ypar + 1) * q]
 
-    def inverse(self, par, ypar):
+    def gain_phi(self, par, ypar):
         q, half = self.half // 2, self.half
         return self.reals[half + par * q : half + (par + 1) * q, ypar * q : (ypar + 1) * q]
 
@@ -199,21 +202,19 @@
         for ypar in range(2):
             cols = slice(ypar * half, (ypar + 1) * half)
             x = mm3(tabs.fwd(par), (yh[par, :, cols], yl[par, :, cols]))
-            g = tabs.gain(par, ypar)
-            inv = tabs.inverse(par, ypar)
+            g = tabs.gain_phi(par, ypar)
             for i in range(2):
                 for j in range(2):
-                    base = x[i * q : (i + 1) * q, j * q : (j + 1) * q] * g
-                    phi = base * inv
+                    phi = x[i * q : (i + 1) * q, j * q : (j + 1) * q] * g
                     rs = slice(par * half + i * q, par * half + (i + 1) * q)
                     c0 = ypar * half + j * q
-                    zh[rs, c0 : c0 + q], zl[rs, c0 : c0 + q] = split(base)
-                    zh[rs, side + c0 : side + c0 + q], zl[rs, side + c0 : side + c0 + q] = split(phi)
+                    zh[rs, c0 : c0 + q], zl[rs, c0 : c0 + q] = split(phi)
 
     w = mm3(tabs.views(), (zh[...], zl[...]))
     ky = tabs.waves()
-    base, base_x = w[:ring, :side], w[ring:, :side]
-    phi, phi_x = w[:ring, side:], w[ring:, side:]
+    ky_sq = jnp.concatenate([ky[0] * ky[0]] * 2 + [ky[1] * ky[1]] * 2, axis=1)
+    phi, phi_x, base, base_x = [w[i * ring : (i + 1) * ring] for i in range(4)]
+    base, base_x = base + ky_sq * phi, base_x + ky_sq * phi_x
     stack = jnp.concatenate([base, phi_x, slope_lanes(phi, ky, 1.0), base_x, slope_lanes(base, ky, 1.0)], axis=0)
     sh, sl = split(stack)
     e = mm3((sh[:, :half], sl[:, :half]), tabs.fwd(0))
@@ -288,10 +289,10 @@
             x = mm(tabs.lift(rs.start, q), pile3)
             for ypar in range(2):
                 g = tabs.gain(par, ypar)
-                inv = tabs.inverse(par, ypar)
+                g_phi = tabs.gain_phi(par, ypar)
                 for j in range(2):
                     c0 = ypar * half + j * q
-                    d = g * (x[:, c0 : c0 + q] + inv * x[:, side + c0 : side + c0 + q])
+                    d = g * x[:, c0 : c0 + q] + g_phi * x[:, side + c0 : side + c0 + q]
                     yh[par, i * q : (i + 1) * q, c0 : c0 + q], yl[par, i * q : (i + 1) * q, c0 : c0 + q] = split(d)
     e = mm3(tabs.back(0), (yh[0], yl[0]))
     o = mm3(tabs.back(1), (yh[1], yl[1]))
@@ -351,8 +352,13 @@
         copy.wait()
 
 
+def arrival_order(groups):
+    first = (2, 3, 1)
+    return list(first) + [k for k in range(groups) if k not in first]
+
+
 def select_kernel(groups, capacity, rows, depths, *refs):
-    msgs = refs[:groups][::-1]
+    msgs = dict(zip(arrival_order(groups), refs[:groups]))
     picks, values, counts_out, kinds_out = refs[groups:]
     side = counts_out.shape[1]
 
@@ -480,7 +486,7 @@
         out_specs=[vmem] * 3,
         scratch_shapes=[
             *[VMEM((2, half, side), BF16)] * 2,
-            *[VMEM((side, 2 * side), BF16)] * 2,
+            *[VMEM((side, side), BF16)] * 2,
         ],
         compiler_params=pltpu.CompilerParams(vmem_limit_bytes=16 * MIB),
         name="fields",
@@ -493,7 +499,7 @@
         out_specs=[vmem] * 2,
         compiler_params=pltpu.CompilerParams(vmem_limit_bytes=4 * MIB),
         name="select",
-    )(*msgs[::-1], picks, values)
+    )(*[msgs[k] for k in arrival_order(groups)], picks, values)
     density, *parts = pl.pallas_call(
         functools.partial(adjoint_kernel, n, rows, side),
         out_shape=[cell] * (1 + n),

time: 30.1 us -> 30 us (level)
  transfers between devices with their start and end apart: 14 -> 14, of which waited for: 6 -> 8; matrix products, arithmetic and copies ran while one was open for 0% -> 0% of each run, Pallas kernels for 18% -> 17%
where the time goes in v5:
time: 30 us; the launch traced here: 29.8 us
  starting transfers between devices  14.1 us (47%)
  Pallas kernels  8.08 us (27%)
  waiting for transfers between devices  6.87 us (23%)
  between operations  0.72 us (2%)
    ppermute x14, starting transfers between devices, swap(): return lax.ppermute(value, axis, [(i, i ^ k) for i in range(size)])  14.1 us
    ppermute x14, waiting for transfers between devices, swap(): return lax.ppermute(value, axis, [(i, i ^ k) for i in range(size)])  6.87 us
    pallas_call x1, Pallas kernels, local(): pl.pallas_call(functools.partial(adjoint_kernel, n, rows, side), out_shap...  1.96 us
    pallas_call x1, Pallas kernels, local(): pl.pallas_call(functools.partial(field_kernel, n, rows, side), out_shape=...  1.77 us
    pallas_call x1, Pallas kernels, local(): pl.pallas_call(table_kernel, out_shape=[VMEM(t.shape, t.dtype) for t in (...  1.58 us
    pallas_call x1, Pallas kernels, local(): pl.pallas_call(functools.partial(message_kernel, groups, capacity, rows,...  1.36 us
    pallas_call x1, Pallas kernels, local(): pl.pallas_call(functools.partial(last_kernel, len(pieces)), out_shape=cel...  0.88 us
  transfers between devices with their start and end apart: 14, of which 8 were waited for; matrix products, arithmetic and copies ran while one was open for 0% of the time, Pallas kernels for 17%

profile of v5, /device:TPU:0, one launch (start us, length us, event | category | flops | bytes accessed | tf_op | source)
XLA Modules:
  0.0 29.8 jit_solution(877859192191986293)
XLA Ops:
  0.6 4.0 %collective-permute-start.5 = (f32[64,512]{1,0:T(8,128)}, f32[64,512]{1,0:T(8,128)S(1)}, u32[]{:S(2)}, u32[]{:S(2)}) collective-permute-start(f32[64,512]{1,0:T(8,128)} %bitcast.8), channel_id=1, source_target_pairs={{0,6},{1,7},{2,4},{3,5},{4,2},{5,3},{6,0},{7,1},{8,14},{9,15},{10,... | collective-permute-start | bytes 393224 | tf_op jit(solution)/shard_map/ppermute | solution.py:429
  4.6 0.5 %collective-permute-start.4 = (f32[64,512]{1,0:T(8,128)}, f32[64,512]{1,0:T(8,128)S(1)}, u32[]{:S(2)}, u32[]{:S(2)}) collective-permute-start(f32[64,512]{1,0:T(8,128)} %bitcast.9), channel_id=1, source_target_pairs={{0,4},{1,5},{2,6},{3,7},{4,0},{5,1},{6,2},{7,3},{8,12},{9,13},{10,... | collective-permute-start | bytes 393224 | tf_op jit(solution)/shard_map/ppermute | solution.py:429
  5.1 0.1 collective-permute-start.3
  5.2 1.4 %messages.1 = (s32[136,128]{1,0:T(8,128)S(1)}, s32[136,128]{1,0:T(8,128)S(1)}, s32[136,128]{1,0:T(8,128)S(1)}, s32[136,128]{1,0:T(8,128)S(1)}, f32[64,512]{1,0:T...) custom-call(s32[512,128]{1,0:T(8,128)} %bitcast.6, f32[64,512]{1,0:T(8,128)} %bitcast.11, ...), custom_call_target="tpu_custom_call" | custom-call | tf_op jit(solution)/shard_map/messages/pallas_call | solution.py:436
  6.6 3.1 %collective-permute-start = (s32[136,128]{1,0:T(8,128)S(1)}, s32[136,128]{1,0:T(8,128)S(1)}, u32[]{:S(2)}, u32[]{:S(2)}) collective-permute-start(s32[136,128]{1,0:T(8,128)S(1)} %get-tuple-element.31), channel_id=1, source_target_pairs={{0,16},{8,24},{16,0},{24,8},{1,17},{9,25},{17,1},{25,9},{2,18},{10... | collective-permute-start | bytes 208904 | tf_op jit(solution)/shard_map/ppermute | solution.py:429
  9.7 1.3 %collective-permute-start.1 = (s32[136,128]{1,0:T(8,128)S(1)}, s32[136,128]{1,0:T(8,128)S(1)}, u32[]{:S(2)}, u32[]{:S(2)}) collective-permute-start(s32[136,128]{1,0:T(8,128)S(1)} %get-tuple-element.32), channel_id=1, source_target_pairs={{0,24},{8,16},{16,8},{24,0},{1,25},{9,17},{17,9},{25,1},{2,26},{10... | collective-permute-start | bytes 208904 | tf_op jit(solution)/shard_map/ppermute | solution.py:429
  11.0 0.0 collective-permute-done.5.refs_3_
  11.0 0.2 collective-permute-start.2
  11.2 0.0 collective-permute-done.4.refs_2_
  11.2 0.1 collective-permute-done.3.refs_1_
  11.4 0.5 %along_y.1.refs_1_ = f32[2,128,512]{2,1,0:T(8,128)S(1)} custom-call(f32[64,512]{1,0:T(8,128)S(1)} %get-tuple-element.36.refs_0_.refs_4_, f32[64,512]{1,0:T(8,128)S(1)} %collective-permute-done.3.refs_1_, f32[64,512]{1,0:T(8,128)S(1)} %collective-permute-done.4.refs_2_, f32[64,512]{1,0:T(8,128)S(1)} %collective-permute-done.5.refs_3_, ...), custom_call_target="tpu_custom_call" | custom-call | tf_op jit(solution)/shard_map/along_y/pallas_call | solution.py:461
  11.8 0.1 collective-permute-start.6
  11.9 1.6 %tables.1 = (bf16[1664,512]{1,0:T(8,128)(2,1)S(1)}, f32[520,256]{1,0:T(8,128)S(1)}) custom-call(bf16[1664,512]{1,0:T(8,128)(2,1)} %constant.7.clone.refs_0_, f32[520,256]{1,0:T(8,128)} %constant.8.clone.refs_1_), custom_call_target="tpu_custom_call" | custom-call | flops 20000000000 | bytes 1 | tf_op jit(solution)/shard_map/tables/pallas_call | solution.py:472
  13.5 0.3 %collective-permute-done.6.refs_2_ = f32[2,128,512]{2,1,0:T(8,128)S(1)} collective-permute-done((f32[2,128,512]{2,1,0:T(8,128)S(1)}, f32[2,128,512]{2,1,0:T(8,128)S(1)}, u32[]{:S(2)}, u32[]{:S(2)}) %collective-permute-start.6) | collective-permute-done | bytes 524320 | tf_op jit(solution)/shard_map/ppermute | solution.py:429
  13.8 1.8 %fields.1 = (f32[64,512]{1,0:T(8,128)S(1)}, f32[64,512]{1,0:T(8,128)S(1)}, f32[400,512]{1,0:T(8,128)S(1)}) custom-call(f32[32,512]{1,0:T(8,128)S(1)} %get-tuple-element.30.refs_0_.refs_5_, f32[2,128,512]{2,1,0:T(8,128)S(1)} %along_y.1.refs_1_, f32[2,128,512]{2,1,0:T(8,128)S(1)} %collective-permute-done.6.refs_2_, ...), custom_call_target="tpu_custom_call" | custom-call | tf_op jit(solution)/shard_map/fields/pallas_call | solution.py:482
  15.6 0.0 collective-permute-done.refs_0_
  15.6 0.3 collective-permute-done.1.refs_1_
  15.9 0.2 collective-permute-done.2.refs_2_
  16.1 0.1 select.1
  16.1 2.0 %adjoint.1 = (f32[64,512]{1,0:T(8,128)}, f32[64,512]{1,0:T(8,128)S(1)}, f32[64,512]{1,0:T(8,128)S(1)}, f32[64,512]{1,0:T(8,128)S(1)}, f32[64,512]{1,0:T(8,128)S(...) custom-call(f32[32,512]{1,0:T(8,128)S(1)} %get-tuple-element.30.refs_0_.refs_, ...), custom_call_target="tpu_custom_call" | custom-call | tf_op jit(solution)/shard_map/adjoint/pallas_call | solution.py:503
  18.1 0.1 collective-permute-start.8
  18.2 0.5 %collective-permute-start.10 = (f32[64,512]{1,0:T(8,128)S(1)}, f32[64,512]{1,0:T(8,128)S(1)}, u32[]{:S(2)}, u32[]{:S(2)}) collective-permute-start(f32[64,512]{1,0:T(8,128)S(1)} %get-tuple-element.54), channel_id=1, source_target_pairs={{0,1},{1,0},{2,3},{3,2},{4,5},{5,4},{6,7},{7,6},{8,9},{9,8},{10,11... | collective-permute-start | bytes 393224 | tf_op jit(solution)/shard_map/ppermute | solution.py:429
  18.7 0.1 collective-permute-start.12
  18.8 0.4 %collective-permute-start.7 = (f32[64,512]{1,0:T(8,128)S(1)}, f32[64,512]{1,0:T(8,128)S(1)}, u32[]{:S(2)}, u32[]{:S(2)}) collective-permute-start(f32[64,512]{1,0:T(8,128)S(1)} %get-tuple-element.50), channel_id=1, source_target_pairs={{0,1},{1,0},{2,3},{3,2},{4,5},{5,4},{6,7},{7,6},{8,9},{9,8},{10,11... | collective-permute-start | bytes 393224 | tf_op jit(solution)/shard_map/ppermute | solution.py:429
  19.2 0.3 %collective-permute-done.8 = f32[64,512]{1,0:T(8,128)S(1)} collective-permute-done((f32[64,512]{1,0:T(8,128)S(1)}, f32[64,512]{1,0:T(8,128)S(1)}, u32[]{:S(2)}, u32[]{:S(2)}) %collective-permute-start.8) | collective-permute-done | bytes 131104 | tf_op jit(solution)/shard_map/ppermute | solution.py:429
  19.5 2.5 %collective-permute-start.9 = (f32[64,512]{1,0:T(8,128)S(1)}, f32[64,512]{1,0:T(8,128)S(1)}, u32[]{:S(2)}, u32[]{:S(2)}) collective-permute-start(f32[64,512]{1,0:T(8,128)S(1)} %add.13), channel_id=1, source_target_pairs={{0,6},{1,7},{2,4},{3,5},{4,2},{5,3},{6,0},{7,1},{8,14},{9,15},{10,... | collective-permute-start | bytes 393224 | tf_op jit(solution)/shard_map/ppermute | solution.py:429
  22.1 0.0 collective-permute-done.10
  22.1 0.6 %collective-permute-start.11 = (f32[64,512]{1,0:T(8,128)S(1)}, f32[64,512]{1,0:T(8,128)S(1)}, u32[]{:S(2)}, u32[]{:S(2)}) collective-permute-start(f32[64,512]{1,0:T(8,128)S(1)} %add.14), channel_id=1, source_target_pairs={{0,4},{1,5},{2,6},{3,7},{4,0},{5,1},{6,2},{7,3},{8,12},{9,13},{10,... | collective-permute-start | bytes 393224 | tf_op jit(solution)/shard_map/ppermute | solution.py:429
  22.7 0.0 collective-permute-done.12
  22.7 0.6 %collective-permute-start.13 = (f32[64,512]{1,0:T(8,128)S(1)}, f32[64,512]{1,0:T(8,128)S(1)}, u32[]{:S(2)}, u32[]{:S(2)}) collective-permute-start(f32[64,512]{1,0:T(8,128)S(1)} %add.15), channel_id=1, source_target_pairs={{0,2},{1,3},{2,0},{3,1},{4,6},{5,7},{6,4},{7,5},{8,10},{9,11},{10,... | collective-permute-start | bytes 393224 | tf_op jit(solution)/shard_map/ppermute | solution.py:429
  23.3 0.0 collective-permute-done.7
  23.3 2.9 %collective-permute-done.9.refs_1_ = f32[64,512]{1,0:T(8,128)S(1)} collective-permute-done((f32[64,512]{1,0:T(8,128)S(1)}, f32[64,512]{1,0:T(8,128)S(1)}, u32[]{:S(2)}, u32[]{:S(2)}) %collective-permute-start.9) | collective-permute-done | bytes 131104 | tf_op jit(solution)/shard_map/ppermute | solution.py:429
  26.2 2.7 %collective-permute-done.11.refs_2_ = f32[64,512]{1,0:T(8,128)S(1)} collective-permute-done((f32[64,512]{1,0:T(8,128)S(1)}, f32[64,512]{1,0:T(8,128)S(1)}, u32[]{:S(2)}, u32[]{:S(2)}) %collective-permute-start.11) | collective-permute-done | bytes 131104 | tf_op jit(solution)/shard_map/ppermute | solution.py:429
  28.9 0.1 collective-permute-done.13.refs_3_
  28.9 0.9 %sum_and_rows.1 = f32[64,512]{1,0:T(8,128)} custom-call(f32[64,512]{1,0:T(8,128)S(1)} %add.12.refs_0_, f32[64,512]{1,0:T(8,128)S(1)} %collective-permute-done.9.refs_1_, f32[64,512]{1,0:T(8,128)S(1)} %collective-permute-done.11.refs_2_, f32[64,512]{1,0:T(8,128)S(1)} %collective-permute-done.13.refs_3_, f32[64,512]{1,0:T(8,128)S(1)} %get-tuple-element.36.refs_0_.refs_4_, ...), custom_call_target="tpu_custom_call" | custom-call | tf_op jit(solution)/shard_map/sum_and_rows/pallas_call | solution.py:520
  (4 shorter events, 0.1 us)
Async XLA Ops:
  0.6 10.4 %collective-permute-start.5 = (f32[64,512]{1,0:T(8,128)}, f32[64,512]{1,0:T(8,128)S(1)}, u32[]{:S(2)}, u32[]{:S(2)}) collective-permute-start(f32[64,512]{1,0:T(8,128)} %bitcast.8), channel_id=1, source_target_pairs={{0,6},{1,7},{2,4},{3,5},{4,2},{5,3},{6,0},{7,1},{8,14},{9,15},{10,... | collective-permute-start | bytes 393224 | tf_op jit(solution)/shard_map/ppermute | solution.py:429
  4.6 6.6 %collective-permute-start.4 = (f32[64,512]{1,0:T(8,128)}, f32[64,512]{1,0:T(8,128)S(1)}, u32[]{:S(2)}, u32[]{:S(2)}) collective-permute-start(f32[64,512]{1,0:T(8,128)} %bitcast.9), channel_id=1, source_target_pairs={{0,4},{1,5},{2,6},{3,7},{4,0},{5,1},{6,2},{7,3},{8,12},{9,13},{10,... | collective-permute-start | bytes 393224 | tf_op jit(solution)/shard_map/ppermute | solution.py:429
  5.1 6.3 %collective-permute-start.3 = (f32[64,512]{1,0:T(8,128)}, f32[64,512]{1,0:T(8,128)S(1)}, u32[]{:S(2)}, u32[]{:S(2)}) collective-permute-start(f32[64,512]{1,0:T(8,128)} %bitcast.10), channel_id=1, source_target_pairs={{0,2},{1,3},{2,0},{3,1},{4,6},{5,7},{6,4},{7,5},{8,10},{9,11},{10,... | collective-permute-start | bytes 393224 | tf_op jit(solution)/shard_map/ppermute | solution.py:429
  6.6 9.0 %collective-permute-start = (s32[136,128]{1,0:T(8,128)S(1)}, s32[136,128]{1,0:T(8,128)S(1)}, u32[]{:S(2)}, u32[]{:S(2)}) collective-permute-start(s32[136,128]{1,0:T(8,128)S(1)} %get-tuple-element.31), channel_id=1, source_target_pairs={{0,16},{8,24},{16,0},{24,8},{1,17},{9,25},{17,1},{25,9},{2,18},{10... | collective-permute-start | bytes 208904 | tf_op jit(solution)/shard_map/ppermute | solution.py:429
  9.7 6.2 %collective-permute-start.1 = (s32[136,128]{1,0:T(8,128)S(1)}, s32[136,128]{1,0:T(8,128)S(1)}, u32[]{:S(2)}, u32[]{:S(2)}) collective-permute-start(s32[136,128]{1,0:T(8,128)S(1)} %get-tuple-element.32), channel_id=1, source_target_pairs={{0,24},{8,16},{16,8},{24,0},{1,25},{9,17},{17,9},{25,1},{2,26},{10... | collective-permute-start | bytes 208904 | tf_op jit(solution)/shard_map/ppermute | solution.py:429
  11.0 5.1 %collective-permute-start.2 = (s32[136,128]{1,0:T(8,128)S(1)}, s32[136,128]{1,0:T(8,128)S(1)}, u32[]{:S(2)}, u32[]{:S(2)}) collective-permute-start(s32[136,128]{1,0:T(8,128)S(1)} %get-tuple-element.33), channel_id=1, source_target_pairs={{0,8},{8,0},{16,24},{24,16},{1,9},{9,1},{17,25},{25,17},{2,10},{10... | collective-permute-start | bytes 208904 | tf_op jit(solution)/shard_map/ppermute | solution.py:429
  11.8 2.0 %collective-permute-start.6 = (f32[2,128,512]{2,1,0:T(8,128)S(1)}, f32[2,128,512]{2,1,0:T(8,128)S(1)}, u32[]{:S(2)}, u32[]{:S(2)}) collective-permute-start(f32[2,128,512]{2,1,0:T(8,128)S(1)} %along_y.1.refs_1_), channel_id=1, source_target_pairs={{0,1},{1,0},{2,3},{3,2},{4,5},{5,4},{6,7},{7,6},{8,9},{9,8},{10,11... | collective-permute-start | bytes 1572872 | tf_op jit(solution)/shard_map/ppermute | solution.py:429
  18.1 1.4 %collective-permute-start.8 = (f32[64,512]{1,0:T(8,128)S(1)}, f32[64,512]{1,0:T(8,128)S(1)}, u32[]{:S(2)}, u32[]{:S(2)}) collective-permute-start(f32[64,512]{1,0:T(8,128)S(1)} %get-tuple-element.52), channel_id=1, source_target_pairs={{0,1},{1,0},{2,3},{3,2},{4,5},{5,4},{6,7},{7,6},{8,9},{9,8},{10,11... | collective-permute-start | bytes 393224 | tf_op jit(solution)/shard_map/ppermute | solution.py:429
  18.2 3.9 %collective-permute-start.10 = (f32[64,512]{1,0:T(8,128)S(1)}, f32[64,512]{1,0:T(8,128)S(1)}, u32[]{:S(2)}, u32[]{:S(2)}) collective-permute-start(f32[64,512]{1,0:T(8,128)S(1)} %get-tuple-element.54), channel_id=1, source_target_pairs={{0,1},{1,0},{2,3},{3,2},{4,5},{5,4},{6,7},{7,6},{8,9},{9,8},{10,11... | collective-permute-start | bytes 393224 | tf_op jit(solution)/shard_map/ppermute | solution.py:429
  18.7 4.0 %collective-permute-start.12 = (f32[64,512]{1,0:T(8,128)S(1)}, f32[64,512]{1,0:T(8,128)S(1)}, u32[]{:S(2)}, u32[]{:S(2)}) collective-permute-start(f32[64,512]{1,0:T(8,128)S(1)} %get-tuple-element.56), channel_id=1, source_target_pairs={{0,1},{1,0},{2,3},{3,2},{4,5},{5,4},{6,7},{7,6},{8,9},{9,8},{10,11... | collective-permute-start | bytes 393224 | tf_op jit(solution)/shard_map/ppermute | solution.py:429
  18.8 4.5 %collective-permute-start.7 = (f32[64,512]{1,0:T(8,128)S(1)}, f32[64,512]{1,0:T(8,128)S(1)}, u32[]{:S(2)}, u32[]{:S(2)}) collective-permute-start(f32[64,512]{1,0:T(8,128)S(1)} %get-tuple-element.50), channel_id=1, source_target_pairs={{0,1},{1,0},{2,3},{3,2},{4,5},{5,4},{6,7},{7,6},{8,9},{9,8},{10,11... | collective-permute-start | bytes 393224 | tf_op jit(solution)/shard_map/ppermute | solution.py:429
  19.5 6.6 %collective-permute-start.9 = (f32[64,512]{1,0:T(8,128)S(1)}, f32[64,512]{1,0:T(8,128)S(1)}, u32[]{:S(2)}, u32[]{:S(2)}) collective-permute-start(f32[64,512]{1,0:T(8,128)S(1)} %add.13), channel_id=1, source_target_pairs={{0,6},{1,7},{2,4},{3,5},{4,2},{5,3},{6,0},{7,1},{8,14},{9,15},{10,... | collective-permute-start | bytes 393224 | tf_op jit(solution)/shard_map/ppermute | solution.py:429
  22.1 6.8 %collective-permute-start.11 = (f32[64,512]{1,0:T(8,128)S(1)}, f32[64,512]{1,0:T(8,128)S(1)}, u32[]{:S(2)}, u32[]{:S(2)}) collective-permute-start(f32[64,512]{1,0:T(8,128)S(1)} %add.14), channel_id=1, source_target_pairs={{0,4},{1,5},{2,6},{3,7},{4,0},{5,1},{6,2},{7,3},{8,12},{9,13},{10,... | collective-permute-start | bytes 393224 | tf_op jit(solution)/shard_map/ppermute | solution.py:429
  22.7 6.3 %collective-permute-start.13 = (f32[64,512]{1,0:T(8,128)S(1)}, f32[64,512]{1,0:T(8,128)S(1)}, u32[]{:S(2)}, u32[]{:S(2)}) collective-permute-start(f32[64,512]{1,0:T(8,128)S(1)} %add.15), channel_id=1, source_target_pairs={{0,2},{1,3},{2,0},{3,1},{4,6},{5,7},{6,4},{7,5},{8,10},{9,11},{10,... | collective-permute-start | bytes 393224 | tf_op jit(solution)/shard_map/ppermute | solution.py:429

commit v6 on v5

--- a/solution.py
+++ b/solution.py
@@ -305,56 +305,38 @@
     leave.wait()
 
 
-def message_kernel(groups, capacity, rows, side, *refs):
-    counts, noise, backs, depth, *small = refs[:9]
-    msgs = refs[9 : 9 + groups]
-    noise_out, backs_out, picks, values = refs[9 + groups : 13 + groups]
-    classes, owner, stencil, *kinds, sems = refs[13 + groups :]
+def message_kernel(groups, capacity, rows, *refs):
+    counts, noise, backs, depth = refs[:4]
+    msgs = refs[4 : 4 + groups]
+    noise_out, backs_out, classes, sems = refs[4 + groups :]
     mine = lax.axis_index("gx")
-    heads = [
-        pltpu.make_async_copy(a, b, sems.at[i]) for i, (a, b) in enumerate(zip((depth, *small), (classes, owner, stencil, *kinds)))
-    ]
-    for copy in heads:
-        copy.start()
+    head = pltpu.make_async_copy(depth, classes, sems.at[groups])
+    head.start()
     copies = []
     for k in range(groups):
         start = lax.bitwise_xor(mine, k) * capacity
         copies.append(
             pltpu.make_async_copy(
-                counts.at[pl.ds(start * rows, capacity * rows)], msgs[k].at[pl.ds(0, capacity * rows), :], sems.at[6 + k]
+                counts.at[pl.ds(start * rows, capacity * rows)], msgs[k].at[pl.ds(0, capacity * rows), :], sems.at[k]
             )
         )
-    copies.append(pltpu.make_async_copy(noise, noise_out, sems.at[6 + groups]))
-    copies.append(pltpu.make_async_copy(backs, backs_out, sems.at[7 + groups]))
+    copies.append(pltpu.make_async_copy(noise, noise_out, sems.at[groups + 1]))
+    copies.append(pltpu.make_async_copy(backs, backs_out, sems.at[groups + 2]))
     for copy in copies:
         copy.start()
-    for copy in heads:
-        copy.wait()
+    head.wait()
     for k in range(groups):
         start = lax.bitwise_xor(mine, k) * capacity
         for r in range(capacity):
             at = capacity * rows + r
             msgs[k][at : at + 1, :] = jnp.full((1, TC), classes[start + r], jnp.int32)
-    for t in range(owner.shape[0]):
-        rank = jnp.int32(0)
-        for t2 in range(t):
-            rank = rank + (owner[t2] == owner[t]).astype(jnp.int32)
-        pick = lax.bitwise_xor(owner[t], mine) * capacity + rank
-        picks[:, t * TC : (t + 1) * TC] = jnp.full((8, TC), pick, jnp.int32)
-    for i in range(stencil.shape[0]):
-        values[i : i + 1, :] = jnp.full((1, side), stencil[i], F32)
-    at = STENCIL_ROWS
-    for kind in kinds:
-        for d in range(kind.shape[0]):
-            values[at : at + 1, :] = jnp.full((1, side), kind[d], F32)
-            at += 1
     for copy in copies:
         copy.wait()
 
 
 def arrival_order(groups):
-    first = (2, 3, 1)
-    return list(first) + [k for k in range(groups) if k not in first]
+    first = [k for k in (2, 3, 1) if k < groups]
+    return first + [k for k in range(groups) if k not in first]
 
 
 def select_kernel(groups, capacity, rows, depths, *refs):
@@ -386,13 +368,33 @@
             kinds_out[i * 8 : (i + 1) * 8, cols] = jnp.broadcast_to(value, (8, TC))
 
 
-def table_kernel(*refs):
-    sems = refs[-1]
-    count = len(refs) // 2
-    copies = [pltpu.make_async_copy(refs[i], refs[count + i], sems.at[i]) for i in range(count)]
+def table_kernel(capacity, count, *refs):
+    small, (*tables, picks, values) = refs[: 5 + count], refs[5 + count : 7 + 2 * count]
+    owner, stencil, *kinds, sems = refs[7 + 2 * count :]
+    side = values.shape[1]
+    mine = lax.axis_index("gx")
+    copies = [
+        pltpu.make_async_copy(a, b, sems.at[i])
+        for i, (a, b) in enumerate(zip(small, (owner, stencil, *kinds, *tables)))
+    ]
     for copy in copies:
         copy.start()
-    for copy in copies:
+    for copy in copies[:5]:
+        copy.wait()
+    for t in range(owner.shape[0]):
+        rank = jnp.int32(0)
+        for t2 in range(t):
+            rank = rank + (owner[t2] == owner[t]).astype(jnp.int32)
+        pick = lax.bitwise_xor(owner[t], mine) * capacity + rank
+        picks[:, t * TC : (t + 1) * TC] = jnp.full((8, TC), pick, jnp.int32)
+    for i in range(stencil.shape[0]):
+        values[i : i + 1, :] = jnp.full((1, side), stencil[i], F32)
+    at = STENCIL_ROWS
+    for kind in kinds:
+        for d in range(kind.shape[0]):
+            values[at : at + 1, :] = jnp.full((1, side), kind[d], F32)
+            at += 1
+    for copy in copies[5:]:
         copy.wait()
 
 
@@ -433,25 +435,16 @@
         blocks[k] = swap(own, k)
     small = (owner.reshape(tiles), stencil, mean_counts, bias_one, bias_two)
     depths = mean_counts.shape[0]
-    *msgs, blocks[0], backs, picks, values = pl.pallas_call(
-        functools.partial(message_kernel, groups, capacity, rows, side),
+    *msgs, blocks[0], backs = pl.pallas_call(
+        functools.partial(message_kernel, groups, capacity, rows),
         out_shape=[VMEM((capacity * rows + 8, TC), jnp.int32)] * groups
-        + [
-            VMEM((rows, side), F32),
-            VMEM(backs.shape, backs.dtype),
-            VMEM((8, side), jnp.int32),
-            VMEM((STENCIL_ROWS + -(-3 * depths // 8) * 8, side), F32),
-        ],
-        in_specs=[hbm] * 9,
-        out_specs=[vmem] * (groups + 4),
-        scratch_shapes=[
-            pltpu.SMEM((slots,), jnp.int32),
-            *[pltpu.SMEM(a.shape, a.dtype) for a in small],
-            pltpu.SemaphoreType.DMA((groups + 8,)),
-        ],
+        + [VMEM((rows, side), F32), VMEM(backs.shape, backs.dtype)],
+        in_specs=[hbm] * 4,
+        out_specs=[vmem] * (groups + 2),
+        scratch_shapes=[pltpu.SMEM((slots,), jnp.int32), pltpu.SemaphoreType.DMA((groups + 3,))],
         compiler_params=pltpu.CompilerParams(vmem_limit_bytes=4 * MIB),
         name="messages",
-    )(*[in_hbm(a) for a in (counts.reshape(slots * rows, TC), own, backs, depth.reshape(slots), *small)])
+    )(*[in_hbm(a) for a in (counts.reshape(slots * rows, TC), own, backs, depth.reshape(slots))])
     for k in range(groups - 1, 0, -1):
         msgs[k] = swap(msgs[k], k, "gx", groups)
 
@@ -469,16 +462,23 @@
     )(*[blocks[k] for k in range(0, n, 2)], backs)
     other = swap(along_y, 1)
     packed, reals, _ = lax.optimization_barrier((packed, reals, along_y))
-    packed, reals = pl.pallas_call(
-        table_kernel,
-        out_shape=[VMEM(t.shape, t.dtype) for t in (packed, reals)],
-        in_specs=[hbm] * 2,
-        out_specs=[vmem] * 2,
-        scratch_shapes=[pltpu.SemaphoreType.DMA((2,))],
+    small = (owner.reshape(tiles), stencil, mean_counts, bias_one, bias_two)
+    depths = mean_counts.shape[0]
+    packed, reals, picks, values = pl.pallas_call(
+        functools.partial(table_kernel, capacity, 2),
+        out_shape=[
+            VMEM(packed.shape, packed.dtype),
+            VMEM(reals.shape, reals.dtype),
+            VMEM((8, side), jnp.int32),
+            VMEM((STENCIL_ROWS + -(-3 * depths // 8) * 8, side), F32),
+        ],
+        in_specs=[hbm] * 7,
+        out_specs=[vmem] * 4,
+        scratch_shapes=[*[pltpu.SMEM(a.shape, a.dtype) for a in small], pltpu.SemaphoreType.DMA((7,))],
         compiler_params=pltpu.CompilerParams(vmem_limit_bytes=4 * MIB),
         cost_estimate=pl.CostEstimate(flops=20_000_000_000, bytes_accessed=1, transcendentals=0),
         name="tables",
-    )(in_hbm(packed), in_hbm(reals))
+    )(*[in_hbm(a) for a in (*small, packed, reals)])
     density, smooth, fields = pl.pallas_call(
         functools.partial(field_kernel, n, rows, side),
         out_shape=[VMEM((rows, side), F32), VMEM((rows, side), F32), VMEM((5 * ring, side), F32)],

time: 30 us -> 29.9 us (level)
  no operation moved by 1% of the time
where the time goes in v6:
time: 29.9 us; the launch traced here: 29.8 us
  starting transfers between devices  14.1 us (47%)
  Pallas kernels  8.1 us (27%)
  waiting for transfers between devices  6.81 us (23%)
  between operations  0.72 us (2%)
    ppermute x14, starting transfers between devices, swap(): return lax.ppermute(value, axis, [(i, i ^ k) for i in range(size)])  14.1 us
    ppermute x14, waiting for transfers between devices, swap(): return lax.ppermute(value, axis, [(i, i ^ k) for i in range(size)])  6.81 us
    pallas_call x1, Pallas kernels, local(): pl.pallas_call(functools.partial(adjoint_kernel, n, rows, side), out_shap...  1.95 us
    pallas_call x1, Pallas kernels, local(): pl.pallas_call(functools.partial(field_kernel, n, rows, side), out_shape=...  1.78 us
    pallas_call x1, Pallas kernels, local(): pl.pallas_call(functools.partial(table_kernel, capacity, 2), out_shape=[V...  1.63 us
    pallas_call x1, Pallas kernels, local(): pl.pallas_call(functools.partial(message_kernel, groups, capacity, rows),...  1.31 us
    pallas_call x1, Pallas kernels, local(): pl.pallas_call(functools.partial(last_kernel, len(pieces)), out_shape=cel...  0.88 us
  transfers between devices with their start and end apart: 14, of which 8 were waited for; matrix products, arithmetic and copies ran while one was open for 0% of the time, Pallas kernels for 17%

profile of v6, /device:TPU:0, one launch (start us, length us, event | category | flops | bytes accessed | tf_op | source)
XLA Modules:
  0.0 29.8 jit_solution(15893173955408718529)
XLA Ops:
  0.6 4.0 %collective-permute-start.2 = (f32[64,512]{1,0:T(8,128)}, f32[64,512]{1,0:T(8,128)S(1)}, u32[]{:S(2)}, u32[]{:S(2)}) collective-permute-start(f32[64,512]{1,0:T(8,128)} %bitcast.7), channel_id=1, source_target_pairs={{0,6},{1,7},{2,4},{3,5},{4,2},{5,3},{6,0},{7,1},{8,14},{9,15},{10,... | collective-permute-start | bytes 393224 | tf_op jit(solution)/shard_map/ppermute | solution.py:431
  4.6 0.5 %collective-permute-start.1 = (f32[64,512]{1,0:T(8,128)}, f32[64,512]{1,0:T(8,128)S(1)}, u32[]{:S(2)}, u32[]{:S(2)}) collective-permute-start(f32[64,512]{1,0:T(8,128)} %bitcast.8), channel_id=1, source_target_pairs={{0,4},{1,5},{2,6},{3,7},{4,0},{5,1},{6,2},{7,3},{8,12},{9,13},{10,... | collective-permute-start | bytes 393224 | tf_op jit(solution)/shard_map/ppermute | solution.py:431
  5.1 0.1 collective-permute-start
  5.2 1.3 %messages.1 = (s32[136,128]{1,0:T(8,128)S(1)}, s32[136,128]{1,0:T(8,128)S(1)}, s32[136,128]{1,0:T(8,128)S(1)}, s32[136,128]{1,0:T(8,128)S(1)}, f32[64,512]{1,0:T(8,128)S(1)}, /*index=5*/bf16[512,512]{1,0:T(8,128)(2,1)S(1)}) custom-call(s32[512,128]{1,0:T(8,128)} %bitcast.6, f32[64,512]{1,0:T(8,128)} %bitcast.10, bf16[512,512]{1,0:T(8,128)(2,1)} %constant.6.clone.refs_2_, ...), custom_call_target="tpu_custom_call" | custom-call | tf_op jit(solution)/shard_map/messages/pallas_call | solution.py:438
  6.5 3.1 %collective-permute-start.3 = (s32[136,128]{1,0:T(8,128)S(1)}, s32[136,128]{1,0:T(8,128)S(1)}, u32[]{:S(2)}, u32[]{:S(2)}) collective-permute-start(s32[136,128]{1,0:T(8,128)S(1)} %get-tuple-element.35), channel_id=1, source_target_pairs={{0,16},{8,24},{16,0},{24,8},{1,17},{9,25},{17,1},{25,9},{2,18},{10... | collective-permute-start | bytes 208904 | tf_op jit(solution)/shard_map/ppermute | solution.py:431
  9.6 1.3 %collective-permute-start.4 = (s32[136,128]{1,0:T(8,128)S(1)}, s32[136,128]{1,0:T(8,128)S(1)}, u32[]{:S(2)}, u32[]{:S(2)}) collective-permute-start(s32[136,128]{1,0:T(8,128)S(1)} %get-tuple-element.36), channel_id=1, source_target_pairs={{0,24},{8,16},{16,8},{24,0},{1,25},{9,17},{17,9},{25,1},{2,26},{10... | collective-permute-start | bytes 208904 | tf_op jit(solution)/shard_map/ppermute | solution.py:431
  11.0 0.0 collective-permute-done.2.refs_3_
  11.0 0.2 collective-permute-start.5
  11.2 0.0 collective-permute-done.1.refs_2_
  11.2 0.2 collective-permute-done.refs_1_
  11.4 0.5 %along_y.1.refs_1_ = f32[2,128,512]{2,1,0:T(8,128)S(1)} custom-call(f32[64,512]{1,0:T(8,128)S(1)} %get-tuple-element.30.refs_0_.refs_4_, f32[64,512]{1,0:T(8,128)S(1)} %collective-permute-done.refs_1_, f32[64,512]{1,0:T(8,128)S(1)} %collective-permute-done.1.refs_2_, f32[64,512]{1,0:T(8,128)S(1)} %collective-permute-done.2.refs_3_, ...), custom_call_target="tpu_custom_call" | custom-call | tf_op jit(solution)/shard_map/along_y/pallas_call | solution.py:454
  11.8 0.1 collective-permute-start.6
  11.9 1.6 %tables.1 = (bf16[1664,512]{1,0:T(8,128)(2,1)S(1)}, f32[520,256]{1,0:T(8,128)S(1)}, s32[8,512]{1,0:T(8,128)S(1)}, f32[32,512]{1,0:T(8,128)S(1)}) custom-call(s32[4]{0:T(128)} %bitcast.14, f32[9]{0:T(128)} %refs_1_.1, f32[4]{0:T(128)} %refs_2_.2, f32[4]{0:T(128)} %refs_3_.1, f32[4]{0:T(128)} %refs_4_.1, bf16[1664,512]{1,0:T(8,128)(2,1)} %constant.7.clone.refs_5_, ...), custom_call_target="tpu_custom_call" | custom-call | flops 20000000000 | bytes 1 | tf_op jit(solution)/shard_map/tables/pallas_call | solution.py:467
  13.5 0.3 collective-permute-done.6.refs_2_
  13.8 1.8 %fields.1 = (f32[64,512]{1,0:T(8,128)S(1)}, f32[64,512]{1,0:T(8,128)S(1)}, f32[400,512]{1,0:T(8,128)S(1)}) custom-call(f32[32,512]{1,0:T(8,128)S(1)} %get-tuple-element.34.refs_0_.refs_5_, f32[2,128,512]{2,1,0:T(8,128)S(1)} %along_y.1.refs_1_, f32[2,128,512]{2,1,0:T(8,128)S(1)} %collective-permute-done.6.refs_2_, ...), custom_call_target="tpu_custom_call" | custom-call | tf_op jit(solution)/shard_map/fields/pallas_call | solution.py:482
  15.6 0.0 collective-permute-done.3.refs_0_
  15.6 0.2 collective-permute-done.4.refs_1_
  15.8 0.2 collective-permute-done.5.refs_2_
  16.0 0.1 select.1
  16.1 2.0 %adjoint.1 = (f32[64,512]{1,0:T(8,128)}, f32[64,512]{1,0:T(8,128)S(1)}, f32[64,512]{1,0:T(8,128)S(1)}, f32[64,512]{1,0:T(8,128)S(1)}, f32[64,512]{1,0:T(8,128)S(...) custom-call(f32[32,512]{1,0:T(8,128)S(1)} %get-tuple-element.34.refs_0_.refs_, ...), custom_call_target="tpu_custom_call" | custom-call | tf_op jit(solution)/shard_map/adjoint/pallas_call | solution.py:503
  18.1 0.1 collective-permute-start.8
  18.1 0.5 %collective-permute-start.10 = (f32[64,512]{1,0:T(8,128)S(1)}, f32[64,512]{1,0:T(8,128)S(1)}, u32[]{:S(2)}, u32[]{:S(2)}) collective-permute-start(f32[64,512]{1,0:T(8,128)S(1)} %get-tuple-element.54), channel_id=1, source_target_pairs={{0,1},{1,0},{2,3},{3,2},{4,5},{5,4},{6,7},{7,6},{8,9},{9,8},{10,11... | collective-permute-start | bytes 393224 | tf_op jit(solution)/shard_map/ppermute | solution.py:431
  18.6 0.1 collective-permute-start.12
  18.7 0.4 %collective-permute-start.7 = (f32[64,512]{1,0:T(8,128)S(1)}, f32[64,512]{1,0:T(8,128)S(1)}, u32[]{:S(2)}, u32[]{:S(2)}) collective-permute-start(f32[64,512]{1,0:T(8,128)S(1)} %get-tuple-element.50), channel_id=1, source_target_pairs={{0,1},{1,0},{2,3},{3,2},{4,5},{5,4},{6,7},{7,6},{8,9},{9,8},{10,11... | collective-permute-start | bytes 393224 | tf_op jit(solution)/shard_map/ppermute | solution.py:431
  19.1 0.3 %collective-permute-done.8 = f32[64,512]{1,0:T(8,128)S(1)} collective-permute-done((f32[64,512]{1,0:T(8,128)S(1)}, f32[64,512]{1,0:T(8,128)S(1)}, u32[]{:S(2)}, u32[]{:S(2)}) %collective-permute-start.8) | collective-permute-done | bytes 131104 | tf_op jit(solution)/shard_map/ppermute | solution.py:431
  19.5 2.5 %collective-permute-start.9 = (f32[64,512]{1,0:T(8,128)S(1)}, f32[64,512]{1,0:T(8,128)S(1)}, u32[]{:S(2)}, u32[]{:S(2)}) collective-permute-start(f32[64,512]{1,0:T(8,128)S(1)} %add.13), channel_id=1, source_target_pairs={{0,6},{1,7},{2,4},{3,5},{4,2},{5,3},{6,0},{7,1},{8,14},{9,15},{10,... | collective-permute-start | bytes 393224 | tf_op jit(solution)/shard_map/ppermute | solution.py:431
  22.0 0.0 collective-permute-done.10
  22.0 0.6 %collective-permute-start.11 = (f32[64,512]{1,0:T(8,128)S(1)}, f32[64,512]{1,0:T(8,128)S(1)}, u32[]{:S(2)}, u32[]{:S(2)}) collective-permute-start(f32[64,512]{1,0:T(8,128)S(1)} %add.14), channel_id=1, source_target_pairs={{0,4},{1,5},{2,6},{3,7},{4,0},{5,1},{6,2},{7,3},{8,12},{9,13},{10,... | collective-permute-start | bytes 393224 | tf_op jit(solution)/shard_map/ppermute | solution.py:431
  22.6 0.0 collective-permute-done.12
  22.6 0.6 %collective-permute-start.13 = (f32[64,512]{1,0:T(8,128)S(1)}, f32[64,512]{1,0:T(8,128)S(1)}, u32[]{:S(2)}, u32[]{:S(2)}) collective-permute-start(f32[64,512]{1,0:T(8,128)S(1)} %add.15), channel_id=1, source_target_pairs={{0,2},{1,3},{2,0},{3,1},{4,6},{5,7},{6,4},{7,5},{8,10},{9,11},{10,... | collective-permute-start | bytes 393224 | tf_op jit(solution)/shard_map/ppermute | solution.py:431
  23.2 0.0 collective-permute-done.7
  23.3 2.9 %collective-permute-done.9.refs_1_ = f32[64,512]{1,0:T(8,128)S(1)} collective-permute-done((f32[64,512]{1,0:T(8,128)S(1)}, f32[64,512]{1,0:T(8,128)S(1)}, u32[]{:S(2)}, u32[]{:S(2)}) %collective-permute-start.9) | collective-permute-done | bytes 131104 | tf_op jit(solution)/shard_map/ppermute | solution.py:431
  26.1 2.7 %collective-permute-done.11.refs_2_ = f32[64,512]{1,0:T(8,128)S(1)} collective-permute-done((f32[64,512]{1,0:T(8,128)S(1)}, f32[64,512]{1,0:T(8,128)S(1)}, u32[]{:S(2)}, u32[]{:S(2)}) %collective-permute-start.11) | collective-permute-done | bytes 131104 | tf_op jit(solution)/shard_map/ppermute | solution.py:431
  28.8 0.1 collective-permute-done.13.refs_3_
  28.9 0.9 %sum_and_rows.1 = f32[64,512]{1,0:T(8,128)} custom-call(f32[64,512]{1,0:T(8,128)S(1)} %add.12.refs_0_, f32[64,512]{1,0:T(8,128)S(1)} %collective-permute-done.9.refs_1_, f32[64,512]{1,0:T(8,128)S(1)} %collective-permute-done.11.refs_2_, f32[64,512]{1,0:T(8,128)S(1)} %collective-permute-done.13.refs_3_, f32[64,512]{1,0:T(8,128)S(1)} %get-tuple-element.30.refs_0_.refs_4_, ...), custom_call_target="tpu_custom_call" | custom-call | tf_op jit(solution)/shard_map/sum_and_rows/pallas_call | solution.py:520
  (4 shorter events, 0.1 us)
Async XLA Ops:
  0.6 10.3 %collective-permute-start.2 = (f32[64,512]{1,0:T(8,128)}, f32[64,512]{1,0:T(8,128)S(1)}, u32[]{:S(2)}, u32[]{:S(2)}) collective-permute-start(f32[64,512]{1,0:T(8,128)} %bitcast.7), channel_id=1, source_target_pairs={{0,6},{1,7},{2,4},{3,5},{4,2},{5,3},{6,0},{7,1},{8,14},{9,15},{10,... | collective-permute-start | bytes 393224 | tf_op jit(solution)/shard_map/ppermute | solution.py:431
  4.6 6.6 %collective-permute-start.1 = (f32[64,512]{1,0:T(8,128)}, f32[64,512]{1,0:T(8,128)S(1)}, u32[]{:S(2)}, u32[]{:S(2)}) collective-permute-start(f32[64,512]{1,0:T(8,128)} %bitcast.8), channel_id=1, source_target_pairs={{0,4},{1,5},{2,6},{3,7},{4,0},{5,1},{6,2},{7,3},{8,12},{9,13},{10,... | collective-permute-start | bytes 393224 | tf_op jit(solution)/shard_map/ppermute | solution.py:431
  5.1 6.3 %collective-permute-start = (f32[64,512]{1,0:T(8,128)}, f32[64,512]{1,0:T(8,128)S(1)}, u32[]{:S(2)}, u32[]{:S(2)}) collective-permute-start(f32[64,512]{1,0:T(8,128)} %bitcast.9), channel_id=1, source_target_pairs={{0,2},{1,3},{2,0},{3,1},{4,6},{5,7},{6,4},{7,5},{8,10},{9,11},{10,... | collective-permute-start | bytes 393224 | tf_op jit(solution)/shard_map/ppermute | solution.py:431
  6.5 9.0 %collective-permute-start.3 = (s32[136,128]{1,0:T(8,128)S(1)}, s32[136,128]{1,0:T(8,128)S(1)}, u32[]{:S(2)}, u32[]{:S(2)}) collective-permute-start(s32[136,128]{1,0:T(8,128)S(1)} %get-tuple-element.35), channel_id=1, source_target_pairs={{0,16},{8,24},{16,0},{24,8},{1,17},{9,25},{17,1},{25,9},{2,18},{10... | collective-permute-start | bytes 208904 | tf_op jit(solution)/shard_map/ppermute | solution.py:431
  9.6 6.2 %collective-permute-start.4 = (s32[136,128]{1,0:T(8,128)S(1)}, s32[136,128]{1,0:T(8,128)S(1)}, u32[]{:S(2)}, u32[]{:S(2)}) collective-permute-start(s32[136,128]{1,0:T(8,128)S(1)} %get-tuple-element.36), channel_id=1, source_target_pairs={{0,24},{8,16},{16,8},{24,0},{1,25},{9,17},{17,9},{25,1},{2,26},{10... | collective-permute-start | bytes 208904 | tf_op jit(solution)/shard_map/ppermute | solution.py:431
  11.0 5.1 %collective-permute-start.5 = (s32[136,128]{1,0:T(8,128)S(1)}, s32[136,128]{1,0:T(8,128)S(1)}, u32[]{:S(2)}, u32[]{:S(2)}) collective-permute-start(s32[136,128]{1,0:T(8,128)S(1)} %get-tuple-element.37), channel_id=1, source_target_pairs={{0,8},{8,0},{16,24},{24,16},{1,9},{9,1},{17,25},{25,17},{2,10},{10... | collective-permute-start | bytes 208904 | tf_op jit(solution)/shard_map/ppermute | solution.py:431
  11.8 2.0 %collective-permute-start.6 = (f32[2,128,512]{2,1,0:T(8,128)S(1)}, f32[2,128,512]{2,1,0:T(8,128)S(1)}, u32[]{:S(2)}, u32[]{:S(2)}) collective-permute-start(f32[2,128,512]{2,1,0:T(8,128)S(1)} %along_y.1.refs_1_), channel_id=1, source_target_pairs={{0,1},{1,0},{2,3},{3,2},{4,5},{5,4},{6,7},{7,6},{8,9},{9,8},{10,11... | collective-permute-start | bytes 1572872 | tf_op jit(solution)/shard_map/ppermute | solution.py:431
  18.1 1.4 %collective-permute-start.8 = (f32[64,512]{1,0:T(8,128)S(1)}, f32[64,512]{1,0:T(8,128)S(1)}, u32[]{:S(2)}, u32[]{:S(2)}) collective-permute-start(f32[64,512]{1,0:T(8,128)S(1)} %get-tuple-element.52), channel_id=1, source_target_pairs={{0,1},{1,0},{2,3},{3,2},{4,5},{5,4},{6,7},{7,6},{8,9},{9,8},{10,11... | collective-permute-start | bytes 393224 | tf_op jit(solution)/shard_map/ppermute | solution.py:431
  18.1 3.9 %collective-permute-start.10 = (f32[64,512]{1,0:T(8,128)S(1)}, f32[64,512]{1,0:T(8,128)S(1)}, u32[]{:S(2)}, u32[]{:S(2)}) collective-permute-start(f32[64,512]{1,0:T(8,128)S(1)} %get-tuple-element.54), channel_id=1, source_target_pairs={{0,1},{1,0},{2,3},{3,2},{4,5},{5,4},{6,7},{7,6},{8,9},{9,8},{10,11... | collective-permute-start | bytes 393224 | tf_op jit(solution)/shard_map/ppermute | solution.py:431
  18.6 4.0 %collective-permute-start.12 = (f32[64,512]{1,0:T(8,128)S(1)}, f32[64,512]{1,0:T(8,128)S(1)}, u32[]{:S(2)}, u32[]{:S(2)}) collective-permute-start(f32[64,512]{1,0:T(8,128)S(1)} %get-tuple-element.56), channel_id=1, source_target_pairs={{0,1},{1,0},{2,3},{3,2},{4,5},{5,4},{6,7},{7,6},{8,9},{9,8},{10,11... | collective-permute-start | bytes 393224 | tf_op jit(solution)/shard_map/ppermute | solution.py:431
  18.7 4.5 %collective-permute-start.7 = (f32[64,512]{1,0:T(8,128)S(1)}, f32[64,512]{1,0:T(8,128)S(1)}, u32[]{:S(2)}, u32[]{:S(2)}) collective-permute-start(f32[64,512]{1,0:T(8,128)S(1)} %get-tuple-element.50), channel_id=1, source_target_pairs={{0,1},{1,0},{2,3},{3,2},{4,5},{5,4},{6,7},{7,6},{8,9},{9,8},{10,11... | collective-permute-start | bytes 393224 | tf_op jit(solution)/shard_map/ppermute | solution.py:431
  19.5 6.6 %collective-permute-start.9 = (f32[64,512]{1,0:T(8,128)S(1)}, f32[64,512]{1,0:T(8,128)S(1)}, u32[]{:S(2)}, u32[]{:S(2)}) collective-permute-start(f32[64,512]{1,0:T(8,128)S(1)} %add.13), channel_id=1, source_target_pairs={{0,6},{1,7},{2,4},{3,5},{4,2},{5,3},{6,0},{7,1},{8,14},{9,15},{10,... | collective-permute-start | bytes 393224 | tf_op jit(solution)/shard_map/ppermute | solution.py:431
  22.0 6.8 %collective-permute-start.11 = (f32[64,512]{1,0:T(8,128)S(1)}, f32[64,512]{1,0:T(8,128)S(1)}, u32[]{:S(2)}, u32[]{:S(2)}) collective-permute-start(f32[64,512]{1,0:T(8,128)S(1)} %add.14), channel_id=1, source_target_pairs={{0,4},{1,5},{2,6},{3,7},{4,0},{5,1},{6,2},{7,3},{8,12},{9,13},{10,... | collective-permute-start | bytes 393224 | tf_op jit(solution)/shard_map/ppermute | solution.py:431
  22.6 6.3 %collective-permute-start.13 = (f32[64,512]{1,0:T(8,128)S(1)}, f32[64,512]{1,0:T(8,128)S(1)}, u32[]{:S(2)}, u32[]{:S(2)}) collective-permute-start(f32[64,512]{1,0:T(8,128)S(1)} %add.15), channel_id=1, source_target_pairs={{0,2},{1,3},{2,0},{3,1},{4,6},{5,7},{6,4},{7,5},{8,10},{9,11},{10,... | collective-permute-start | bytes 393224 | tf_op jit(solution)/shard_map/ppermute | solution.py:431

commit v7 on v6

--- a/solution.py
+++ b/solution.py
@@ -14,7 +14,7 @@
 AMPLITUDE = 0.75
 PIVOT = 1.0
 GROWTH = 7.0 / 8.0
-PAD = 16
+PAD = 8
 STENCIL_ROWS = 16
 MIB = 1024 * 1024
 VMEM = pltpu.VMEM

time: 29.9 us -> 29.8 us (level)
  no operation moved by 1% of the time
where the time goes in v7:
time: 29.8 us; the launch traced here: 29.7 us
  starting transfers between devices  14.1 us (47%)
  Pallas kernels  7.93 us (27%)
  waiting for transfers between devices  6.88 us (23%)
  between operations  0.72 us (2%)
    ppermute x14, starting transfers between devices, swap(): return lax.ppermute(value, axis, [(i, i ^ k) for i in range(size)])  14.1 us
    ppermute x14, waiting for transfers between devices, swap(): return lax.ppermute(value, axis, [(i, i ^ k) for i in range(size)])  6.88 us
    pallas_call x1, Pallas kernels, local(): pl.pallas_call(functools.partial(adjoint_kernel, n, rows, side), out_shap...  1.84 us
    pallas_call x1, Pallas kernels, local(): pl.pallas_call(functools.partial(field_kernel, n, rows, side), out_shape=...  1.73 us
    pallas_call x1, Pallas kernels, local(): pl.pallas_call(functools.partial(table_kernel, capacity, 2), out_shape=[V...  1.61 us
    pallas_call x1, Pallas kernels, local(): pl.pallas_call(functools.partial(message_kernel, groups, capacity, rows),...  1.31 us
    pallas_call x1, Pallas kernels, local(): pl.pallas_call(functools.partial(last_kernel, len(pieces)), out_shape=cel...  0.88 us
  transfers between devices with their start and end apart: 14, of which 8 were waited for; matrix products, arithmetic and copies ran while one was open for 0% of the time, Pallas kernels for 17%

profile of v7, /device:TPU:0, one launch (start us, length us, event | category | flops | bytes accessed | tf_op | source)
XLA Modules:
  0.0 29.7 jit_solution(1451457869344193295)
XLA Ops:
  0.6 4.0 %collective-permute-start.2 = (f32[64,512]{1,0:T(8,128)}, f32[64,512]{1,0:T(8,128)S(1)}, u32[]{:S(2)}, u32[]{:S(2)}) collective-permute-start(f32[64,512]{1,0:T(8,128)} %bitcast.7), channel_id=1, source_target_pairs={{0,6},{1,7},{2,4},{3,5},{4,2},{5,3},{6,0},{7,1},{8,14},{9,15},{10,... | collective-permute-start | bytes 393224 | tf_op jit(solution)/shard_map/ppermute | solution.py:431
  4.6 0.5 %collective-permute-start.1 = (f32[64,512]{1,0:T(8,128)}, f32[64,512]{1,0:T(8,128)S(1)}, u32[]{:S(2)}, u32[]{:S(2)}) collective-permute-start(f32[64,512]{1,0:T(8,128)} %bitcast.8), channel_id=1, source_target_pairs={{0,4},{1,5},{2,6},{3,7},{4,0},{5,1},{6,2},{7,3},{8,12},{9,13},{10,... | collective-permute-start | bytes 393224 | tf_op jit(solution)/shard_map/ppermute | solution.py:431
  5.1 0.1 collective-permute-start
  5.2 1.3 %messages.1 = (s32[136,128]{1,0:T(8,128)S(1)}, s32[136,128]{1,0:T(8,128)S(1)}, s32[136,128]{1,0:T(8,128)S(1)}, s32[136,128]{1,0:T(8,128)S(1)}, f32[64,512]{1,0:T(8,128)S(1)}, /*index=5*/bf16[512,512]{1,0:T(8,128)(2,1)S(1)}) custom-call(s32[512,128]{1,0:T(8,128)} %bitcast.6, f32[64,512]{1,0:T(8,128)} %bitcast.10, bf16[512,512]{1,0:T(8,128)(2,1)} %constant.6.clone.refs_2_, ...), custom_call_target="tpu_custom_call" | custom-call | tf_op jit(solution)/shard_map/messages/pallas_call | solution.py:438
  6.5 3.1 %collective-permute-start.3 = (s32[136,128]{1,0:T(8,128)S(1)}, s32[136,128]{1,0:T(8,128)S(1)}, u32[]{:S(2)}, u32[]{:S(2)}) collective-permute-start(s32[136,128]{1,0:T(8,128)S(1)} %get-tuple-element.35), channel_id=1, source_target_pairs={{0,16},{8,24},{16,0},{24,8},{1,17},{9,25},{17,1},{25,9},{2,18},{10... | collective-permute-start | bytes 208904 | tf_op jit(solution)/shard_map/ppermute | solution.py:431
  9.6 1.3 %collective-permute-start.4 = (s32[136,128]{1,0:T(8,128)S(1)}, s32[136,128]{1,0:T(8,128)S(1)}, u32[]{:S(2)}, u32[]{:S(2)}) collective-permute-start(s32[136,128]{1,0:T(8,128)S(1)} %get-tuple-element.36), channel_id=1, source_target_pairs={{0,24},{8,16},{16,8},{24,0},{1,25},{9,17},{17,9},{25,1},{2,26},{10... | collective-permute-start | bytes 208904 | tf_op jit(solution)/shard_map/ppermute | solution.py:431
  11.0 0.0 collective-permute-done.2.refs_3_
  11.0 0.2 collective-permute-start.5
  11.2 0.0 collective-permute-done.1.refs_2_
  11.2 0.2 collective-permute-done.refs_1_
  11.4 0.5 %along_y.1.refs_1_ = f32[2,128,512]{2,1,0:T(8,128)S(1)} custom-call(f32[64,512]{1,0:T(8,128)S(1)} %get-tuple-element.30.refs_0_.refs_4_, f32[64,512]{1,0:T(8,128)S(1)} %collective-permute-done.refs_1_, f32[64,512]{1,0:T(8,128)S(1)} %collective-permute-done.1.refs_2_, f32[64,512]{1,0:T(8,128)S(1)} %collective-permute-done.2.refs_3_, ...), custom_call_target="tpu_custom_call" | custom-call | tf_op jit(solution)/shard_map/along_y/pallas_call | solution.py:454
  11.8 0.1 collective-permute-start.6
  11.9 1.6 %tables.1 = (bf16[1600,512]{1,0:T(8,128)(2,1)S(1)}, f32[520,256]{1,0:T(8,128)S(1)}, s32[8,512]{1,0:T(8,128)S(1)}, f32[32,512]{1,0:T(8,128)S(1)}) custom-call(s32[4]{0:T(128)} %bitcast.14, f32[9]{0:T(128)} %refs_1_.1, f32[4]{0:T(128)} %refs_2_.2, f32[4]{0:T(128)} %refs_3_.1, f32[4]{0:T(128)} %refs_4_.1, bf16[1600,512]{1,0:T(8,128)(2,1)} %constant.7.clone.refs_5_, ...), custom_call_target="tpu_custom_call" | custom-call | flops 20000000000 | bytes 1 | tf_op jit(solution)/shard_map/tables/pallas_call | solution.py:467
  13.5 0.3 collective-permute-done.6.refs_2_
  13.8 1.7 %fields.1 = (f32[64,512]{1,0:T(8,128)S(1)}, f32[64,512]{1,0:T(8,128)S(1)}, f32[360,512]{1,0:T(8,128)S(1)}) custom-call(f32[32,512]{1,0:T(8,128)S(1)} %get-tuple-element.34.refs_0_.refs_5_, f32[2,128,512]{2,1,0:T(8,128)S(1)} %along_y.1.refs_1_, f32[2,128,512]{2,1,0:T(8,128)S(1)} %collective-permute-done.6.refs_2_, ...), custom_call_target="tpu_custom_call" | custom-call | tf_op jit(solution)/shard_map/fields/pallas_call | solution.py:482
  15.5 0.0 collective-permute-done.3.refs_0_
  15.6 0.3 collective-permute-done.4.refs_1_
  15.8 0.2 collective-permute-done.5.refs_2_
  16.0 0.1 select.1
  16.1 1.8 %adjoint.1 = (f32[64,512]{1,0:T(8,128)}, f32[64,512]{1,0:T(8,128)S(1)}, f32[64,512]{1,0:T(8,128)S(1)}, f32[64,512]{1,0:T(8,128)S(1)}, f32[64,512]{1,0:T(8,128)S(...) custom-call(f32[32,512]{1,0:T(8,128)S(1)} %get-tuple-element.34.refs_0_.refs_, ...), custom_call_target="tpu_custom_call" | custom-call | tf_op jit(solution)/shard_map/adjoint/pallas_call | solution.py:503
  17.9 0.1 collective-permute-start.8
  18.0 0.5 %collective-permute-start.10 = (f32[64,512]{1,0:T(8,128)S(1)}, f32[64,512]{1,0:T(8,128)S(1)}, u32[]{:S(2)}, u32[]{:S(2)}) collective-permute-start(f32[64,512]{1,0:T(8,128)S(1)} %get-tuple-element.54), channel_id=1, source_target_pairs={{0,1},{1,0},{2,3},{3,2},{4,5},{5,4},{6,7},{7,6},{8,9},{9,8},{10,11... | collective-permute-start | bytes 393224 | tf_op jit(solution)/shard_map/ppermute | solution.py:431
  18.5 0.1 collective-permute-start.12
  18.6 0.4 %collective-permute-start.7 = (f32[64,512]{1,0:T(8,128)S(1)}, f32[64,512]{1,0:T(8,128)S(1)}, u32[]{:S(2)}, u32[]{:S(2)}) collective-permute-start(f32[64,512]{1,0:T(8,128)S(1)} %get-tuple-element.50), channel_id=1, source_target_pairs={{0,1},{1,0},{2,3},{3,2},{4,5},{5,4},{6,7},{7,6},{8,9},{9,8},{10,11... | collective-permute-start | bytes 393224 | tf_op jit(solution)/shard_map/ppermute | solution.py:431
  19.0 0.3 %collective-permute-done.8 = f32[64,512]{1,0:T(8,128)S(1)} collective-permute-done((f32[64,512]{1,0:T(8,128)S(1)}, f32[64,512]{1,0:T(8,128)S(1)}, u32[]{:S(2)}, u32[]{:S(2)}) %collective-permute-start.8) | collective-permute-done | bytes 131104 | tf_op jit(solution)/shard_map/ppermute | solution.py:431
  19.4 2.5 %collective-permute-start.9 = (f32[64,512]{1,0:T(8,128)S(1)}, f32[64,512]{1,0:T(8,128)S(1)}, u32[]{:S(2)}, u32[]{:S(2)}) collective-permute-start(f32[64,512]{1,0:T(8,128)S(1)} %add.13), channel_id=1, source_target_pairs={{0,6},{1,7},{2,4},{3,5},{4,2},{5,3},{6,0},{7,1},{8,14},{9,15},{10,... | collective-permute-start | bytes 393224 | tf_op jit(solution)/shard_map/ppermute | solution.py:431
  21.9 0.0 collective-permute-done.10
  21.9 0.6 %collective-permute-start.11 = (f32[64,512]{1,0:T(8,128)S(1)}, f32[64,512]{1,0:T(8,128)S(1)}, u32[]{:S(2)}, u32[]{:S(2)}) collective-permute-start(f32[64,512]{1,0:T(8,128)S(1)} %add.14), channel_id=1, source_target_pairs={{0,4},{1,5},{2,6},{3,7},{4,0},{5,1},{6,2},{7,3},{8,12},{9,13},{10,... | collective-permute-start | bytes 393224 | tf_op jit(solution)/shard_map/ppermute | solution.py:431
  22.5 0.0 collective-permute-done.12
  22.5 0.6 %collective-permute-start.13 = (f32[64,512]{1,0:T(8,128)S(1)}, f32[64,512]{1,0:T(8,128)S(1)}, u32[]{:S(2)}, u32[]{:S(2)}) collective-permute-start(f32[64,512]{1,0:T(8,128)S(1)} %add.15), channel_id=1, source_target_pairs={{0,2},{1,3},{2,0},{3,1},{4,6},{5,7},{6,4},{7,5},{8,10},{9,11},{10,... | collective-permute-start | bytes 393224 | tf_op jit(solution)/shard_map/ppermute | solution.py:431
  23.1 0.0 collective-permute-done.7
  23.1 2.9 %collective-permute-done.9.refs_1_ = f32[64,512]{1,0:T(8,128)S(1)} collective-permute-done((f32[64,512]{1,0:T(8,128)S(1)}, f32[64,512]{1,0:T(8,128)S(1)}, u32[]{:S(2)}, u32[]{:S(2)}) %collective-permute-start.9) | collective-permute-done | bytes 131104 | tf_op jit(solution)/shard_map/ppermute | solution.py:431
  26.0 2.7 %collective-permute-done.11.refs_2_ = f32[64,512]{1,0:T(8,128)S(1)} collective-permute-done((f32[64,512]{1,0:T(8,128)S(1)}, f32[64,512]{1,0:T(8,128)S(1)}, u32[]{:S(2)}, u32[]{:S(2)}) %collective-permute-start.11) | collective-permute-done | bytes 131104 | tf_op jit(solution)/shard_map/ppermute | solution.py:431
  28.7 0.1 collective-permute-done.13.refs_3_
  28.8 0.9 %sum_and_rows.1 = f32[64,512]{1,0:T(8,128)} custom-call(f32[64,512]{1,0:T(8,128)S(1)} %add.12.refs_0_, f32[64,512]{1,0:T(8,128)S(1)} %collective-permute-done.9.refs_1_, f32[64,512]{1,0:T(8,128)S(1)} %collective-permute-done.11.refs_2_, f32[64,512]{1,0:T(8,128)S(1)} %collective-permute-done.13.refs_3_, f32[64,512]{1,0:T(8,128)S(1)} %get-tuple-element.30.refs_0_.refs_4_, ...), custom_call_target="tpu_custom_call" | custom-call | tf_op jit(solution)/shard_map/sum_and_rows/pallas_call | solution.py:520
  (4 shorter events, 0.1 us)
Async XLA Ops:
  0.6 10.3 %collective-permute-start.2 = (f32[64,512]{1,0:T(8,128)}, f32[64,512]{1,0:T(8,128)S(1)}, u32[]{:S(2)}, u32[]{:S(2)}) collective-permute-start(f32[64,512]{1,0:T(8,128)} %bitcast.7), channel_id=1, source_target_pairs={{0,6},{1,7},{2,4},{3,5},{4,2},{5,3},{6,0},{7,1},{8,14},{9,15},{10,... | collective-permute-start | bytes 393224 | tf_op jit(solution)/shard_map/ppermute | solution.py:431
  4.6 6.6 %collective-permute-start.1 = (f32[64,512]{1,0:T(8,128)}, f32[64,512]{1,0:T(8,128)S(1)}, u32[]{:S(2)}, u32[]{:S(2)}) collective-permute-start(f32[64,512]{1,0:T(8,128)} %bitcast.8), channel_id=1, source_target_pairs={{0,4},{1,5},{2,6},{3,7},{4,0},{5,1},{6,2},{7,3},{8,12},{9,13},{10,... | collective-permute-start | bytes 393224 | tf_op jit(solution)/shard_map/ppermute | solution.py:431
  5.1 6.3 %collective-permute-start = (f32[64,512]{1,0:T(8,128)}, f32[64,512]{1,0:T(8,128)S(1)}, u32[]{:S(2)}, u32[]{:S(2)}) collective-permute-start(f32[64,512]{1,0:T(8,128)} %bitcast.9), channel_id=1, source_target_pairs={{0,2},{1,3},{2,0},{3,1},{4,6},{5,7},{6,4},{7,5},{8,10},{9,11},{10,... | collective-permute-start | bytes 393224 | tf_op jit(solution)/shard_map/ppermute | solution.py:431
  6.5 9.0 %collective-permute-start.3 = (s32[136,128]{1,0:T(8,128)S(1)}, s32[136,128]{1,0:T(8,128)S(1)}, u32[]{:S(2)}, u32[]{:S(2)}) collective-permute-start(s32[136,128]{1,0:T(8,128)S(1)} %get-tuple-element.35), channel_id=1, source_target_pairs={{0,16},{8,24},{16,0},{24,8},{1,17},{9,25},{17,1},{25,9},{2,18},{10... | collective-permute-start | bytes 208904 | tf_op jit(solution)/shard_map/ppermute | solution.py:431
  9.6 6.2 %collective-permute-start.4 = (s32[136,128]{1,0:T(8,128)S(1)}, s32[136,128]{1,0:T(8,128)S(1)}, u32[]{:S(2)}, u32[]{:S(2)}) collective-permute-start(s32[136,128]{1,0:T(8,128)S(1)} %get-tuple-element.36), channel_id=1, source_target_pairs={{0,24},{8,16},{16,8},{24,0},{1,25},{9,17},{17,9},{25,1},{2,26},{10... | collective-permute-start | bytes 208904 | tf_op jit(solution)/shard_map/ppermute | solution.py:431
  11.0 5.1 %collective-permute-start.5 = (s32[136,128]{1,0:T(8,128)S(1)}, s32[136,128]{1,0:T(8,128)S(1)}, u32[]{:S(2)}, u32[]{:S(2)}) collective-permute-start(s32[136,128]{1,0:T(8,128)S(1)} %get-tuple-element.37), channel_id=1, source_target_pairs={{0,8},{8,0},{16,24},{24,16},{1,9},{9,1},{17,25},{25,17},{2,10},{10... | collective-permute-start | bytes 208904 | tf_op jit(solution)/shard_map/ppermute | solution.py:431
  11.8 2.0 %collective-permute-start.6 = (f32[2,128,512]{2,1,0:T(8,128)S(1)}, f32[2,128,512]{2,1,0:T(8,128)S(1)}, u32[]{:S(2)}, u32[]{:S(2)}) collective-permute-start(f32[2,128,512]{2,1,0:T(8,128)S(1)} %along_y.1.refs_1_), channel_id=1, source_target_pairs={{0,1},{1,0},{2,3},{3,2},{4,5},{5,4},{6,7},{7,6},{8,9},{9,8},{10,11... | collective-permute-start | bytes 1572872 | tf_op jit(solution)/shard_map/ppermute | solution.py:431
  17.9 1.4 %collective-permute-start.8 = (f32[64,512]{1,0:T(8,128)S(1)}, f32[64,512]{1,0:T(8,128)S(1)}, u32[]{:S(2)}, u32[]{:S(2)}) collective-permute-start(f32[64,512]{1,0:T(8,128)S(1)} %get-tuple-element.52), channel_id=1, source_target_pairs={{0,1},{1,0},{2,3},{3,2},{4,5},{5,4},{6,7},{7,6},{8,9},{9,8},{10,11... | collective-permute-start | bytes 393224 | tf_op jit(solution)/shard_map/ppermute | solution.py:431
  18.0 3.9 %collective-permute-start.10 = (f32[64,512]{1,0:T(8,128)S(1)}, f32[64,512]{1,0:T(8,128)S(1)}, u32[]{:S(2)}, u32[]{:S(2)}) collective-permute-start(f32[64,512]{1,0:T(8,128)S(1)} %get-tuple-element.54), channel_id=1, source_target_pairs={{0,1},{1,0},{2,3},{3,2},{4,5},{5,4},{6,7},{7,6},{8,9},{9,8},{10,11... | collective-permute-start | bytes 393224 | tf_op jit(solution)/shard_map/ppermute | solution.py:431
  18.5 4.0 %collective-permute-start.12 = (f32[64,512]{1,0:T(8,128)S(1)}, f32[64,512]{1,0:T(8,128)S(1)}, u32[]{:S(2)}, u32[]{:S(2)}) collective-permute-start(f32[64,512]{1,0:T(8,128)S(1)} %get-tuple-element.56), channel_id=1, source_target_pairs={{0,1},{1,0},{2,3},{3,2},{4,5},{5,4},{6,7},{7,6},{8,9},{9,8},{10,11... | collective-permute-start | bytes 393224 | tf_op jit(solution)/shard_map/ppermute | solution.py:431
  18.6 4.5 %collective-permute-start.7 = (f32[64,512]{1,0:T(8,128)S(1)}, f32[64,512]{1,0:T(8,128)S(1)}, u32[]{:S(2)}, u32[]{:S(2)}) collective-permute-start(f32[64,512]{1,0:T(8,128)S(1)} %get-tuple-element.50), channel_id=1, source_target_pairs={{0,1},{1,0},{2,3},{3,2},{4,5},{5,4},{6,7},{7,6},{8,9},{9,8},{10,11... | collective-permute-start | bytes 393224 | tf_op jit(solution)/shard_map/ppermute | solution.py:431
  19.4 6.6 %collective-permute-start.9 = (f32[64,512]{1,0:T(8,128)S(1)}, f32[64,512]{1,0:T(8,128)S(1)}, u32[]{:S(2)}, u32[]{:S(2)}) collective-permute-start(f32[64,512]{1,0:T(8,128)S(1)} %add.13), channel_id=1, source_target_pairs={{0,6},{1,7},{2,4},{3,5},{4,2},{5,3},{6,0},{7,1},{8,14},{9,15},{10,... | collective-permute-start | bytes 393224 | tf_op jit(solution)/shard_map/ppermute | solution.py:431
  21.9 6.8 %collective-permute-start.11 = (f32[64,512]{1,0:T(8,128)S(1)}, f32[64,512]{1,0:T(8,128)S(1)}, u32[]{:S(2)}, u32[]{:S(2)}) collective-permute-start(f32[64,512]{1,0:T(8,128)S(1)} %add.14), channel_id=1, source_target_pairs={{0,4},{1,5},{2,6},{3,7},{4,0},{5,1},{6,2},{7,3},{8,12},{9,13},{10,... | collective-permute-start | bytes 393224 | tf_op jit(solution)/shard_map/ppermute | solution.py:431
  22.5 6.3 %collective-permute-start.13 = (f32[64,512]{1,0:T(8,128)S(1)}, f32[64,512]{1,0:T(8,128)S(1)}, u32[]{:S(2)}, u32[]{:S(2)}) collective-permute-start(f32[64,512]{1,0:T(8,128)S(1)} %add.15), channel_id=1, source_target_pairs={{0,2},{1,3},{2,0},{3,1},{4,6},{5,7},{6,4},{7,5},{8,10},{9,11},{10,... | collective-permute-start | bytes 393224 | tf_op jit(solution)/shard_map/ppermute | solution.py:431
